TPU v7x, 128 devices: a whole 4x4x4 slice. The times are simulated.
128 devices in a mesh: dp: 16 (over y, z_hi, core), ctx: 8 (over z_lo, x).
Axes of the slice: x: 4, y: 4, z: 4 (z_hi: 2, z_lo: 2; z = z_hi * 2 + z_lo), core: 2. Of those that a mesh axis runs over, the one named last changes fastest.
Arguments:
- qkv_in: bfloat16 [16, 4096, 1280], P('dp', 'ctx'), may hold values from -40 to 40
- dest: int32 [16, 4096], P('dp', 'ctx'), may hold values from 0 to 8191, as said below
- lengths: int32 [16, 4], P('dp'), may hold values from 1 to 2048, 4096 in all within a row
- grad_out: bfloat16 [16, 4096, 8192], P('dp', 'ctx'), may hold values from -0.1875 to 0.1875
Outputs:
- attention: bfloat16 [16, 4096, 1024], P('dp', 'ctx')
- grad_proj: float32 [1024, 8192], P(('dp', 'ctx'))
Inputs may be any that keep to these rules, and one draw needn't show every extreme that they name: `dest`: within each slot c of the ctx axis, the values over all data groups at positions c * 512 to (c + 1) * 512 - 1 are each number from 0 to the largest value once, and every device's rows go in equal numbers to each data group. Each group's lengths sum to 4096 and the longest is exactly 2048.
All inputs are finite; a program needn't handle non-finite values.
Results may differ from a plain program's by a relative error of at most 0.017.
Values may be sent and summed in bfloat16 or wider, within the bound.
No kernel may reach another device: no remote copies, remote signals or barrier semaphores. Data moves between devices by JAX's collectives and lax.ppermute only.
A program may use at most 128 MiB of HBM per device.

v0:
```python
import functools

import jax
import jax.numpy as jnp
import numpy as np
from jax import lax
from jax.experimental import pallas as pl
from jax.experimental.pallas import tpu as pltpu
from jax.sharding import PartitionSpec as P

HQ = 8
DH = 128
ROWS = 512
GROUPS = 16
SLOTS = 8
BACK = 4
TILE = 256
AXES = ("dp", "ctx")
CHIPS = 64
MIB = 1024 * 1024
SCORE_FLOOR = -1e30
TOTAL_LIMIT = 2.0**90
EXP_SCALE = float(DH**-0.5 * np.log2(np.e))
WIDTHS = (1408, 1408, 1280)
OFFSETS = (0, 1408, 2816)
HALF = 4096

FLIPS = {
    "xa": (1, 0, 0),
    "xb": (3, 0, 0),
    "ya": (0, 1, 0),
    "yb": (0, 3, 0),
    "za": (0, 0, 1),
    "zb": (0, 0, 3),
}
SET_A = ("xa", "ya", "za")
SET_B = ("xb", "yb", "zb")


def rotate(names, by):
    return names[by:] + names[:by]


ORDERS = (
    tuple(rotate(SET_A, part) + SET_B for part in range(3)),
    tuple(rotate(SET_B, part) + SET_A for part in range(3)),
)


def place_of(index):
    dp, ctx = index // SLOTS, index % SLOTS
    y, z_hi, core = dp // 4, (dp // 2) % 2, dp % 2
    return ctx % 4, y, z_hi * 2 + ctx // 4, core


def index_of(x, y, z, core):
    return (y * 4 + (z // 2) * 2 + core) * SLOTS + (z % 2) * 4 + x


def flip_pairs(flip_of_core):
    pairs = []
    for index in range(2 * CHIPS):
        x, y, z, core = place_of(index)
        fx, fy, fz = FLIPS[flip_of_core[core]]
        pairs.append((index, index_of(x ^ fx, y ^ fy, z ^ fz, core)))
    return pairs


def core_pairs():
    pairs = []
    for index in range(2 * CHIPS):
        x, y, z, core = place_of(index)
        pairs.append((index, index_of(x, y, z, 1 - core)))
    return pairs


def flip_table():
    table = np.zeros((2, CHIPS, 3), np.int32)
    for core in range(2):
        for block in range(CHIPS):
            for level, name in enumerate(ORDERS[core][0]):
                if (block >> (5 - level)) & 1:
                    table[core, block] ^= np.array(FLIPS[name], np.int32)
    return table


def dot(a, b, contract):
    return lax.dot_general(
        a, b, ((contract[:1], contract[1:]), ((), ())), preferred_element_type=jnp.float32
    )


def as_bf16(mask):
    return mask.astype(jnp.float32).astype(jnp.bfloat16)


def vmem_call(body, out_shape, scratch=(), smem=0, operands=(), mib=16, flops=0, nbytes=0):
    specs = [pl.BlockSpec(memory_space=pltpu.SMEM)] * smem
    specs += [pl.BlockSpec(memory_space=pltpu.VMEM)] * (len(operands) - smem)
    out_specs = jax.tree.map(lambda _: pl.BlockSpec(memory_space=pltpu.VMEM), out_shape)
    return pl.pallas_call(
        body,
        out_shape=out_shape,
        in_specs=specs,
        out_specs=out_specs,
        scratch_shapes=list(scratch),
        compiler_params=pltpu.CompilerParams(vmem_limit_bytes=mib * MIB),
        cost_estimate=pl.CostEstimate(flops=flops, bytes_accessed=nbytes, transcendentals=0),
    )(*operands)


def sort_kernel(dest_ref, rows_ref, key_vals_ref, queries_ref):
    dest = dest_ref[...]
    target = dest >> 9
    slot = dest & (ROWS - 1)
    member = as_bf16(lax.broadcasted_iota(jnp.int32, (GROUPS, ROWS), 0) == target)
    same = dot(member, member, (0, 0))
    row = lax.broadcasted_iota(jnp.int32, (ROWS, ROWS), 0)
    col = lax.broadcasted_iota(jnp.int32, (ROWS, ROWS), 1)
    rank = jnp.sum(jnp.where(row < col, same, 0.0), axis=0, keepdims=True)
    place = target * (ROWS // GROUPS) + rank.astype(jnp.int32)
    order = as_bf16(row == place)
    line = lax.broadcasted_iota(jnp.int32, (DH, ROWS), 0)
    coded = jnp.where(line == 0, slot >> 4, jnp.where(line == 1, slot & 15, 0))
    coded = coded.astype(jnp.float32).astype(jnp.bfloat16)
    key_vals_ref[:, 2 * DH :] = dot(order, coded, (1, 1)).astype(jnp.bfloat16)
    key_vals_ref[:, : 2 * DH] = dot(order, rows_ref[:, HQ * DH :], (1, 0)).astype(jnp.bfloat16)
    queries_ref[...] = dot(order, rows_ref[:, : HQ * DH], (1, 0)).astype(jnp.bfloat16)


def place_kernel(got_ref, key_vals_ref, inverse_ref):
    lane = lax.broadcasted_iota(jnp.int32, (16, DH), 1)
    coef = jnp.where(lane == 0, 16.0, jnp.where(lane == 1, 1.0, 0.0)).astype(jnp.bfloat16)
    slots = dot(coef, got_ref[:, 2 * DH :], (1, 1))[:1].astype(jnp.int32)
    inverse = as_bf16(lax.broadcasted_iota(jnp.int32, (ROWS, ROWS), 0) == slots)
    inverse_ref[...] = inverse
    key_vals_ref[...] = dot(inverse, got_ref[:, : 2 * DH], (1, 0)).astype(jnp.bfloat16)


def attend_kernel(
    slot_ref,
    lengths_ref,
    table_ref,
    inverse_ref,
    got_ref,
    kv0_ref,
    kv1_ref,
    kv2_ref,
    kv3_ref,
    kv4_ref,
    out_ref,
    own_ref,
    swap_ref,
    q_ref,
    k_ref,
    v_ref,
    top_ref,
    acc_ref,
    done_ref,
):
    for back, kv_ref in enumerate((kv0_ref, kv1_ref, kv2_ref, kv3_ref, kv4_ref)):
        at = (BACK - back) * ROWS
        k_ref[at : at + ROWS, :] = kv_ref[:, :DH]
        v_ref[at : at + ROWS, :DH] = kv_ref[:, DH:]
    v_ref[:, DH:] = jnp.ones(((BACK + 1) * ROWS, DH), jnp.bfloat16)
    q_ref[...] = dot(inverse_ref[...], got_ref[...], (1, 0)).astype(jnp.bfloat16)

    slot = slot_ref[0]
    start1 = lengths_ref[0, 0]
    start2 = start1 + lengths_ref[0, 1]
    start3 = start2 + lengths_ref[0, 2]

    def first_of(position):
        found = jnp.where(position >= start1, start1, 0)
        found = jnp.where(position >= start2, start2, found)
        return jnp.where(position >= start3, start3, found)

    for tile in range(ROWS // TILE):
        q_rows = slice(tile * TILE, (tile + 1) * TILE)
        p_first = slot * ROWS + tile * TILE
        low_first = first_of(p_first)
        high_first = first_of(p_first + TILE - 1)
        own_at = BACK * ROWS + tile * TILE
        count = (p_first - low_first + TILE - 1) // TILE
        clear = jnp.maximum(p_first - high_first, 0) // TILE

        def parts(j, p_first=p_first, own_at=own_at):
            at = pl.multiple_of(own_at - j * TILE, TILE)
            return k_ref[pl.ds(at, TILE), :], v_ref[pl.ds(at, TILE), :]

        def visible_of(j, p_first=p_first):
            q_pos = p_first + lax.broadcasted_iota(jnp.int32, (TILE, TILE), 0)
            k_pos = p_first - j * TILE + lax.broadcasted_iota(jnp.int32, (TILE, TILE), 1)
            return (k_pos >= first_of(q_pos)) & (k_pos <= q_pos)

        def scores_of(h, keys, visible, q_rows=q_rows):
            scores = dot(q_ref[q_rows, h * DH : (h + 1) * DH], keys, (1, 1))
            return scores if visible is None else jnp.where(visible, scores, SCORE_FLOOR)

        own_keys = k_ref[own_at : own_at + TILE, :].astype(jnp.float32)
        ones = jnp.ones((DH, DH), jnp.bfloat16)
        for h in range(HQ):
            pair = q_ref[q_rows, h * DH : (h + 1) * DH].astype(jnp.float32) * own_keys
            top_ref[h * TILE : (h + 1) * TILE, :] = (
                dot(pair.astype(jnp.bfloat16), ones, (1, 0)) * EXP_SCALE
            )
        acc_ref[...] = jnp.zeros_like(acc_ref)

        def add(j, masked):
            keys, values = parts(j)
            visible = visible_of(j) if masked else None
            for h in range(HQ):
                rows = slice(h * TILE, (h + 1) * TILE)
                scores = scores_of(h, keys, visible)
                top = top_ref[rows, :]
                top = jnp.concatenate([top, top], axis=1)
                weights = jnp.exp2(scores * EXP_SCALE - top).astype(jnp.bfloat16)
                acc_ref[rows, :] += dot(weights, values, (1, 0))

        add(0, True)

        @pl.loop(1, 1 + clear)
        def _(j):
            add(j, False)

        @pl.loop(1 + clear, 1 + count)
        def _(j):
            add(j, True)

        @pl.when(jnp.max(acc_ref[:, DH:]) > TOTAL_LIMIT)
        def _():
            top_ref[...] = jnp.full_like(top_ref, SCORE_FLOOR)
            acc_ref[...] = jnp.zeros_like(acc_ref)

            @pl.loop(0, 1 + count)
            def _(j):
                keys, values = parts(j)
                visible = visible_of(j)

                @pl.loop(0, HQ)
                def _(h):
                    rows = pl.ds(pl.multiple_of(h * TILE, TILE), TILE)
                    cols = pl.ds(pl.multiple_of(h * DH, DH), DH)
                    scores = dot(q_ref[q_rows, cols], keys, (1, 1))
                    scores = jnp.where(visible, scores, SCORE_FLOOR)
                    old = top_ref[rows, :]
                    best = jnp.max(scores, axis=1, keepdims=True) * EXP_SCALE
                    top = jnp.maximum(old, best)
                    rescale = jnp.exp2(old - top)
                    top_ref[rows, :] = top
                    top = jnp.concatenate([top, top], axis=1)
                    weights = jnp.exp2(scores * EXP_SCALE - top).astype(jnp.bfloat16)
                    rescale = jnp.concatenate([rescale, rescale], axis=1)
                    acc_ref[rows, :] = acc_ref[rows, :] * rescale + dot(weights, values, (1, 0))

        for h in range(HQ):
            rows = slice(h * TILE, (h + 1) * TILE)
            done = acc_ref[rows, :DH] / acc_ref[rows, DH:]
            out_ref[q_rows, h * DH : (h + 1) * DH] = done.astype(jnp.bfloat16)
            done_ref[h * DH : (h + 1) * DH, q_rows] = done.T

    for side, ordered_ref in enumerate((own_ref, swap_ref)):

        @pl.loop(0, CHIPS, unroll=4)
        def _(block, side=side, ordered_ref=ordered_ref):
            at = pl.multiple_of(table_ref[side, block], 8)
            both = jnp.concatenate(
                [done_ref[pl.ds(at, 8), :], done_ref[pl.ds(at + 64, 8), :]], axis=0
            )
            ordered_ref[pl.ds(pl.multiple_of(block * 16, 16), 16), :] = both.astype(jnp.bfloat16)


def project_kernel(level, half, left_ref, left2_ref, own_ref, other_ref, out_ref):
    run = 512 >> level
    step = min(run, 256)
    for at in range(0, 512, step):
        rows = slice(at, at + step)
        source = (at // run) * 2 * run + half * run + at % run
        source = slice(source, source + step)
        term = dot(left_ref[source, :], own_ref[...], (1, 0))
        term += dot(left2_ref[source, :], other_ref[...], (1, 0))
        out_ref[rows, :] = term.astype(out_ref.dtype)


def shape(rows, cols, dtype=jnp.bfloat16):
    return jax.ShapeDtypeStruct((rows, cols), dtype)


def body(qkv_in, dest, lengths, grad_out):
    dp_at = lax.axis_index("dp")
    slot = lax.axis_index("ctx")
    core = dp_at % 2
    x, y, z = slot % 4, dp_at // 4, ((dp_at // 2) % 2) * 2 + slot // 4
    swap = core_pairs()

    tokens = grad_out[0]
    own_cols = [
        lax.dynamic_slice(tokens, (0, core * HALF + at), (ROWS, width))
        for at, width in zip(OFFSETS, WIDTHS)
    ]
    other_cols = [
        lax.ppermute(
            lax.dynamic_slice(tokens, (0, (1 - core) * HALF + at), (ROWS, width)), AXES, swap
        )
        for at, width in zip(OFFSETS, WIDTHS)
    ]

    sent_kv, sent_q = vmem_call(
        sort_kernel,
        (shape(ROWS, 3 * DH), shape(ROWS, HQ * DH)),
        operands=(dest, qkv_in[0]),
        flops=10**9,
        nbytes=3 * MIB,
    )
    got_kv = lax.all_to_all(
        sent_kv.reshape(GROUPS, ROWS // GROUPS, 3 * DH), "dp", 0, 0, tiled=True
    ).reshape(ROWS, 3 * DH)
    got_q = lax.all_to_all(
        sent_q.reshape(GROUPS, ROWS // GROUPS, HQ * DH), "dp", 0, 0, tiled=True
    ).reshape(ROWS, HQ * DH)
    key_vals, inverse = vmem_call(
        place_kernel,
        (shape(ROWS, 2 * DH), shape(ROWS, ROWS)),
        operands=(got_kv,),
        flops=2 * 10**8,
        nbytes=MIB,
    )
    earlier = [
        lax.ppermute(key_vals, "ctx", [(at, at + back) for at in range(SLOTS - back)])
        for back in range(1, BACK + 1)
    ]

    flips = jnp.asarray(flip_table())
    flips = jnp.where(core == 0, flips, flips[::-1])
    to_x, to_y, to_z = x ^ flips[..., 0], y ^ flips[..., 1], z ^ flips[..., 2]
    table = ((to_y * 2 + to_z // 2) * 128 + ((to_z % 2) * 4 + to_x) * 8).astype(jnp.int32)

    (table, inverse, got_q, key_vals, earlier), own_cols, other_cols = lax.optimization_barrier(
        ((table, inverse, got_q, key_vals, earlier), own_cols, other_cols)
    )
    attention, left, swap_left = vmem_call(
        attend_kernel,
        (shape(ROWS, HQ * DH), shape(HQ * DH, ROWS), shape(HQ * DH, ROWS)),
        scratch=(
            pltpu.VMEM((ROWS, HQ * DH), jnp.bfloat16),
            pltpu.VMEM(((BACK + 1) * ROWS, DH), jnp.bfloat16),
            pltpu.VMEM(((BACK + 1) * ROWS, 2 * DH), jnp.bfloat16),
            pltpu.VMEM((HQ * TILE, DH), jnp.float32),
            pltpu.VMEM((HQ * TILE, 2 * DH), jnp.float32),
            pltpu.VMEM((HQ * DH, ROWS), jnp.float32),
        ),
        smem=3,
        operands=(slot.reshape(1), lengths, table, inverse, got_q, key_vals, *earlier),
        mib=24,
        flops=10**10,
        nbytes=6 * MIB,
    )
    left2 = lax.ppermute(swap_left, AXES, swap)

    def project(part, half):
        return vmem_call(
            functools.partial(project_kernel, part, half),
            shape(512, WIDTHS[part]),
            operands=(left, left2, own_cols[part], other_cols[part]),
            flops=2 * 512 * 1024 * WIDTHS[part],
            nbytes=5 * MIB,
        )

    sends = [project(part, 1) for part in range(3)]
    coming = [
        lax.ppermute(sends[part], AXES, flip_pairs([ORDERS[c][part][0] for c in range(2)]))
        for part in range(3)
    ]
    keeps = [project(part, 0) for part in range(3)]
    for level in range(1, 4):
        sums = [
            keep.astype(jnp.float32) + came.astype(jnp.float32)
            for keep, came in zip(keeps, coming)
        ]
        lead = [2 if (level, part) == (1, 1) else 1 for part in range(3)]
        sums = [
            total.reshape(ahead, 2, -1, total.shape[1]) for ahead, total in zip(lead, sums)
        ]
        keeps = [total[:, 0].reshape(-1, total.shape[-1]) for total in sums]
        sends = [total[:, 1].reshape(-1, total.shape[-1]).astype(jnp.bfloat16) for total in sums]
        if level < 3:
            coming = [
                lax.ppermute(
                    sends[part], AXES, flip_pairs([ORDERS[c][part][level] for c in range(2)])
                )
                for part in range(3)
            ]
    keep, send = jnp.concatenate(keeps, axis=1), jnp.concatenate(sends, axis=1)
    for level in range(3, 6):
        came = lax.ppermute(send, AXES, flip_pairs([ORDERS[c][0][level] for c in range(2)]))
        total = keep + came.astype(jnp.float32)
        rows = total.shape[0] // 2
        keep, send = total[:rows], total[rows:].astype(jnp.bfloat16)
    both = total.reshape(2, 8, HALF)
    mine = lax.dynamic_index_in_dim(both, core, 0, keepdims=False)
    theirs = lax.dynamic_index_in_dim(both, 1 - core, 0, keepdims=False).astype(jnp.bfloat16)
    came = lax.ppermute(theirs, AXES, swap).astype(jnp.float32)
    grad_proj = jnp.where(
        core == 0,
        jnp.concatenate([mine, came], axis=1),
        jnp.concatenate([came, mine], axis=1),
    )
    return attention[None], grad_proj


def solution(mesh):
    in_specs = (P("dp", "ctx", None), P("dp", "ctx"), P("dp", None), P("dp", "ctx", None))
    out_specs = (P("dp", "ctx", None), P(("dp", "ctx"), None))
    return jax.shard_map(body, mesh=mesh, in_specs=in_specs, out_specs=out_specs, check_vma=False)
```

profile of v0, /device:TPU:0, one launch (start us, length us, event | category | flops | bytes accessed | tf_op | source)
XLA Modules:
  0.0 172.8 jit_solution(1379102802703292347)
XLA Ops:
  0.6 1.3 copy-done.2
  1.9 0.7 copy-done.3
  2.6 1.5 shard_map.68
  4.2 1.0 copy-done.1
  5.1 8.0 %all-to-all-start = ((bf16[16,32,384]{2,1,0:T(8,128)(2,1)}), bf16[16,32,384]{2,1,0:T(8,128)(2,1)S(1)}, u32[]{:S(2)}, u32[]{:S(2)}) async-start(bf16[16,32,384]{2,1,0:T(8,128)(2,1)} %bitcast.5), calls=%async_computation | async-start | bytes 786432 | tf_op jit(solution)/shard_map/all_to_all | solution.py:315
  13.1 4.7 %dynamic-slice_bitcast_fusion = (bf16[512,1408]{1,0:T(8,128)(2,1)}, bf16[512,1408]{1,0:T(8,128)(2,1)}, bf16[512,1408]{1,0:T(8,128)(2,1)S(1)}, bf16[512,1408]{1,0:T(8,128)(2,1)S(1)}) fusion(bf16[1,512,8192]{2,1,0:T(8,128)(2,1)} %param.8, s32[]{:T(128)S(6)} %select_n.91, s32[]{:T(128)S(6)} %select_n.90, s32[]{:T(128)S(6)} %select_n.88, s32[]{:T(128)S(6)} %select_n.87), kind=kLoop, calls=%fused_computation.8 | loop fusion | bytes 11534352 | tf_op jit(solution)/shard_map/dynamic_slice | solution.py:303
  17.9 0.4 collective-permute-start.5
  18.4 3.5 %dynamic-slice_bitcast_fusion.4 = (bf16[512,1280]{1,0:T(8,128)(2,1)}, bf16[512,1280]{1,0:T(8,128)(2,1)}) fusion(bf16[1,512,8192]{2,1,0:T(8,128)(2,1)} %param.8, s32[]{:T(128)S(6)} %select_n.92, s32[]{:T(128)S(6)} %select_n.89), kind=kLoop, calls=%fused_computation.15 | loop fusion | bytes 5242888 | tf_op jit(solution)/shard_map/dynamic_slice | solution.py:303
  21.9 0.4 collective-permute-start.6
  22.2 1.6 all-to-all-done
  23.8 5.6 %all-to-all-start.1 = ((bf16[16,32,1024]{2,1,0:T(8,128)(2,1)}), bf16[16,32,1024]{2,1,0:T(8,128)(2,1)}, u32[]{:S(2)}, u32[]{:S(2)}) async-start(bf16[16,32,1024]{2,1,0:T(8,128)(2,1)} %bitcast.95), calls=%async_computation.1 | async-start | bytes 2097152 | tf_op jit(solution)/shard_map/all_to_all | solution.py:318
  29.4 0.5 shard_map.69
  29.9 0.8 copy-done.5
  30.7 2.9 %collective-permute-start.3 = (bf16[512,256]{1,0:T(8,128)(2,1)S(1)}, bf16[512,256]{1,0:T(8,128)(2,1)S(1)}, u32[]{:S(2)}, u32[]{:S(2)}) collective-permute-start(bf16[512,256]{1,0:T(8,128)(2,1)S(1)} %get-tuple-element.30.kv0_ref), channel_id=1, source_target_pairs={{0,4},{1,5},{2,6},{3,7},{8,12},{9,13},{10,14},{11,15},{16,20},{17,... | collective-permute-start | bytes 786440 | tf_op jit(solution)/shard_map/ppermute | solution.py:329
  33.6 5.4 %collective-permute-start.2 = (bf16[512,256]{1,0:T(8,128)(2,1)S(1)}, bf16[512,256]{1,0:T(8,128)(2,1)}, u32[]{:S(2)}, u32[]{:S(2)}) collective-permute-start(bf16[512,256]{1,0:T(8,128)(2,1)S(1)} %get-tuple-element.30.kv0_ref), channel_id=1, source_target_pairs={{0,3},{1,4},{2,5},{3,6},{4,7},{8,11},{9,12},{10,13},{11,14},{12,15... | collective-permute-start | bytes 786440 | tf_op jit(solution)/shard_map/ppermute | solution.py:329
  39.0 14.5 %collective-permute-done.3.kv4_ref = bf16[512,256]{1,0:T(8,128)(2,1)S(1)} collective-permute-done((bf16[512,256]{1,0:T(8,128)(2,1)S(1)}, bf16[512,256]{1,0:T(8,128)(2,1)S(1)}, u32[]{:S(2)}, u32[]{:S(2)}) %collective-permute-start.3) | collective-permute-done | bytes 262176 | tf_op jit(solution)/shard_map/ppermute | solution.py:329
  53.5 5.6 %collective-permute-start.1 = (bf16[512,256]{1,0:T(8,128)(2,1)S(1)}, bf16[512,256]{1,0:T(8,128)(2,1)}, u32[]{:S(2)}, u32[]{:S(2)}) collective-permute-start(bf16[512,256]{1,0:T(8,128)(2,1)S(1)} %get-tuple-element.30.kv0_ref), channel_id=1, source_target_pairs={{0,2},{1,3},{2,4},{3,5},{4,6},{5,7},{8,10},{9,11},{10,12},{11,13},... | collective-permute-start | bytes 786440 | tf_op jit(solution)/shard_map/ppermute | solution.py:329
  59.1 2.0 %collective-permute-start = (bf16[512,256]{1,0:T(8,128)(2,1)S(1)}, bf16[512,256]{1,0:T(8,128)(2,1)}, u32[]{:S(2)}, u32[]{:S(2)}) collective-permute-start(bf16[512,256]{1,0:T(8,128)(2,1)S(1)} %get-tuple-element.30.kv0_ref), channel_id=1, source_target_pairs={{0,1},{1,2},{2,3},{3,4},{4,5},{5,6},{6,7},{8,9},{9,10},{10,11},{11... | collective-permute-start | bytes 786440 | tf_op jit(solution)/shard_map/ppermute | solution.py:329
  61.2 4.0 %collective-permute-done.1.kv2_ref = bf16[512,256]{1,0:T(8,128)(2,1)} collective-permute-done((bf16[512,256]{1,0:T(8,128)(2,1)S(1)}, bf16[512,256]{1,0:T(8,128)(2,1)}, u32[]{:S(2)}, u32[]{:S(2)}) %collective-permute-start.1) | collective-permute-done | bytes 262176 | tf_op jit(solution)/shard_map/ppermute | solution.py:329
  65.2 4.4 %collective-permute-done.kv1_ref = bf16[512,256]{1,0:T(8,128)(2,1)} collective-permute-done((bf16[512,256]{1,0:T(8,128)(2,1)S(1)}, bf16[512,256]{1,0:T(8,128)(2,1)}, u32[]{:S(2)}, u32[]{:S(2)}) %collective-permute-start) | collective-permute-done | bytes 262176 | tf_op jit(solution)/shard_map/ppermute | solution.py:329
  69.6 1.0 copy-done.6
  70.6 8.0 %shard_map.70 = (bf16[512,1024]{1,0:T(8,128)(2,1)}, bf16[1024,512]{1,0:T(8,128)(2,1)S(1)}, bf16[1024,512]{1,0:T(8,128)(2,1)S(1)}) custom-call(s32[1]{0:T(128)} %bitcast.slot_ref, s32[1,4]{1,0:T(1,128)S(1)} %copy-done.4, s32[2,64]{1,0:T(2,128)S(1)} %multiply_add_fusion.table_ref, bf16[512,512]{1,0:T(8,128)(2,1)S(1)} %copy-done.6, ...), custom_call_target="tpu_custom_call" | custom-call | flops 10000000000 | bytes 6291456 | tf_op jit(solution)/shard_map/pallas_call | solution.py:101
  78.6 2.7 %collective-permute-done.7.left2_ref = bf16[1024,512]{1,0:T(8,128)(2,1)S(1)} collective-permute-done((bf16[1024,512]{1,0:T(8,128)(2,1)S(1)}, bf16[1024,512]{1,0:T(8,128)(2,1)S(1)}, u32[]{:S(2)}, u32[]{:S(2)}) %collective-permute-start.7) | collective-permute-done | bytes 1048608 | tf_op jit(solution)/shard_map/ppermute | solution.py:358
  81.3 2.8 %shard_map.76 = bf16[512,1280]{1,0:T(8,128)(2,1)S(1)} custom-call(bf16[1024,512]{1,0:T(8,128)(2,1)S(1)} %get-tuple-element.36.left_ref, bf16[1024,512]{1,0:T(8,128)(2,1)S(1)} %collective-permute-done.7.left2_ref, bf16[512,1280]{1,0:T(8,128)(2,1)S(1)} %copy-done, bf16[512,1280]{1,0:T(8,128)(2,1)} %collective-permute-done.6.other_ref), custom_call_target="tpu_custom_call" | custom-call | flops 1342177280 | bytes 5242880 | tf_op jit(solution)/shard_map/pallas_call | solution.py:101
  84.1 8.4 %collective-permute-start.14 = (bf16[512,1280]{1,0:T(8,128)(2,1)S(1)}, bf16[512,1280]{1,0:T(8,128)(2,1)S(1)}, u32[]{:S(2)}, u32[]{:S(2)}) collective-permute-start(bf16[512,1280]{1,0:T(8,128)(2,1)S(1)} %shard_map.76), channel_id=1, source_target_pairs={{0,4},{1,5},{2,6},{3,7},{4,0},{5,1},{6,2},{7,3},{8,28},{9,29},{10,... | collective-permute-start | bytes 3932168 | tf_op jit(solution)/shard_map/ppermute | solution.py:371
  92.5 3.2 %shard_map.72 = bf16[512,1408]{1,0:T(8,128)(2,1)S(1)} custom-call(bf16[1024,512]{1,0:T(8,128)(2,1)S(1)} %get-tuple-element.36.left_ref, bf16[1024,512]{1,0:T(8,128)(2,1)S(1)} %collective-permute-done.7.left2_ref, bf16[512,1408]{1,0:T(8,128)(2,1)S(1)} %get-tuple-element.38.own_ref, bf16[512,1408]{1,0:T(8,128)(2,1)} %collective-permute-done.4.other_ref), custom_call_target="tpu_custom_call" | custom-call | flops 1476395008 | bytes 5242880 | tf_op jit(solution)/shard_map/pallas_call | solution.py:101
  95.7 3.7 %collective-permute-start.8 = (bf16[512,1408]{1,0:T(8,128)(2,1)S(1)}, bf16[512,1408]{1,0:T(8,128)(2,1)S(1)}, u32[]{:S(2)}, u32[]{:S(2)}) collective-permute-start(bf16[512,1408]{1,0:T(8,128)(2,1)S(1)} %shard_map.72), channel_id=1, source_target_pairs={{0,1},{1,0},{2,3},{3,2},{4,5},{5,4},{6,7},{7,6},{8,11},{9,10},{10,... | collective-permute-start | bytes 4325384 | tf_op jit(solution)/shard_map/ppermute | solution.py:371
  99.4 3.2 %shard_map.74 = bf16[512,1408]{1,0:T(8,128)(2,1)S(1)} custom-call(bf16[1024,512]{1,0:T(8,128)(2,1)S(1)} %get-tuple-element.36.left_ref, bf16[1024,512]{1,0:T(8,128)(2,1)S(1)} %collective-permute-done.7.left2_ref, bf16[512,1408]{1,0:T(8,128)(2,1)S(1)} %get-tuple-element.40.own_ref, bf16[512,1408]{1,0:T(8,128)(2,1)} %collective-permute-done.5.other_ref), custom_call_target="tpu_custom_call" | custom-call | flops 1476395008 | bytes 5242880 | tf_op jit(solution)/shard_map/pallas_call | solution.py:101
  102.6 3.2 %shard_map.73 = bf16[512,1408]{1,0:T(8,128)(2,1)S(1)} custom-call(bf16[1024,512]{1,0:T(8,128)(2,1)S(1)} %get-tuple-element.36.left_ref, bf16[1024,512]{1,0:T(8,128)(2,1)S(1)} %collective-permute-done.7.left2_ref, bf16[512,1408]{1,0:T(8,128)(2,1)S(1)} %get-tuple-element.40.own_ref, bf16[512,1408]{1,0:T(8,128)(2,1)} %collective-permute-done.5.other_ref), custom_call_target="tpu_custom_call" | custom-call | flops 1476395008 | bytes 5242880 | tf_op jit(solution)/shard_map/pallas_call | solution.py:101
  105.8 2.8 %shard_map.75 = bf16[512,1280]{1,0:T(8,128)(2,1)S(1)} custom-call(bf16[1024,512]{1,0:T(8,128)(2,1)S(1)} %get-tuple-element.36.left_ref, bf16[1024,512]{1,0:T(8,128)(2,1)S(1)} %collective-permute-done.7.left2_ref, bf16[512,1280]{1,0:T(8,128)(2,1)S(1)} %copy-done, bf16[512,1280]{1,0:T(8,128)(2,1)} %collective-permute-done.6.other_ref), custom_call_target="tpu_custom_call" | custom-call | flops 1342177280 | bytes 5242880 | tf_op jit(solution)/shard_map/pallas_call | solution.py:101
  108.6 3.2 %shard_map.71 = bf16[512,1408]{1,0:T(8,128)(2,1)S(1)} custom-call(bf16[1024,512]{1,0:T(8,128)(2,1)S(1)} %get-tuple-element.36.left_ref, bf16[1024,512]{1,0:T(8,128)(2,1)S(1)} %collective-permute-done.7.left2_ref, bf16[512,1408]{1,0:T(8,128)(2,1)S(1)} %get-tuple-element.38.own_ref, bf16[512,1408]{1,0:T(8,128)(2,1)} %collective-permute-done.4.other_ref), custom_call_target="tpu_custom_call" | custom-call | flops 1476395008 | bytes 5242880 | tf_op jit(solution)/shard_map/pallas_call | solution.py:101
  112.2 4.1 %collective-permute-done.8 = bf16[512,1408]{1,0:T(8,128)(2,1)S(1)} collective-permute-done((bf16[512,1408]{1,0:T(8,128)(2,1)S(1)}, bf16[512,1408]{1,0:T(8,128)(2,1)S(1)}, u32[]{:S(2)}, u32[]{:S(2)}) %collective-permute-start.8) | collective-permute-done | bytes 1441824 | tf_op jit(solution)/shard_map/ppermute | solution.py:371
  116.3 0.3 convert_add_fusion.1
  116.6 5.0 %collective-permute-done.11 = bf16[512,1408]{1,0:T(8,128)(2,1)S(1)} collective-permute-done((bf16[512,1408]{1,0:T(8,128)(2,1)S(1)}, bf16[512,1408]{1,0:T(8,128)(2,1)S(1)}, u32[]{:S(2)}, u32[]{:S(2)}) %collective-permute-start.11) | collective-permute-done | bytes 1441824 | tf_op jit(solution)/shard_map/ppermute | solution.py:371
  121.6 0.3 convert_add_fusion
  122.4 1.0 collective-permute-done.15
  123.5 1.5 collective-permute-start.16
  125.1 8.5 %collective-permute-done.9 = bf16[256,1408]{1,0:T(8,128)(2,1)S(1)} collective-permute-done((bf16[256,1408]{1,0:T(8,128)(2,1)S(1)}, bf16[256,1408]{1,0:T(8,128)(2,1)S(1)}, u32[]{:S(2)}, u32[]{:S(2)}) %collective-permute-start.9) | collective-permute-done | bytes 720928 | tf_op jit(solution)/shard_map/ppermute | solution.py:388
  134.1 2.9 %collective-permute-done.16 = bf16[128,1280]{1,0:T(8,128)(2,1)S(1)} collective-permute-done((bf16[128,1280]{1,0:T(8,128)(2,1)S(1)}, bf16[128,1280]{1,0:T(8,128)(2,1)S(1)}, u32[]{:S(2)}, u32[]{:S(2)}) %collective-permute-start.16) | collective-permute-done | bytes 327712 | tf_op jit(solution)/shard_map/ppermute | solution.py:388
  137.1 4.1 %collective-permute-done.10 = bf16[128,1408]{1,0:T(8,128)(2,1)S(1)} collective-permute-done((bf16[128,1408]{1,0:T(8,128)(2,1)S(1)}, bf16[128,1408]{1,0:T(8,128)(2,1)S(1)}, u32[]{:S(2)}, u32[]{:S(2)}) %collective-permute-start.10) | collective-permute-done | bytes 360480 | tf_op jit(solution)/shard_map/ppermute | solution.py:388
  141.7 6.1 %collective-permute-start.17 = (bf16[64,4096]{1,0:T(8,128)(2,1)S(1)}, bf16[64,4096]{1,0:T(8,128)(2,1)S(1)}, u32[]{:S(2)}, u32[]{:S(2)}) collective-permute-start(bf16[64,4096]{1,0:T(8,128)(2,1)S(1)} %pad_maximum_fusion), channel_id=1, source_target_pairs={{0,3},{1,2},{2,1},{3,0},{4,7},{5,6},{6,5},{7,4},{8,9},{9,8},{10,11... | collective-permute-start | bytes 1572872 | tf_op jit(solution)/shard_map/ppermute | solution.py:395
  147.9 7.1 %collective-permute-done.17 = bf16[64,4096]{1,0:T(8,128)(2,1)S(1)} collective-permute-done((bf16[64,4096]{1,0:T(8,128)(2,1)S(1)}, bf16[64,4096]{1,0:T(8,128)(2,1)S(1)}, u32[]{:S(2)}, u32[]{:S(2)}) %collective-permute-start.17) | collective-permute-done | bytes 524320 | tf_op jit(solution)/shard_map/ppermute | solution.py:395
  155.2 4.8 %collective-permute-start.18 = (bf16[32,4096]{1,0:T(8,128)(2,1)S(1)}, bf16[32,4096]{1,0:T(8,128)(2,1)S(1)}, u32[]{:S(2)}, u32[]{:S(2)}) collective-permute-start(bf16[32,4096]{1,0:T(8,128)(2,1)S(1)} %slice.207), channel_id=1, source_target_pairs={{0,96},{1,97},{2,98},{3,99},{4,100},{5,101},{6,102},{7,103},{8,40}... | collective-permute-start | bytes 786440 | tf_op jit(solution)/shard_map/ppermute | solution.py:395
  160.0 4.4 %collective-permute-done.18 = bf16[32,4096]{1,0:T(8,128)(2,1)S(1)} collective-permute-done((bf16[32,4096]{1,0:T(8,128)(2,1)S(1)}, bf16[32,4096]{1,0:T(8,128)(2,1)S(1)}, u32[]{:S(2)}, u32[]{:S(2)}) %collective-permute-start.18) | collective-permute-done | bytes 262176 | tf_op jit(solution)/shard_map/ppermute | solution.py:395
  164.4 1.6 collective-permute-start.19
  166.0 4.7 %collective-permute-done.19 = bf16[16,4096]{1,0:T(8,128)(2,1)S(1)} collective-permute-done((bf16[16,4096]{1,0:T(8,128)(2,1)S(1)}, bf16[16,4096]{1,0:T(8,128)(2,1)S(1)}, u32[]{:S(2)}, u32[]{:S(2)}) %collective-permute-start.19) | collective-permute-done | bytes 131104 | tf_op jit(solution)/shard_map/ppermute | solution.py:395
  170.9 1.2 collective-permute-done.20
  172.1 0.7 maximum_select_fusion
  (59 shorter events, 2.8 us)
Async XLA Ops:
  0.6 1.3 copy-start.2
  1.9 0.7 copy-start.3
  4.2 1.0 copy-start.1
  5.1 18.7 %all-to-all-start = ((bf16[16,32,384]{2,1,0:T(8,128)(2,1)}), bf16[16,32,384]{2,1,0:T(8,128)(2,1)S(1)}, u32[]{:S(2)}, u32[]{:S(2)}) async-start(bf16[16,32,384]{2,1,0:T(8,128)(2,1)} %bitcast.5), calls=%async_computation | async-start | bytes 786432 | tf_op jit(solution)/shard_map/all_to_all | solution.py:315
  17.9 51.7 %collective-permute-start.5 = (bf16[512,1408]{1,0:T(8,128)(2,1)}, bf16[512,1408]{1,0:T(8,128)(2,1)}, u32[]{:S(2)}, u32[]{:S(2)}) collective-permute-start(bf16[512,1408]{1,0:T(8,128)(2,1)} %get-tuple-element.46), channel_id=1, source_target_pairs={{0,8},{1,9},{2,10},{3,11},{4,12},{5,13},{6,14},{7,15},{8,0},{9,1},... | collective-permute-start | bytes 4325384 | tf_op jit(solution)/shard_map/ppermute | solution.py:302
  18.2 51.3 %collective-permute-start.4 = (bf16[512,1408]{1,0:T(8,128)(2,1)}, bf16[512,1408]{1,0:T(8,128)(2,1)}, u32[]{:S(2)}, u32[]{:S(2)}) collective-permute-start(bf16[512,1408]{1,0:T(8,128)(2,1)} %get-tuple-element.47), channel_id=1, source_target_pairs={{0,8},{1,9},{2,10},{3,11},{4,12},{5,13},{6,14},{7,15},{8,0},{9,1},... | collective-permute-start | bytes 4325384 | tf_op jit(solution)/shard_map/ppermute | solution.py:302
  21.9 39.2 %copy-start.7 = (s32[2,64,3]{1,0,2:T(2,128)S(1)}, s32[2,64,3]{1,0,2:T(2,128)}, u32[]{:S(2)}) copy-start(s32[2,64,3]{1,0,2:T(2,128)} %constant.121) | copy-start | bytes 4612
  21.9 39.2 %copy-start.8 = (s32[2,64,3]{1,0,2:T(2,128)S(1)}, s32[2,64,3]{1,0,2:T(2,128)}, u32[]{:S(2)}) copy-start(s32[2,64,3]{1,0,2:T(2,128)} %constant.116.clone) | copy-start | bytes 4612
  21.9 47.7 %collective-permute-start.6 = (bf16[512,1280]{1,0:T(8,128)(2,1)}, bf16[512,1280]{1,0:T(8,128)(2,1)}, u32[]{:S(2)}, u32[]{:S(2)}) collective-permute-start(bf16[512,1280]{1,0:T(8,128)(2,1)} %get-tuple-element.44), channel_id=1, source_target_pairs={{0,8},{1,9},{2,10},{3,11},{4,12},{5,13},{6,14},{7,15},{8,0},{9,1},... | collective-permute-start | bytes 3932168 | tf_op jit(solution)/shard_map/ppermute | solution.py:302
  23.8 45.8 %copy-start.4 = (s32[1,4]{1,0:T(1,128)S(1)}, s32[1,4]{1,0:T(1,128)}, u32[]{:S(2)}) copy-start(s32[1,4]{1,0:T(1,128)} %lengths_ref.1) | copy-start | bytes 52
  23.8 45.7 %all-to-all-start.1 = ((bf16[16,32,1024]{2,1,0:T(8,128)(2,1)}), bf16[16,32,1024]{2,1,0:T(8,128)(2,1)}, u32[]{:S(2)}, u32[]{:S(2)}) async-start(bf16[16,32,1024]{2,1,0:T(8,128)(2,1)} %bitcast.95), calls=%async_computation.1 | async-start | bytes 2097152 | tf_op jit(solution)/shard_map/all_to_all | solution.py:318
  29.9 0.8 copy-start.5
  30.7 22.8 %collective-permute-start.3 = (bf16[512,256]{1,0:T(8,128)(2,1)S(1)}, bf16[512,256]{1,0:T(8,128)(2,1)S(1)}, u32[]{:S(2)}, u32[]{:S(2)}) collective-permute-start(bf16[512,256]{1,0:T(8,128)(2,1)S(1)} %get-tuple-element.30.kv0_ref), channel_id=1, source_target_pairs={{0,4},{1,5},{2,6},{3,7},{8,12},{9,13},{10,14},{11,15},{16,20},{17,... | collective-permute-start | bytes 786440 | tf_op jit(solution)/shard_map/ppermute | solution.py:329
  33.6 25.5 %collective-permute-start.2 = (bf16[512,256]{1,0:T(8,128)(2,1)S(1)}, bf16[512,256]{1,0:T(8,128)(2,1)}, u32[]{:S(2)}, u32[]{:S(2)}) collective-permute-start(bf16[512,256]{1,0:T(8,128)(2,1)S(1)} %get-tuple-element.30.kv0_ref), channel_id=1, source_target_pairs={{0,3},{1,4},{2,5},{3,6},{4,7},{8,11},{9,12},{10,13},{11,14},{12,15... | collective-permute-start | bytes 786440 | tf_op jit(solution)/shard_map/ppermute | solution.py:329
  53.5 11.7 %collective-permute-start.1 = (bf16[512,256]{1,0:T(8,128)(2,1)S(1)}, bf16[512,256]{1,0:T(8,128)(2,1)}, u32[]{:S(2)}, u32[]{:S(2)}) collective-permute-start(bf16[512,256]{1,0:T(8,128)(2,1)S(1)} %get-tuple-element.30.kv0_ref), channel_id=1, source_target_pairs={{0,2},{1,3},{2,4},{3,5},{4,6},{5,7},{8,10},{9,11},{10,12},{11,13},... | collective-permute-start | bytes 786440 | tf_op jit(solution)/shard_map/ppermute | solution.py:329
  59.1 10.4 %collective-permute-start = (bf16[512,256]{1,0:T(8,128)(2,1)S(1)}, bf16[512,256]{1,0:T(8,128)(2,1)}, u32[]{:S(2)}, u32[]{:S(2)}) collective-permute-start(bf16[512,256]{1,0:T(8,128)(2,1)S(1)} %get-tuple-element.30.kv0_ref), channel_id=1, source_target_pairs={{0,1},{1,2},{2,3},{3,4},{4,5},{5,6},{6,7},{8,9},{9,10},{10,11},{11... | collective-permute-start | bytes 786440 | tf_op jit(solution)/shard_map/ppermute | solution.py:329
  69.6 1.0 copy-start.6
  70.6 10.7 %copy-start = (bf16[512,1280]{1,0:T(8,128)(2,1)S(1)}, bf16[512,1280]{1,0:T(8,128)(2,1)}, u32[]{:S(2)}) copy-start(bf16[512,1280]{1,0:T(8,128)(2,1)} %get-tuple-element.42.own_ref) | copy-start | bytes 3932164
  78.6 2.7 %collective-permute-start.7 = (bf16[1024,512]{1,0:T(8,128)(2,1)S(1)}, bf16[1024,512]{1,0:T(8,128)(2,1)S(1)}, u32[]{:S(2)}, u32[]{:S(2)}) collective-permute-start(bf16[1024,512]{1,0:T(8,128)(2,1)S(1)} %get-tuple-element.37), channel_id=1, source_target_pairs={{0,8},{1,9},{2,10},{3,11},{4,12},{5,13},{6,14},{7,15},{8,0},{9,1},... | collective-permute-start | bytes 3145736 | tf_op jit(solution)/shard_map/ppermute | solution.py:358
  84.1 27.7 %collective-permute-start.14 = (bf16[512,1280]{1,0:T(8,128)(2,1)S(1)}, bf16[512,1280]{1,0:T(8,128)(2,1)S(1)}, u32[]{:S(2)}, u32[]{:S(2)}) collective-permute-start(bf16[512,1280]{1,0:T(8,128)(2,1)S(1)} %shard_map.76), channel_id=1, source_target_pairs={{0,4},{1,5},{2,6},{3,7},{4,0},{5,1},{6,2},{7,3},{8,28},{9,29},{10,... | collective-permute-start | bytes 3932168 | tf_op jit(solution)/shard_map/ppermute | solution.py:371
  95.7 20.7 %collective-permute-start.8 = (bf16[512,1408]{1,0:T(8,128)(2,1)S(1)}, bf16[512,1408]{1,0:T(8,128)(2,1)S(1)}, u32[]{:S(2)}, u32[]{:S(2)}) collective-permute-start(bf16[512,1408]{1,0:T(8,128)(2,1)S(1)} %shard_map.72), channel_id=1, source_target_pairs={{0,1},{1,0},{2,3},{3,2},{4,5},{5,4},{6,7},{7,6},{8,11},{9,10},{10,... | collective-permute-start | bytes 4325384 | tf_op jit(solution)/shard_map/ppermute | solution.py:371
  102.5 19.1 %collective-permute-start.11 = (bf16[512,1408]{1,0:T(8,128)(2,1)S(1)}, bf16[512,1408]{1,0:T(8,128)(2,1)S(1)}, u32[]{:S(2)}, u32[]{:S(2)}) collective-permute-start(bf16[512,1408]{1,0:T(8,128)(2,1)S(1)} %shard_map.74), channel_id=1, source_target_pairs={{0,32},{1,33},{2,34},{3,35},{4,36},{5,37},{6,38},{7,39},{8,104},{9... | collective-permute-start | bytes 4325384 | tf_op jit(solution)/shard_map/ppermute | solution.py:371
  112.2 11.2 %collective-permute-start.15 = (bf16[256,1280]{1,0:T(8,128)(2,1)S(1)}, bf16[256,1280]{1,0:T(8,128)(2,1)S(1)}, u32[]{:S(2)}, u32[]{:S(2)}) collective-permute-start(bf16[256,1280]{1,0:T(8,128)(2,1)S(1)} %fusion.5), channel_id=1, source_target_pairs={{0,1},{1,0},{2,3},{3,2},{4,5},{5,4},{6,7},{7,6},{8,11},{9,10},{10,... | collective-permute-start | bytes 1966088 | tf_op jit(solution)/shard_map/ppermute | solution.py:388
  122.2 11.4 %collective-permute-start.9 = (bf16[256,1408]{1,0:T(8,128)(2,1)S(1)}, bf16[256,1408]{1,0:T(8,128)(2,1)S(1)}, u32[]{:S(2)}, u32[]{:S(2)}) collective-permute-start(bf16[256,1408]{1,0:T(8,128)(2,1)S(1)} %fusion.2), channel_id=1, source_target_pairs={{0,32},{1,33},{2,34},{3,35},{4,36},{5,37},{6,38},{7,39},{8,104},{9... | collective-permute-start | bytes 2162696 | tf_op jit(solution)/shard_map/ppermute | solution.py:388
  122.3 11.6 %collective-permute-start.12 = (bf16[256,1408]{1,0:T(8,128)(2,1)S(1)}, bf16[256,1408]{1,0:T(8,128)(2,1)S(1)}, u32[]{:S(2)}, u32[]{:S(2)}) collective-permute-start(bf16[256,1408]{1,0:T(8,128)(2,1)S(1)} %bitcast.116), channel_id=1, source_target_pairs={{0,4},{1,5},{2,6},{3,7},{4,0},{5,1},{6,2},{7,3},{8,28},{9,29},{10,... | collective-permute-start | bytes 2162696 | tf_op jit(solution)/shard_map/ppermute | solution.py:388
  123.5 13.5 %collective-permute-start.16 = (bf16[128,1280]{1,0:T(8,128)(2,1)S(1)}, bf16[128,1280]{1,0:T(8,128)(2,1)S(1)}, u32[]{:S(2)}, u32[]{:S(2)}) collective-permute-start(bf16[128,1280]{1,0:T(8,128)(2,1)S(1)} %fusion.9), channel_id=1, source_target_pairs={{0,32},{1,33},{2,34},{3,35},{4,36},{5,37},{6,38},{7,39},{8,104},{9... | collective-permute-start | bytes 983048 | tf_op jit(solution)/shard_map/ppermute | solution.py:388
  133.7 7.5 %collective-permute-start.10 = (bf16[128,1408]{1,0:T(8,128)(2,1)S(1)}, bf16[128,1408]{1,0:T(8,128)(2,1)S(1)}, u32[]{:S(2)}, u32[]{:S(2)}) collective-permute-start(bf16[128,1408]{1,0:T(8,128)(2,1)S(1)} %fusion.7), channel_id=1, source_target_pairs={{0,4},{1,5},{2,6},{3,7},{4,0},{5,1},{6,2},{7,3},{8,28},{9,29},{10,... | collective-permute-start | bytes 1081352 | tf_op jit(solution)/shard_map/ppermute | solution.py:388
  134.0 7.5 %collective-permute-start.13 = (bf16[128,1408]{1,0:T(8,128)(2,1)S(1)}, bf16[128,1408]{1,0:T(8,128)(2,1)S(1)}, u32[]{:S(2)}, u32[]{:S(2)}) collective-permute-start(bf16[128,1408]{1,0:T(8,128)(2,1)S(1)} %fusion.8), channel_id=1, source_target_pairs={{0,1},{1,0},{2,3},{3,2},{4,5},{5,4},{6,7},{7,6},{8,11},{9,10},{10,... | collective-permute-start | bytes 1081352 | tf_op jit(solution)/shard_map/ppermute | solution.py:388
  141.7 13.3 %collective-permute-start.17 = (bf16[64,4096]{1,0:T(8,128)(2,1)S(1)}, bf16[64,4096]{1,0:T(8,128)(2,1)S(1)}, u32[]{:S(2)}, u32[]{:S(2)}) collective-permute-start(bf16[64,4096]{1,0:T(8,128)(2,1)S(1)} %pad_maximum_fusion), channel_id=1, source_target_pairs={{0,3},{1,2},{2,1},{3,0},{4,7},{5,6},{6,5},{7,4},{8,9},{9,8},{10,11... | collective-permute-start | bytes 1572872 | tf_op jit(solution)/shard_map/ppermute | solution.py:395
  155.2 9.2 %collective-permute-start.18 = (bf16[32,4096]{1,0:T(8,128)(2,1)S(1)}, bf16[32,4096]{1,0:T(8,128)(2,1)S(1)}, u32[]{:S(2)}, u32[]{:S(2)}) collective-permute-start(bf16[32,4096]{1,0:T(8,128)(2,1)S(1)} %slice.207), channel_id=1, source_target_pairs={{0,96},{1,97},{2,98},{3,99},{4,100},{5,101},{6,102},{7,103},{8,40}... | collective-permute-start | bytes 786440 | tf_op jit(solution)/shard_map/ppermute | solution.py:395
  164.4 6.3 %collective-permute-start.19 = (bf16[16,4096]{1,0:T(8,128)(2,1)S(1)}, bf16[16,4096]{1,0:T(8,128)(2,1)S(1)}, u32[]{:S(2)}, u32[]{:S(2)}) collective-permute-start(bf16[16,4096]{1,0:T(8,128)(2,1)S(1)} %slice.208), channel_id=1, source_target_pairs={{0,20},{1,21},{2,22},{3,23},{4,16},{5,17},{6,18},{7,19},{8,12},{9,... | collective-permute-start | bytes 393224 | tf_op jit(solution)/shard_map/ppermute | solution.py:395
  170.8 1.3 collective-permute-start.20
where the time goes:
time: 174 us; the launch traced here: 173 us
  waiting for transfers between devices  70.2 us (40%)
  starting transfers between devices  57.2 us (33%)
  Pallas kernels  28.3 us (16%)
  local copies, waits for them, and re-layouts  13.7 us (8%)
  other arithmetic  2.39 us (1%)
    pallas_call x9, Pallas kernels, vmem_call(): pl.pallas_call(body, out_shape=out_shape, in_specs=specs, out_specs=out_s...  28.3 us
    ppermute x4, waiting for transfers between devices, body(): lax.ppermute(key_vals, 'ctx', [(at, at + back) for at in range(SLOTS - ba...  22.8 us
    ppermute x6, waiting for transfers between devices, body(): lax.ppermute(sends[part], AXES, flip_pairs([ORDERS[c][part][level] for c...  16.7 us
    ppermute x3, waiting for transfers between devices, body(): lax.ppermute(send, AXES, flip_pairs([ORDERS[c][0][level] for c in range(2...  16.1 us
    ppermute x4, starting transfers between devices, body(): lax.ppermute(key_vals, 'ctx', [(at, at + back) for at in range(SLOTS - ba...  15.9 us
    ppermute x3, starting transfers between devices, body(): lax.ppermute(send, AXES, flip_pairs([ORDERS[c][0][level] for c in range(2...  12.6 us
    ppermute x3, starting transfers between devices, body(): lax.ppermute(sends[part], AXES, flip_pairs([ORDERS[c][part][0] for c in r...  12.1 us
    ppermute x3, waiting for transfers between devices, body(): lax.ppermute(sends[part], AXES, flip_pairs([ORDERS[c][part][0] for c in r...  9.08 us
  transfers between devices with their start and end apart: 23, of which 16 were waited for; matrix products, arithmetic and copies ran while one was open for 6% of the time, Pallas kernels for 9%

commit v1 on v0

v1 whole, which is shorter than its diff:
```python
import functools

import jax
import jax.numpy as jnp
import numpy as np
from jax import lax
from jax.experimental import pallas as pl
from jax.experimental.pallas import tpu as pltpu
from jax.sharding import PartitionSpec as P

HQ = 8
DH = 128
ROWS = 512
GROUPS = 16
SLOTS = 8
BACK = 4
QUERIES = HQ * DH
HEAD = 3 * DH
SENT = QUERIES + HEAD
TILE = 256
AXES = ("dp", "ctx")
CHIPS = 64
MIB = 1024 * 1024
SCORE_FLOOR = -1e30
TOTAL_LIMIT = 2.0**90
EXP_SCALE = float(DH**-0.5 * np.log2(np.e))
WIDTHS = (1536, 1408, 1152)
OFFSETS = (0, 1536, 2944)
HALF = 4096

FLIPS = {
    "xa": (1, 0, 0),
    "xb": (3, 0, 0),
    "ya": (0, 1, 0),
    "yb": (0, 3, 0),
    "za": (0, 0, 1),
    "zb": (0, 0, 3),
}
SET_A = ("xa", "ya", "za")
SET_B = ("xb", "yb", "zb")


def rotate(names, by):
    return names[by:] + names[:by]


ORDERS = (
    tuple(rotate(SET_A, part) + SET_B for part in range(3)),
    tuple(rotate(SET_B, part) + SET_A for part in range(3)),
)


def place_of(index):
    dp, ctx = index // SLOTS, index % SLOTS
    y, z_hi, core = dp // 4, (dp // 2) % 2, dp % 2
    return ctx % 4, y, z_hi * 2 + ctx // 4, core


def index_of(x, y, z, core):
    return (y * 4 + (z // 2) * 2 + core) * SLOTS + (z % 2) * 4 + x


def flip_of(names):
    flips = [FLIPS[name] for name in names]
    return [functools.reduce(lambda a, b: a ^ b, axis) for axis in zip(*flips)]


def flip_pairs(names_of_core):
    pairs = []
    for index in range(2 * CHIPS):
        x, y, z, core = place_of(index)
        names = names_of_core[core]
        fx, fy, fz = flip_of((names,) if isinstance(names, str) else names)
        pairs.append((index, index_of(x ^ fx, y ^ fy, z ^ fz, core)))
    return pairs


def core_pairs():
    pairs = []
    for index in range(2 * CHIPS):
        x, y, z, core = place_of(index)
        pairs.append((index, index_of(x, y, z, 1 - core)))
    return pairs


def flip_table():
    table = np.zeros((2, CHIPS, 3), np.int32)
    for core in range(2):
        for block in range(CHIPS):
            for level, name in enumerate(ORDERS[core][0]):
                if (block >> (5 - level)) & 1:
                    table[core, block] ^= np.array(FLIPS[name], np.int32)
    return table


def dot(a, b, contract):
    return lax.dot_general(
        a, b, ((contract[:1], contract[1:]), ((), ())), preferred_element_type=jnp.float32
    )


def as_bf16(mask):
    return mask.astype(jnp.float32).astype(jnp.bfloat16)


def vmem_call(body, out_shape, scratch=(), smem=0, operands=(), mib=16, flops=0, nbytes=0):
    specs = [pl.BlockSpec(memory_space=pltpu.SMEM)] * smem
    specs += [pl.BlockSpec(memory_space=pltpu.VMEM)] * (len(operands) - smem)
    out_specs = jax.tree.map(lambda _: pl.BlockSpec(memory_space=pltpu.VMEM), out_shape)
    return pl.pallas_call(
        body,
        out_shape=out_shape,
        in_specs=specs,
        out_specs=out_specs,
        scratch_shapes=list(scratch),
        compiler_params=pltpu.CompilerParams(vmem_limit_bytes=mib * MIB),
        cost_estimate=pl.CostEstimate(flops=flops, bytes_accessed=nbytes, transcendentals=0),
    )(*operands)


def sort_kernel(dest_ref, rows_ref, sent_ref, held_ref, sem_ref):
    rows_copy = pltpu.make_async_copy(rows_ref.at[0], held_ref, sem_ref)
    rows_copy.start()
    dest = dest_ref[...]
    target = dest >> 9
    slot = dest & (ROWS - 1)
    member = as_bf16(lax.broadcasted_iota(jnp.int32, (GROUPS, ROWS), 0) == target)
    same = dot(member, member, (0, 0))
    row = lax.broadcasted_iota(jnp.int32, (ROWS, ROWS), 0)
    col = lax.broadcasted_iota(jnp.int32, (ROWS, ROWS), 1)
    rank = jnp.sum(jnp.where(row < col, same, 0.0), axis=0, keepdims=True)
    place = target * (ROWS // GROUPS) + rank.astype(jnp.int32)
    order = as_bf16(row == place)
    line = lax.broadcasted_iota(jnp.int32, (DH, ROWS), 0)
    coded = jnp.where(line == 0, slot >> 4, jnp.where(line == 1, slot & 15, 0))
    coded = coded.astype(jnp.float32).astype(jnp.bfloat16)
    sent_ref[:, 2 * DH : HEAD] = dot(order, coded, (1, 1)).astype(jnp.bfloat16)
    rows_copy.wait()
    sent_ref[:, : 2 * DH] = dot(order, held_ref[:, QUERIES:], (1, 0)).astype(jnp.bfloat16)
    sent_ref[:, HEAD:] = dot(order, held_ref[:, :QUERIES], (1, 0)).astype(jnp.bfloat16)


def place_kernel(got_ref, key_vals_ref, inverse_ref):
    lane = lax.broadcasted_iota(jnp.int32, (16, DH), 1)
    coef = jnp.where(lane == 0, 16.0, jnp.where(lane == 1, 1.0, 0.0)).astype(jnp.bfloat16)
    slots = dot(coef, got_ref[:, 2 * DH :], (1, 1))[:1].astype(jnp.int32)
    inverse = as_bf16(lax.broadcasted_iota(jnp.int32, (ROWS, ROWS), 0) == slots)
    inverse_ref[...] = inverse
    key_vals_ref[...] = dot(
        inverse, got_ref[:, : 2 * DH], (1, 0)
    ).astype(jnp.bfloat16)


def doc_starts(lengths_ref):
    start1 = lengths_ref[0, 0]
    start2 = start1 + lengths_ref[0, 1]
    start3 = start2 + lengths_ref[0, 2]

    def first_of(position):
        found = jnp.where(position >= start1, start1, 0)
        found = jnp.where(position >= start2, start2, found)
        return jnp.where(position >= start3, start3, found)

    return first_of


def visible_keys(first_of, p_first, k_first):
    q_pos = p_first + lax.broadcasted_iota(jnp.int32, (TILE, TILE), 0)
    k_pos = k_first + lax.broadcasted_iota(jnp.int32, (TILE, TILE), 1)
    return (k_pos >= first_of(q_pos)) & (k_pos <= q_pos)


def tile_weights(queries, keys, top, visible):
    scores = dot(queries, keys, (1, 1))
    if visible is not None:
        scores = jnp.where(visible, scores, SCORE_FLOOR)
    top = jnp.concatenate([top] * (scores.shape[1] // DH), axis=1)
    return jnp.exp2(scores * EXP_SCALE - top).astype(jnp.bfloat16)


def rows_of(h, tile=0):
    return slice((tile * HQ + h) * TILE, (tile * HQ + h + 1) * TILE)


def cols_of(h):
    return slice(h * DH, (h + 1) * DH)


def own_kernel(slot_ref, lengths_ref, inverse_ref, got_ref, kv_ref, q_ref, top_ref, acc_ref, v_ref):
    q_ref[...] = dot(inverse_ref[...], got_ref[:, HEAD:], (1, 0)).astype(jnp.bfloat16)
    v_ref[:, :DH] = kv_ref[:, DH:]
    v_ref[:, DH:] = jnp.ones((ROWS, DH), jnp.bfloat16)
    first_of = doc_starts(lengths_ref)
    ones = jnp.ones((DH, DH), jnp.bfloat16)
    for tile in range(ROWS // TILE):
        q_rows = slice(tile * TILE, (tile + 1) * TILE)
        p_first = slot_ref[0] * ROWS + tile * TILE
        own_keys = kv_ref[q_rows, :DH].astype(jnp.float32)
        for h in range(HQ):
            pair = q_ref[q_rows, cols_of(h)].astype(jnp.float32) * own_keys
            top_ref[rows_of(h, tile), :] = (
                dot(pair.astype(jnp.bfloat16), ones, (1, 0)) * EXP_SCALE
            )
        for at in range(tile, -1, -1):
            k_rows = slice(at * TILE, (at + 1) * TILE)
            visible = visible_keys(first_of, p_first, slot_ref[0] * ROWS + at * TILE)
            for h in range(HQ):
                weights = tile_weights(
                    q_ref[q_rows, cols_of(h)],
                    kv_ref[k_rows, :DH],
                    top_ref[rows_of(h, tile), :],
                    visible,
                )
                term = dot(weights, v_ref[k_rows, :], (1, 0))
                if at == tile:
                    acc_ref[rows_of(h, tile), :] = term
                else:
                    acc_ref[rows_of(h, tile), :] += term


def attend_kernel(
    slot_ref,
    lengths_ref,
    table_ref,
    q_ref,
    top_ref,
    total_ref,
    kv_ref,
    near0_ref,
    near1_ref,
    near2_ref,
    far0_ref,
    far1_ref,
    far2_ref,
    last_ref,
    *refs,
):
    grads, refs = refs[:6], refs[6:]
    (out_ref, own_ref, swap_ref), held, refs = refs[:3], refs[3:9], refs[9:]
    k_ref, v_ref, exact_ref, acc_ref, done_ref, sem_ref = refs
    copies = [
        pltpu.make_async_copy(grad_ref, held_ref, sem_ref.at[at])
        for at, (grad_ref, held_ref) in enumerate(zip(grads, held))
    ]
    for copy in copies:
        copy.start()
    slot = slot_ref[0]
    core = slot_ref[1]
    x = slot % 4
    k_ref[BACK * ROWS :, :] = kv_ref[:, :DH]
    v_ref[BACK * ROWS :, :DH] = kv_ref[:, DH:]
    v_ref[:, DH:] = jnp.ones(((BACK + 1) * ROWS, DH), jnp.bfloat16)
    came = (
        (near0_ref, (1, 0), (3, 0)),
        (near1_ref, (3, 0), (0, 1)),
        (near2_ref, (0, 1), (1, 0)),
        (far0_ref, (2, 0), (2, 0)),
        (far1_ref, (3, 1), (3, 1)),
        (far2_ref, (1, 1), (1, 1)),
        (last_ref, (2, 1), (2, 1)),
    )
    for came_ref, flip0, flip1 in came:
        flip_x = jnp.where(core == 0, flip0[0], flip1[0])
        flip_z = jnp.where(core == 0, flip0[1], flip1[1])
        back = slot - ((slot // 4) ^ flip_z) * 4 - (x ^ flip_x)

        @pl.when((back >= 1) & (back <= BACK))
        def _(came_ref=came_ref, back=back):
            at = pl.ds(pl.multiple_of((BACK - back) * ROWS, ROWS), ROWS)
            k_ref[at, :] = came_ref[:, :DH]
            v_ref[at, :DH] = came_ref[:, DH:]

    first_of = doc_starts(lengths_ref)
    for tile in range(ROWS // TILE):
        q_rows = slice(tile * TILE, (tile + 1) * TILE)
        p_first = slot * ROWS + tile * TILE
        low_first = first_of(p_first)
        high_first = first_of(p_first + TILE - 1)
        own_at = BACK * ROWS + tile * TILE
        count = (p_first - low_first + TILE - 1) // TILE
        clear = jnp.maximum(p_first - high_first, 0) // TILE
        acc_ref[...] = total_ref[tile * HQ * TILE : (tile + 1) * HQ * TILE, :]

        def add(j, masked, wide=1, tile=tile, q_rows=q_rows, p_first=p_first, own_at=own_at):
            at = pl.ds(pl.multiple_of(own_at - j * TILE, TILE), wide * TILE)
            visible = visible_keys(first_of, p_first, p_first - j * TILE) if masked else None
            for h in range(HQ):
                weights = tile_weights(
                    q_ref[q_rows, cols_of(h)], k_ref[at, :], top_ref[rows_of(h, tile), :], visible
                )
                acc_ref[rows_of(h), :] += dot(weights, v_ref[at, :], (1, 0))

        clear = jnp.maximum(clear, tile)

        pairs = (clear - tile) // 2

        @pl.loop(0, pairs)
        def _(i):
            add(2 + tile + 2 * i, False, 2)

        @pl.loop(1 + tile + 2 * pairs, 1 + clear)
        def _(j):
            add(j, False)

        @pl.loop(1 + clear, 1 + count)
        def _(j):
            add(j, True)

        @pl.when(jnp.max(acc_ref[:, DH:]) > TOTAL_LIMIT)
        def _(q_rows=q_rows, p_first=p_first, own_at=own_at, count=count):
            exact_ref[...] = jnp.full_like(exact_ref, SCORE_FLOOR)
            acc_ref[...] = jnp.zeros_like(acc_ref)

            @pl.loop(0, 1 + count)
            def _(j):
                at = pl.ds(pl.multiple_of(own_at - j * TILE, TILE), TILE)
                visible = visible_keys(first_of, p_first, p_first - j * TILE)

                @pl.loop(0, HQ)
                def _(h):
                    rows = pl.ds(pl.multiple_of(h * TILE, TILE), TILE)
                    cols = pl.ds(pl.multiple_of(h * DH, DH), DH)
                    scores = dot(q_ref[q_rows, cols], k_ref[at, :], (1, 1))
                    scores = jnp.where(visible, scores, SCORE_FLOOR)
                    old = exact_ref[rows, :]
                    best = jnp.max(scores, axis=1, keepdims=True) * EXP_SCALE
                    top = jnp.maximum(old, best)
                    rescale = jnp.exp2(old - top)
                    exact_ref[rows, :] = top
                    weights = tile_weights(q_ref[q_rows, cols], k_ref[at, :], top, visible)
                    rescale = jnp.concatenate([rescale, rescale], axis=1)
                    acc_ref[rows, :] = acc_ref[rows, :] * rescale + dot(
                        weights, v_ref[at, :], (1, 0)
                    )

        for h in range(HQ):
            done = acc_ref[rows_of(h), :DH] / acc_ref[rows_of(h), DH:]
            out_ref[q_rows, cols_of(h)] = done.astype(jnp.bfloat16)
            done_ref[cols_of(h), q_rows] = done.T

    for side, ordered_ref in enumerate((own_ref, swap_ref)):

        @pl.loop(0, CHIPS, unroll=4)
        def _(block, side=side, ordered_ref=ordered_ref):
            at = pl.multiple_of(table_ref[side, block], 8)
            both = jnp.concatenate(
                [done_ref[pl.ds(at, 8), :], done_ref[pl.ds(at + 64, 8), :]], axis=0
            )
            ordered_ref[pl.ds(pl.multiple_of(block * 16, 16), 16), :] = both.astype(jnp.bfloat16)
    for copy in copies:
        copy.wait()


def project_kernel(level, half, left_ref, left2_ref, own_ref, other_ref, out_ref):
    run = 512 >> level
    step = min(run, 256)
    for at in range(0, 512, step):
        rows = slice(at, at + step)
        source = (at // run) * 2 * run + half * run + at % run
        source = slice(source, source + step)
        term = dot(left_ref[source, :], own_ref[...], (1, 0))
        term += dot(left2_ref[source, :], other_ref[...], (1, 0))
        out_ref[rows, :] = term.astype(out_ref.dtype)


def shape(rows, cols, dtype=jnp.bfloat16):
    return jax.ShapeDtypeStruct((rows, cols), dtype)


def body(qkv_in, dest, lengths, grad_out):
    dp_at = lax.axis_index("dp")
    slot = lax.axis_index("ctx")
    core = dp_at % 2
    x, y, z = slot % 4, dp_at // 4, ((dp_at // 2) % 2) * 2 + slot // 4
    swap = core_pairs()

    tokens = grad_out[0]
    own_cols = [
        lax.dynamic_slice(tokens, (0, core * HALF + at), (ROWS, width))
        for at, width in zip(OFFSETS, WIDTHS)
    ]
    other_cols = [
        lax.ppermute(
            lax.dynamic_slice(tokens, (0, (1 - core) * HALF + at), (ROWS, width)), AXES, swap
        )
        for at, width in zip(OFFSETS, WIDTHS)
    ]

    sent = pl.pallas_call(
        sort_kernel,
        out_shape=shape(ROWS, SENT),
        in_specs=[
            pl.BlockSpec(memory_space=pltpu.VMEM),
            pl.BlockSpec(memory_space=pltpu.HBM),
        ],
        out_specs=pl.BlockSpec(memory_space=pltpu.VMEM),
        scratch_shapes=[
            pltpu.VMEM((ROWS, QUERIES + 2 * DH), jnp.bfloat16),
            pltpu.SemaphoreType.DMA,
        ],
        compiler_params=pltpu.CompilerParams(vmem_limit_bytes=60 * MIB),
        cost_estimate=pl.CostEstimate(flops=10**9, bytes_accessed=3 * MIB, transcendentals=0),
    )(dest, qkv_in)
    got = lax.all_to_all(
        sent.reshape(GROUPS, ROWS // GROUPS, SENT), "dp", 0, 0, tiled=True
    ).reshape(ROWS, SENT)
    key_vals, inverse = pl.pallas_call(
        place_kernel,
        grid=(1,),
        out_shape=(shape(ROWS, 2 * DH), shape(ROWS, ROWS)),
        in_specs=[pl.BlockSpec((ROWS, HEAD), lambda _: (0, 0))],
        out_specs=(
            pl.BlockSpec((ROWS, 2 * DH), lambda _: (0, 0)),
            pl.BlockSpec((ROWS, ROWS), lambda _: (0, 0)),
        ),
        compiler_params=pltpu.CompilerParams(vmem_limit_bytes=8 * MIB),
        cost_estimate=pl.CostEstimate(flops=2 * 10**8, bytes_accessed=MIB, transcendentals=0),
    )(got)
    near0 = lax.ppermute(key_vals, AXES, flip_pairs(("xa", "xb")))
    near1 = lax.ppermute(key_vals, AXES, flip_pairs(("xb", "za")))
    near2 = lax.ppermute(key_vals, AXES, flip_pairs(("za", "xa")))
    far0 = lax.ppermute(near0, AXES, flip_pairs(("xb", "xa")))
    far1 = lax.ppermute(near1, AXES, flip_pairs(("za", "xb")))
    far2 = lax.ppermute(near2, AXES, flip_pairs(("xa", "za")))
    last = lax.ppermute(far0, AXES, flip_pairs(("za", "za")))

    place = jnp.stack([slot, core]).astype(jnp.int32)
    queries, tops, totals = vmem_call(
        own_kernel,
        (
            shape(ROWS, QUERIES),
            shape(2 * HQ * TILE, DH, jnp.float32),
            shape(2 * HQ * TILE, 2 * DH, jnp.float32),
        ),
        scratch=(pltpu.VMEM((ROWS, 2 * DH), jnp.bfloat16),),
        smem=2,
        operands=(place, lengths, inverse, got, key_vals),
        mib=20,
        flops=2 * 10**9,
        nbytes=4 * MIB,
    )

    flips = jnp.asarray(flip_table())
    flips = jnp.where(core == 0, flips, flips[::-1])
    to_x, to_y, to_z = x ^ flips[..., 0], y ^ flips[..., 1], z ^ flips[..., 2]
    table = ((to_y * 2 + to_z // 2) * 128 + ((to_z % 2) * 4 + to_x) * 8).astype(jnp.int32)

    (table, queries, last), own_cols, other_cols = lax.optimization_barrier(
        ((table, queries, last), own_cols, other_cols)
    )
    vmem = pl.BlockSpec(memory_space=pltpu.VMEM)
    smem = pl.BlockSpec(memory_space=pltpu.SMEM)
    columns = (*own_cols, *other_cols)
    attention, left, swap_left, *columns = pl.pallas_call(
        attend_kernel,
        out_shape=(
            shape(ROWS, QUERIES),
            shape(QUERIES, ROWS),
            shape(QUERIES, ROWS),
            *(shape(*a.shape) for a in columns),
        ),
        in_specs=[smem] * 3 + [vmem] * 11 + [pl.BlockSpec(memory_space=pltpu.HBM)] * 6,
        out_specs=(vmem,) * 9,
        scratch_shapes=[
            pltpu.VMEM(((BACK + 1) * ROWS, DH), jnp.bfloat16),
            pltpu.VMEM(((BACK + 1) * ROWS, 2 * DH), jnp.bfloat16),
            pltpu.VMEM((HQ * TILE, DH), jnp.float32),
            pltpu.VMEM((HQ * TILE, 2 * DH), jnp.float32),
            pltpu.VMEM((QUERIES, ROWS), jnp.float32),
            pltpu.SemaphoreType.DMA((6,)),
        ],
        compiler_params=pltpu.CompilerParams(vmem_limit_bytes=28 * MIB),
        cost_estimate=pl.CostEstimate(
            flops=10**10, bytes_accessed=16 * MIB, transcendentals=0
        ),
    )(
        place,
        lengths,
        table,
        queries,
        tops,
        totals,
        key_vals,
        near0,
        near1,
        near2,
        far0,
        far1,
        far2,
        last,
        *columns,
    )
    own_cols, other_cols = columns[:3], columns[3:]
    left2 = lax.ppermute(swap_left, AXES, swap)

    def project(part, half):
        return vmem_call(
            functools.partial(project_kernel, part, half),
            shape(512, WIDTHS[part]),
            operands=(left, left2, own_cols[part], other_cols[part]),
            flops=2 * 512 * 1024 * WIDTHS[part],
            nbytes=5 * MIB,
        )

    sends = []
    for part in range(3):
        sends.append(project(part, 1))
        left, _ = lax.optimization_barrier((left, sends[-1]))
    keeps = [project(part, 0) for part in range(3)]
    for level in range(3):
        coming = [
            lax.ppermute(
                sends[part], AXES, flip_pairs([ORDERS[c][part][level] for c in range(2)])
            )
            for part in range(3)
        ]
        coming, keeps = lax.optimization_barrier((coming, keeps))
        halves = []
        for part in range(3):
            lead = 2 if (level, part) == (0, 1) else 1
            width = WIDTHS[part]
            halves.append(
                [
                    [a.reshape(lead, 2, -1, width)[:, bit].reshape(-1, width).astype(jnp.float32)
                     for a in (keeps[part], coming[part])]
                    for bit in range(2)
                ]
            )
        sends = [(pair[1][0] + pair[1][1]).astype(jnp.bfloat16) for pair in halves]
        keeps = [pair[0][0] + pair[0][1] for pair in halves]
    keep, send = jnp.concatenate(keeps, axis=1), jnp.concatenate(sends, axis=1)
    for level in range(3, 4):
        came = lax.ppermute(send, AXES, flip_pairs([ORDERS[c][0][level] for c in range(2)]))
        total = keep + came.astype(jnp.float32)
        rows = total.shape[0] // 2
        keep, send = total[:rows], total[rows:].astype(jnp.bfloat16)
    blocks = total.reshape(-1, 16, HALF)
    coming = []
    for block in range(blocks.shape[0] - 1, 0, -1):
        names = [
            [ORDERS[c][0][5 - bit] for bit in range(2) if (block >> bit) & 1]
            for c in range(2)
        ]
        coming.append(lax.ppermute(blocks[block].astype(jnp.bfloat16), AXES, flip_pairs(names)))
    coming = lax.optimization_barrier(coming)
    total = blocks[0]
    for came in coming:
        total = total + came.astype(jnp.float32)
    both = total.reshape(2, 8, HALF)
    mine = lax.dynamic_index_in_dim(both, core, 0, keepdims=False)
    theirs = lax.dynamic_index_in_dim(both, 1 - core, 0, keepdims=False).astype(jnp.bfloat16)
    came = lax.ppermute(theirs, AXES, swap).astype(jnp.float32)
    grad_proj = jnp.where(
        core == 0,
        jnp.concatenate([mine, came], axis=1),
        jnp.concatenate([came, mine], axis=1),
    )
    return attention[None], grad_proj


def solution(mesh):
    in_specs = (P("dp", "ctx", None), P("dp", "ctx"), P("dp", None), P("dp", "ctx", None))
    out_specs = (P("dp", "ctx", None), P(("dp", "ctx"), None))
    return jax.shard_map(body, mesh=mesh, in_specs=in_specs, out_specs=out_specs, check_vma=False)
```

time: 174 us -> 152 us (0.87)
  waiting for transfers between devices: 70.2 us -> 59.4 us
  starting transfers between devices: 57.2 us -> 47.6 us
    ppermute x7 -> x10, waiting for transfers between devices: 31.9 us -> 14.5 us  [the longest x1 5.64 us: body(): far0 = lax.ppermute(near0, AXES, flip_pairs(('xb', 'xa')))]
    ppermute x6 -> x9, starting transfers between devices: 2 us -> 17.4 us  [body(): lax.ppermute(sends[part], AXES, flip_pairs([ORDERS[c][part][level] for c...]
    pallas_call x9 -> x7, Pallas kernels: 28.3 us -> 14.5 us  [vmem_call(): pl.pallas_call(body, out_shape=out_shape, in_specs=specs, out_specs=out_s...]
    ppermute x7 -> x10, starting transfers between devices: 28.1 us -> 15.6 us  [the longest x3 5.99 us: body(): lax.ppermute(blocks[block].astype(jnp.bfloat16), AXES, flip_pairs(names))]
    pallas_call x0 -> x3, Pallas kernels: none -> 12.3 us  [the longest x1 6.95 us: body(): pl.pallas_call(attend_kernel, out_shape=(shape(ROWS, QUERIES), shape(QUER...]
    all_to_all x2 -> x1, waiting for transfers between devices: 1.59 us -> 11.1 us  [body(): lax.all_to_all(sent.reshape(GROUPS, ROWS // GROUPS, SENT), 'dp', 0, 0, ti...]
    ppermute x3 -> x1, waiting for transfers between devices: 16.1 us -> 7.16 us  [body(): lax.ppermute(send, AXES, flip_pairs([ORDERS[c][0][level] for c in range(2...]
    ppermute x3 -> x1, starting transfers between devices: 12.6 us -> 5.4 us  [body(): lax.ppermute(send, AXES, flip_pairs([ORDERS[c][0][level] for c in range(2...]
  transfers between devices with their start and end apart: 23 -> 26, of which waited for: 16 -> 13; matrix products, arithmetic and copies ran while one was open for 6% -> 7% of each run, Pallas kernels for 9% -> 9%
where the time goes in v1:
time: 152 us; the launch traced here: 150 us
  waiting for transfers between devices  59.4 us (39%)
  starting transfers between devices  47.6 us (31%)
  Pallas kernels  26.8 us (18%)
  local copies, waits for them, and re-layouts  12.1 us (8%)
  other arithmetic  2.65 us (2%)
    ppermute x9, waiting for transfers between devices, body(): lax.ppermute(sends[part], AXES, flip_pairs([ORDERS[c][part][level] for c...  22.9 us
    ppermute x9, starting transfers between devices, body(): lax.ppermute(sends[part], AXES, flip_pairs([ORDERS[c][part][level] for c...  17.4 us
    pallas_call x7, Pallas kernels, vmem_call(): pl.pallas_call(body, out_shape=out_shape, in_specs=specs, out_specs=out_s...  14.5 us
    all_to_all x1, waiting for transfers between devices, body(): lax.all_to_all(sent.reshape(GROUPS, ROWS // GROUPS, SENT), 'dp', 0, 0, ti...  11.1 us
    dynamic_slice x3, local copies, waits for them, and re-layouts, body(): lax.dynamic_slice(tokens, (0, (1 - core) * HALF + at), (ROWS, width))  10.1 us
    all_to_all x1, starting transfers between devices, body(): lax.all_to_all(sent.reshape(GROUPS, ROWS // GROUPS, SENT), 'dp', 0, 0, ti...  7.98 us
    ppermute x1, waiting for transfers between devices, body(): lax.ppermute(send, AXES, flip_pairs([ORDERS[c][0][level] for c in range(2...  7.16 us
    pallas_call x1, Pallas kernels, body(): pl.pallas_call(attend_kernel, out_shape=(shape(ROWS, QUERIES), shape(QUER...  6.95 us
  transfers between devices with their start and end apart: 26, of which 13 were waited for; matrix products, arithmetic and copies ran while one was open for 7% of the time, Pallas kernels for 9%

profile of v1, /device:TPU:0, one launch (start us, length us, event | category | flops | bytes accessed | tf_op | source)
XLA Modules:
  0.0 149.6 jit_solution(10879856582569902446)
XLA Ops:
  0.6 4.1 %shard_map.68 = bf16[512,1408]{1,0:T(8,128)(2,1)} custom-call(s32[1,512]{1,0:T(1,128)} %dest_ref.1, bf16[1,512,1280]{2,1,0:T(8,128)(2,1)} %rows_ref.1), custom_call_target="tpu_custom_call" | custom-call | flops 1000000000 | bytes 3145728 | tf_op jit(solution)/shard_map/pallas_call | solution.py:389
  4.8 8.0 %all-to-all-start = ((bf16[16,32,1408]{2,1,0:T(8,128)(2,1)}), bf16[16,32,1408]{2,1,0:T(8,128)(2,1)S(1)}, u32[]{:S(2)}, u32[]{:S(2)}) async-start(bf16[16,32,1408]{2,1,0:T(8,128)(2,1)} %bitcast.103), calls=%async_computation | async-start | bytes 2883584 | tf_op jit(solution)/shard_map/all_to_all | solution.py:404
  12.8 3.3 %dynamic-slice_bitcast_fusion.4 = (bf16[512,1152]{1,0:T(8,128)(2,1)}, bf16[512,1152]{1,0:T(8,128)(2,1)}) fusion(bf16[1,512,8192]{2,1,0:T(8,128)(2,1)} %param.8, s32[]{:T(128)S(6)} %select_n.92, s32[]{:T(128)S(6)} %select_n.89), kind=kLoop, calls=%fused_computation.10 | loop fusion | bytes 4718600 | tf_op jit(solution)/shard_map/dynamic_slice | solution.py:384
  16.1 0.4 collective-permute-start.5
  16.4 3.2 %dynamic-slice_bitcast_fusion = (bf16[512,1536]{1,0:T(8,128)(2,1)}, bf16[512,1536]{1,0:T(8,128)(2,1)S(1)}) fusion(bf16[1,512,8192]{2,1,0:T(8,128)(2,1)} %param.8, s32[]{:T(128)S(6)} %select_n.90, s32[]{:T(128)S(6)} %select_n.87), kind=kLoop, calls=%fused_computation.2 | loop fusion | bytes 6291464 | tf_op jit(solution)/shard_map/dynamic_slice | solution.py:384
  19.8 3.6 %dynamic-slice_bitcast_fusion.2 = (bf16[512,1408]{1,0:T(8,128)(2,1)}, bf16[512,1408]{1,0:T(8,128)(2,1)}) fusion(bf16[1,512,8192]{2,1,0:T(8,128)(2,1)} %param.8, s32[]{:T(128)S(6)} %select_n.91, s32[]{:T(128)S(6)} %select_n.88), kind=kLoop, calls=%fused_computation.6 | loop fusion | bytes 5767176 | tf_op jit(solution)/shard_map/dynamic_slice | solution.py:384
  23.4 0.4 collective-permute-start.4
  23.9 11.1 %all-to-all-done = bf16[16,32,1408]{2,1,0:T(8,128)(2,1)S(1)} async-done(((bf16[16,32,1408]{2,1,0:T(8,128)(2,1)}), bf16[16,32,1408]{2,1,0:T(8,128)(2,1)S(1)}, u32[]{:S(2)}, u32[]{:S(2)}) %all-to-all-start) | async-done | bytes 1441824 | tf_op jit(solution)/shard_map/all_to_all | solution.py:404
  34.9 1.2 shard_map.69
  36.1 1.5 collective-permute-start
  37.6 1.0 collective-permute-start.7
  38.7 2.1 %collective-permute-start.6 = (bf16[512,256]{1,0:T(8,128)(2,1)}, bf16[512,256]{1,0:T(8,128)(2,1)}, u32[]{:S(2)}, u32[]{:S(2)}) collective-permute-start(bf16[512,256]{1,0:T(8,128)(2,1)} %get-tuple-element.50.kv_ref), channel_id=1, source_target_pairs={{0,3},{1,2},{2,1},{3,0},{4,7},{5,6},{6,5},{7,4},{8,12},{9,13},{10,... | collective-permute-start | bytes 786440 | tf_op jit(solution)/shard_map/ppermute | solution.py:420
  40.8 3.9 %collective-permute-done.near0_ref = bf16[512,256]{1,0:T(8,128)(2,1)} collective-permute-done((bf16[512,256]{1,0:T(8,128)(2,1)}, bf16[512,256]{1,0:T(8,128)(2,1)}, u32[]{:S(2)}, u32[]{:S(2)}) %collective-permute-start) | collective-permute-done | bytes 262176 | tf_op jit(solution)/shard_map/ppermute | solution.py:419
  44.7 2.6 %collective-permute-start.1 = (bf16[512,256]{1,0:T(8,128)(2,1)}, bf16[512,256]{1,0:T(8,128)(2,1)}, u32[]{:S(2)}, u32[]{:S(2)}) collective-permute-start(bf16[512,256]{1,0:T(8,128)(2,1)} %collective-permute-done.near0_ref), channel_id=1, source_target_pairs={{0,3},{1,2},{2,1},{3,0},{4,7},{5,6},{6,5},{7,4},{8,9},{9,8},{10,11... | collective-permute-start | bytes 786440 | tf_op jit(solution)/shard_map/ppermute | solution.py:422
  47.4 0.4 collective-permute-start.9
  47.7 1.0 collective-permute-start.8
  48.8 5.6 %collective-permute-done.1.far0_ref = bf16[512,256]{1,0:T(8,128)(2,1)} collective-permute-done((bf16[512,256]{1,0:T(8,128)(2,1)}, bf16[512,256]{1,0:T(8,128)(2,1)}, u32[]{:S(2)}, u32[]{:S(2)}) %collective-permute-start.1) | collective-permute-done | bytes 262176 | tf_op jit(solution)/shard_map/ppermute | solution.py:422
  54.4 1.0 collective-permute-start.2
  55.5 4.1 %shard_map.70 = (bf16[512,1024]{1,0:T(8,128)(2,1)S(1)}, f32[4096,128]{1,0:T(8,128)S(1)}, f32[4096,256]{1,0:T(8,128)S(1)}) custom-call(s32[2]{0:T(128)S(1)} %pad_add_fusion.slot_ref, s32[1,4]{1,0:T(1,128)S(1)} %copy-done.2, bf16[512,512]{1,0:T(8,128)(2,1)S(1)} %get-tuple-element.49.inverse_ref, bf16[512,1408]{1,0:T(8,128)(2,1)S(1)} %bitcast.93, ...), custom_call_target="tpu_custom_call" | custom-call | flops 2000000000 | bytes 4194304 | tf_op jit(solution)/shard_map/pallas_call | solution.py:110
  59.6 1.9 %copy-done.3 = f32[4096,256]{1,0:T(8,128)} copy-done((f32[4096,256]{1,0:T(8,128)}, f32[4096,256]{1,0:T(8,128)S(1)}, u32[]{:S(2)}) %copy-start.3) | copy-done | bytes 4194328
  61.6 6.9 %shard_map.71 = (bf16[512,1024]{1,0:T(8,128)(2,1)}, bf16[1024,512]{1,0:T(8,128)(2,1)S(1)}, bf16[1024,512]{1,0:T(8,128)(2,1)S(1)}, bf16[512,1536]{1,0:T(8,128)(2,...) custom-call(s32[2]{0:T(128)S(1)} %pad_add_fusion.slot_ref, ...), custom_call_target="tpu_custom_call" | custom-call | flops 10000000000 | bytes 16777216 | tf_op jit(solution)/shard_map/pallas_call | solution.py:454
  68.7 2.6 %collective-permute-done.10.left2_ref = bf16[1024,512]{1,0:T(8,128)(2,1)S(1)} collective-permute-done((bf16[1024,512]{1,0:T(8,128)(2,1)S(1)}, bf16[1024,512]{1,0:T(8,128)(2,1)S(1)}, u32[]{:S(2)}, u32[]{:S(2)}) %collective-permute-start.10) | collective-permute-done | bytes 1048608 | tf_op jit(solution)/shard_map/ppermute | solution.py:494
  71.3 1.8 %shard_map.72 = bf16[512,1536]{1,0:T(8,128)(2,1)S(1)} custom-call(bf16[1024,512]{1,0:T(8,128)(2,1)S(1)} %get-tuple-element.74.left_ref, bf16[1024,512]{1,0:T(8,128)(2,1)S(1)} %collective-permute-done.10.left2_ref, bf16[512,1536]{1,0:T(8,128)(2,1)S(1)} %get-tuple-element.66.own_ref, bf16[512,1536]{1,0:T(8,128)(2,1)S(1)} %get-tuple-element.67.other_ref), custom_call_target="tpu_custom_call" | custom-call | flops 1610612736 | bytes 5242880 | tf_op jit(solution)/shard_map/pallas_call | solution.py:110
  73.1 5.4 %collective-permute-start.11 = (bf16[512,1536]{1,0:T(8,128)(2,1)S(1)}, bf16[512,1536]{1,0:T(8,128)(2,1)S(1)}, u32[]{:S(2)}, u32[]{:S(2)}) collective-permute-start(bf16[512,1536]{1,0:T(8,128)(2,1)S(1)} %shard_map.72), channel_id=1, source_target_pairs={{0,1},{1,0},{2,3},{3,2},{4,5},{5,4},{6,7},{7,6},{8,11},{9,10},{10,... | collective-permute-start | bytes 4718600 | tf_op jit(solution)/shard_map/ppermute | solution.py:512
  78.5 1.8 %shard_map.73 = bf16[512,1408]{1,0:T(8,128)(2,1)S(1)} custom-call(bf16[1024,512]{1,0:T(8,128)(2,1)S(1)} %get-tuple-element.74.left_ref, bf16[1024,512]{1,0:T(8,128)(2,1)S(1)} %collective-permute-done.10.left2_ref, bf16[512,1408]{1,0:T(8,128)(2,1)S(1)} %get-tuple-element.69.own_ref, bf16[512,1408]{1,0:T(8,128)(2,1)S(1)} %get-tuple-element.70.other_ref), custom_call_target="tpu_custom_call" | custom-call | flops 1476395008 | bytes 5242880 | tf_op jit(solution)/shard_map/pallas_call | solution.py:110
  80.4 1.6 %shard_map.74 = bf16[512,1152]{1,0:T(8,128)(2,1)S(1)} custom-call(bf16[1024,512]{1,0:T(8,128)(2,1)S(1)} %get-tuple-element.74.left_ref, bf16[1024,512]{1,0:T(8,128)(2,1)S(1)} %collective-permute-done.10.left2_ref, bf16[512,1152]{1,0:T(8,128)(2,1)S(1)} %get-tuple-element.72.own_ref, bf16[512,1152]{1,0:T(8,128)(2,1)S(1)} %get-tuple-element.73.other_ref), custom_call_target="tpu_custom_call" | custom-call | flops 1207959552 | bytes 5242880 | tf_op jit(solution)/shard_map/pallas_call | solution.py:110
  82.0 2.8 %collective-permute-start.13 = (bf16[512,1152]{1,0:T(8,128)(2,1)S(1)}, bf16[512,1152]{1,0:T(8,128)(2,1)S(1)}, u32[]{:S(2)}, u32[]{:S(2)}) collective-permute-start(bf16[512,1152]{1,0:T(8,128)(2,1)S(1)} %shard_map.74), channel_id=1, source_target_pairs={{0,4},{1,5},{2,6},{3,7},{4,0},{5,1},{6,2},{7,3},{8,28},{9,29},{10,... | collective-permute-start | bytes 3538952 | tf_op jit(solution)/shard_map/ppermute | solution.py:512
  84.8 1.6 %shard_map.77 = bf16[512,1152]{1,0:T(8,128)(2,1)S(1)} custom-call(bf16[1024,512]{1,0:T(8,128)(2,1)S(1)} %get-tuple-element.74.left_ref, bf16[1024,512]{1,0:T(8,128)(2,1)S(1)} %collective-permute-done.10.left2_ref, bf16[512,1152]{1,0:T(8,128)(2,1)S(1)} %get-tuple-element.72.own_ref, bf16[512,1152]{1,0:T(8,128)(2,1)S(1)} %get-tuple-element.73.other_ref), custom_call_target="tpu_custom_call" | custom-call | flops 1207959552 | bytes 5242880 | tf_op jit(solution)/shard_map/pallas_call | solution.py:110
  86.4 1.8 %shard_map.76 = bf16[512,1408]{1,0:T(8,128)(2,1)S(1)} custom-call(bf16[1024,512]{1,0:T(8,128)(2,1)S(1)} %get-tuple-element.74.left_ref, bf16[1024,512]{1,0:T(8,128)(2,1)S(1)} %collective-permute-done.10.left2_ref, bf16[512,1408]{1,0:T(8,128)(2,1)S(1)} %get-tuple-element.69.own_ref, bf16[512,1408]{1,0:T(8,128)(2,1)S(1)} %get-tuple-element.70.other_ref), custom_call_target="tpu_custom_call" | custom-call | flops 1476395008 | bytes 5242880 | tf_op jit(solution)/shard_map/pallas_call | solution.py:110
  88.2 1.8 %shard_map.75 = bf16[512,1536]{1,0:T(8,128)(2,1)S(1)} custom-call(bf16[1024,512]{1,0:T(8,128)(2,1)S(1)} %get-tuple-element.74.left_ref, bf16[1024,512]{1,0:T(8,128)(2,1)S(1)} %collective-permute-done.10.left2_ref, bf16[512,1536]{1,0:T(8,128)(2,1)S(1)} %get-tuple-element.66.own_ref, bf16[512,1536]{1,0:T(8,128)(2,1)S(1)} %get-tuple-element.67.other_ref), custom_call_target="tpu_custom_call" | custom-call | flops 1610612736 | bytes 5242880 | tf_op jit(solution)/shard_map/pallas_call | solution.py:110
  90.1 8.9 %collective-permute-done.13 = bf16[512,1152]{1,0:T(8,128)(2,1)S(1)} collective-permute-done((bf16[512,1152]{1,0:T(8,128)(2,1)S(1)}, bf16[512,1152]{1,0:T(8,128)(2,1)S(1)}, u32[]{:S(2)}, u32[]{:S(2)}) %collective-permute-start.13) | collective-permute-done | bytes 1179680 | tf_op jit(solution)/shard_map/ppermute | solution.py:512
  99.0 0.4 collective-permute-done.12
  99.8 1.2 collective-permute-start.14
  101.3 1.5 collective-permute-start.15
  103.0 2.1 %collective-permute-start.16 = (bf16[256,1152]{1,0:T(8,128)(2,1)S(1)}, bf16[256,1152]{1,0:T(8,128)(2,1)S(1)}, u32[]{:S(2)}, u32[]{:S(2)}) collective-permute-start(bf16[256,1152]{1,0:T(8,128)(2,1)S(1)} %get-tuple-element.111), channel_id=1, source_target_pairs={{0,1},{1,0},{2,3},{3,2},{4,5},{5,4},{6,7},{7,6},{8,11},{9,10},{10,... | collective-permute-start | bytes 1769480 | tf_op jit(solution)/shard_map/ppermute | solution.py:512
  105.1 7.9 %collective-permute-done.16 = bf16[256,1152]{1,0:T(8,128)(2,1)S(1)} collective-permute-done((bf16[256,1152]{1,0:T(8,128)(2,1)S(1)}, bf16[256,1152]{1,0:T(8,128)(2,1)S(1)}, u32[]{:S(2)}, u32[]{:S(2)}) %collective-permute-start.16) | collective-permute-done | bytes 589856 | tf_op jit(solution)/shard_map/ppermute | solution.py:512
  113.2 1.1 collective-permute-start.17
  114.5 2.1 %collective-permute-start.18 = (bf16[128,1408]{1,0:T(8,128)(2,1)S(1)}, bf16[128,1408]{1,0:T(8,128)(2,1)S(1)}, u32[]{:S(2)}, u32[]{:S(2)}) collective-permute-start(bf16[128,1408]{1,0:T(8,128)(2,1)S(1)} %get-tuple-element.113), channel_id=1, source_target_pairs={{0,1},{1,0},{2,3},{3,2},{4,5},{5,4},{6,7},{7,6},{8,11},{9,10},{10,... | collective-permute-start | bytes 1081352 | tf_op jit(solution)/shard_map/ppermute | solution.py:512
  116.7 1.2 collective-permute-start.19
  117.9 5.6 %collective-permute-done.19 = bf16[128,1152]{1,0:T(8,128)(2,1)S(1)} collective-permute-done((bf16[128,1152]{1,0:T(8,128)(2,1)S(1)}, bf16[128,1152]{1,0:T(8,128)(2,1)S(1)}, u32[]{:S(2)}, u32[]{:S(2)}) %collective-permute-start.19) | collective-permute-done | bytes 294944 | tf_op jit(solution)/shard_map/ppermute | solution.py:512
  123.8 5.4 %collective-permute-start.20 = (bf16[64,4096]{1,0:T(8,128)(2,1)S(1)}, bf16[64,4096]{1,0:T(8,128)(2,1)S(1)}, u32[]{:S(2)}, u32[]{:S(2)}) collective-permute-start(bf16[64,4096]{1,0:T(8,128)(2,1)S(1)} %pad_maximum_fusion), channel_id=1, source_target_pairs={{0,3},{1,2},{2,1},{3,0},{4,7},{5,6},{6,5},{7,4},{8,9},{9,8},{10,11... | collective-permute-start | bytes 1572872 | tf_op jit(solution)/shard_map/ppermute | solution.py:533
  129.2 7.2 %collective-permute-done.20 = bf16[64,4096]{1,0:T(8,128)(2,1)S(1)} collective-permute-done((bf16[64,4096]{1,0:T(8,128)(2,1)S(1)}, bf16[64,4096]{1,0:T(8,128)(2,1)S(1)}, u32[]{:S(2)}, u32[]{:S(2)}) %collective-permute-start.20) | collective-permute-done | bytes 524320 | tf_op jit(solution)/shard_map/ppermute | solution.py:533
  136.5 2.5 %collective-permute-start.23 = (bf16[16,4096]{1,0:T(8,128)(2,1)S(1)}, bf16[16,4096]{1,0:T(8,128)(2,1)S(1)}, u32[]{:S(2)}, u32[]{:S(2)}) collective-permute-start(bf16[16,4096]{1,0:T(8,128)(2,1)S(1)} %get-tuple-element.122), channel_id=1, source_target_pairs={{0,20},{1,21},{2,22},{3,23},{4,16},{5,17},{6,18},{7,19},{8,12},{9,... | collective-permute-start | bytes 393224 | tf_op jit(solution)/shard_map/ppermute | solution.py:544
  139.1 3.4 %collective-permute-start.21 = (bf16[16,4096]{1,0:T(8,128)(2,1)S(1)}, bf16[16,4096]{1,0:T(8,128)(2,1)S(1)}, u32[]{:S(2)}, u32[]{:S(2)}) collective-permute-start(bf16[16,4096]{1,0:T(8,128)(2,1)S(1)} %get-tuple-element.124), channel_id=1, source_target_pairs={{0,116},{1,117},{2,118},{3,119},{4,112},{5,113},{6,114},{7,115},{8... | collective-permute-start | bytes 393224 | tf_op jit(solution)/shard_map/ppermute | solution.py:544
  142.8 2.5 %collective-permute-done.22 = bf16[16,4096]{1,0:T(8,128)(2,1)S(1)} collective-permute-done((bf16[16,4096]{1,0:T(8,128)(2,1)S(1)}, bf16[16,4096]{1,0:T(8,128)(2,1)S(1)}, u32[]{:S(2)}, u32[]{:S(2)}) %collective-permute-start.22) | collective-permute-done | bytes 131104 | tf_op jit(solution)/shard_map/ppermute | solution.py:544
  145.2 2.2 %collective-permute-done.21 = bf16[16,4096]{1,0:T(8,128)(2,1)S(1)} collective-permute-done((bf16[16,4096]{1,0:T(8,128)(2,1)S(1)}, bf16[16,4096]{1,0:T(8,128)(2,1)S(1)}, u32[]{:S(2)}, u32[]{:S(2)}) %collective-permute-start.21) | collective-permute-done | bytes 131104 | tf_op jit(solution)/shard_map/ppermute | solution.py:544
  147.6 1.2 collective-permute-done.24
  148.9 0.7 maximum_select_fusion
  (49 shorter events, 2.8 us)
Async XLA Ops:
  4.8 30.2 %all-to-all-start = ((bf16[16,32,1408]{2,1,0:T(8,128)(2,1)}), bf16[16,32,1408]{2,1,0:T(8,128)(2,1)S(1)}, u32[]{:S(2)}, u32[]{:S(2)}) async-start(bf16[16,32,1408]{2,1,0:T(8,128)(2,1)} %bitcast.103), calls=%async_computation | async-start | bytes 2883584 | tf_op jit(solution)/shard_map/all_to_all | solution.py:404
  16.1 22.6 %collective-permute-start.5 = (bf16[512,1152]{1,0:T(8,128)(2,1)}, bf16[512,1152]{1,0:T(8,128)(2,1)}, u32[]{:S(2)}, u32[]{:S(2)}) collective-permute-start(bf16[512,1152]{1,0:T(8,128)(2,1)} %get-tuple-element.98), channel_id=1, source_target_pairs={{0,8},{1,9},{2,10},{3,11},{4,12},{5,13},{6,14},{7,15},{8,0},{9,1},... | collective-permute-start | bytes 3538952 | tf_op jit(solution)/shard_map/ppermute | solution.py:383
  19.7 41.9 %collective-permute-start.3 = (bf16[512,1536]{1,0:T(8,128)(2,1)}, bf16[512,1536]{1,0:T(8,128)(2,1)}, u32[]{:S(2)}, u32[]{:S(2)}) collective-permute-start(bf16[512,1536]{1,0:T(8,128)(2,1)} %get-tuple-element.102), channel_id=1, source_target_pairs={{0,8},{1,9},{2,10},{3,11},{4,12},{5,13},{6,14},{7,15},{8,0},{9,1},... | collective-permute-start | bytes 4718600 | tf_op jit(solution)/shard_map/ppermute | solution.py:383
  23.4 23.9 %copy-start.4 = (s32[2,64,3]{1,0,2:T(2,128)S(1)}, s32[2,64,3]{1,0,2:T(2,128)}, u32[]{:S(2)}) copy-start(s32[2,64,3]{1,0,2:T(2,128)} %constant.121) | copy-start | bytes 4612
  23.4 23.9 %copy-start.5 = (s32[2,64,3]{1,0,2:T(2,128)S(1)}, s32[2,64,3]{1,0,2:T(2,128)}, u32[]{:S(2)}) copy-start(s32[2,64,3]{1,0,2:T(2,128)} %constant.116.clone) | copy-start | bytes 4612
  23.4 32.1 %copy-start.2 = (s32[1,4]{1,0:T(1,128)S(1)}, s32[1,4]{1,0:T(1,128)}, u32[]{:S(2)}) copy-start(s32[1,4]{1,0:T(1,128)} %lengths_ref.3) | copy-start | bytes 52
  23.4 38.2 %collective-permute-start.4 = (bf16[512,1408]{1,0:T(8,128)(2,1)}, bf16[512,1408]{1,0:T(8,128)(2,1)}, u32[]{:S(2)}, u32[]{:S(2)}) collective-permute-start(bf16[512,1408]{1,0:T(8,128)(2,1)} %get-tuple-element.100), channel_id=1, source_target_pairs={{0,8},{1,9},{2,10},{3,11},{4,12},{5,13},{6,14},{7,15},{8,0},{9,1},... | collective-permute-start | bytes 4325384 | tf_op jit(solution)/shard_map/ppermute | solution.py:383
  36.1 8.5 %collective-permute-start = (bf16[512,256]{1,0:T(8,128)(2,1)}, bf16[512,256]{1,0:T(8,128)(2,1)}, u32[]{:S(2)}, u32[]{:S(2)}) collective-permute-start(bf16[512,256]{1,0:T(8,128)(2,1)} %get-tuple-element.50.kv_ref), channel_id=1, source_target_pairs={{0,1},{1,0},{2,3},{3,2},{4,5},{5,4},{6,7},{7,6},{8,11},{9,10},{10,... | collective-permute-start | bytes 786440 | tf_op jit(solution)/shard_map/ppermute | solution.py:419
  37.6 9.7 %collective-permute-start.7 = (bf16[512,256]{1,0:T(8,128)(2,1)}, bf16[512,256]{1,0:T(8,128)(2,1)}, u32[]{:S(2)}, u32[]{:S(2)}) collective-permute-start(bf16[512,256]{1,0:T(8,128)(2,1)} %get-tuple-element.50.kv_ref), channel_id=1, source_target_pairs={{0,4},{1,5},{2,6},{3,7},{4,0},{5,1},{6,2},{7,3},{8,9},{9,8},{10,11... | collective-permute-start | bytes 786440 | tf_op jit(solution)/shard_map/ppermute | solution.py:421
  38.7 9.1 %collective-permute-start.6 = (bf16[512,256]{1,0:T(8,128)(2,1)}, bf16[512,256]{1,0:T(8,128)(2,1)}, u32[]{:S(2)}, u32[]{:S(2)}) collective-permute-start(bf16[512,256]{1,0:T(8,128)(2,1)} %get-tuple-element.50.kv_ref), channel_id=1, source_target_pairs={{0,3},{1,2},{2,1},{3,0},{4,7},{5,6},{6,5},{7,4},{8,12},{9,13},{10,... | collective-permute-start | bytes 786440 | tf_op jit(solution)/shard_map/ppermute | solution.py:420
  44.7 9.7 %collective-permute-start.1 = (bf16[512,256]{1,0:T(8,128)(2,1)}, bf16[512,256]{1,0:T(8,128)(2,1)}, u32[]{:S(2)}, u32[]{:S(2)}) collective-permute-start(bf16[512,256]{1,0:T(8,128)(2,1)} %collective-permute-done.near0_ref), channel_id=1, source_target_pairs={{0,3},{1,2},{2,1},{3,0},{4,7},{5,6},{6,5},{7,4},{8,9},{9,8},{10,11... | collective-permute-start | bytes 786440 | tf_op jit(solution)/shard_map/ppermute | solution.py:422
  47.4 14.2 %collective-permute-start.9 = (bf16[512,256]{1,0:T(8,128)(2,1)}, bf16[512,256]{1,0:T(8,128)(2,1)S(1)}, u32[]{:S(2)}, u32[]{:S(2)}) collective-permute-start(bf16[512,256]{1,0:T(8,128)(2,1)} %collective-permute-done.7.near2_ref), channel_id=1, source_target_pairs={{0,1},{1,0},{2,3},{3,2},{4,5},{5,4},{6,7},{7,6},{8,12},{9,13},{10,... | collective-permute-start | bytes 786440 | tf_op jit(solution)/shard_map/ppermute | solution.py:424
  47.7 13.9 %collective-permute-start.8 = (bf16[512,256]{1,0:T(8,128)(2,1)}, bf16[512,256]{1,0:T(8,128)(2,1)S(1)}, u32[]{:S(2)}, u32[]{:S(2)}) collective-permute-start(bf16[512,256]{1,0:T(8,128)(2,1)} %collective-permute-done.6.near1_ref), channel_id=1, source_target_pairs={{0,4},{1,5},{2,6},{3,7},{4,0},{5,1},{6,2},{7,3},{8,11},{9,10},{10,... | collective-permute-start | bytes 786440 | tf_op jit(solution)/shard_map/ppermute | solution.py:423
  54.4 7.2 %collective-permute-start.2 = (bf16[512,256]{1,0:T(8,128)(2,1)}, bf16[512,256]{1,0:T(8,128)(2,1)S(1)}, u32[]{:S(2)}, u32[]{:S(2)}) collective-permute-start(bf16[512,256]{1,0:T(8,128)(2,1)} %collective-permute-done.1.far0_ref), channel_id=1, source_target_pairs={{0,4},{1,5},{2,6},{3,7},{4,0},{5,1},{6,2},{7,3},{8,12},{9,13},{10,... | collective-permute-start | bytes 786440 | tf_op jit(solution)/shard_map/ppermute | solution.py:425
  55.5 6.1 %copy-start = (bf16[512,1408]{1,0:T(8,128)(2,1)S(1)}, bf16[512,1408]{1,0:T(8,128)(2,1)}, u32[]{:S(2)}) copy-start(bf16[512,1408]{1,0:T(8,128)(2,1)} %get-tuple-element.58.refs_1_) | copy-start | bytes 4325380
  55.5 6.1 %copy-start.1 = (bf16[512,1152]{1,0:T(8,128)(2,1)S(1)}, bf16[512,1152]{1,0:T(8,128)(2,1)}, u32[]{:S(2)}) copy-start(bf16[512,1152]{1,0:T(8,128)(2,1)} %get-tuple-element.59.refs_2_) | copy-start | bytes 3538948
  59.6 2.0 %copy-start.3 = (f32[4096,256]{1,0:T(8,128)}, f32[4096,256]{1,0:T(8,128)S(1)}, u32[]{:S(2)}) copy-start(f32[4096,256]{1,0:T(8,128)S(1)} %get-tuple-element.55.total_ref) | copy-start | bytes 12582916
  68.6 2.7 %collective-permute-start.10 = (bf16[1024,512]{1,0:T(8,128)(2,1)S(1)}, bf16[1024,512]{1,0:T(8,128)(2,1)S(1)}, u32[]{:S(2)}, u32[]{:S(2)}) collective-permute-start(bf16[1024,512]{1,0:T(8,128)(2,1)S(1)} %get-tuple-element.65), channel_id=1, source_target_pairs={{0,8},{1,9},{2,10},{3,11},{4,12},{5,13},{6,14},{7,15},{8,0},{9,1},... | collective-permute-start | bytes 3145736 | tf_op jit(solution)/shard_map/ppermute | solution.py:494
  73.1 26.3 %collective-permute-start.11 = (bf16[512,1536]{1,0:T(8,128)(2,1)S(1)}, bf16[512,1536]{1,0:T(8,128)(2,1)S(1)}, u32[]{:S(2)}, u32[]{:S(2)}) collective-permute-start(bf16[512,1536]{1,0:T(8,128)(2,1)S(1)} %shard_map.72), channel_id=1, source_target_pairs={{0,1},{1,0},{2,3},{3,2},{4,5},{5,4},{6,7},{7,6},{8,11},{9,10},{10,... | collective-permute-start | bytes 4718600 | tf_op jit(solution)/shard_map/ppermute | solution.py:512
  80.3 19.1 %collective-permute-start.12 = (bf16[512,1408]{1,0:T(8,128)(2,1)S(1)}, bf16[512,1408]{1,0:T(8,128)(2,1)S(1)}, u32[]{:S(2)}, u32[]{:S(2)}) collective-permute-start(bf16[512,1408]{1,0:T(8,128)(2,1)S(1)} %shard_map.73), channel_id=1, source_target_pairs={{0,32},{1,33},{2,34},{3,35},{4,36},{5,37},{6,38},{7,39},{8,104},{9... | collective-permute-start | bytes 4325384 | tf_op jit(solution)/shard_map/ppermute | solution.py:512
  82.0 17.0 %collective-permute-start.13 = (bf16[512,1152]{1,0:T(8,128)(2,1)S(1)}, bf16[512,1152]{1,0:T(8,128)(2,1)S(1)}, u32[]{:S(2)}, u32[]{:S(2)}) collective-permute-start(bf16[512,1152]{1,0:T(8,128)(2,1)S(1)} %shard_map.74), channel_id=1, source_target_pairs={{0,4},{1,5},{2,6},{3,7},{4,0},{5,1},{6,2},{7,3},{8,28},{9,29},{10,... | collective-permute-start | bytes 3538952 | tf_op jit(solution)/shard_map/ppermute | solution.py:512
  99.8 13.2 %collective-permute-start.14 = (bf16[256,1536]{1,0:T(8,128)(2,1)S(1)}, bf16[256,1536]{1,0:T(8,128)(2,1)S(1)}, u32[]{:S(2)}, u32[]{:S(2)}) collective-permute-start(bf16[256,1536]{1,0:T(8,128)(2,1)S(1)} %get-tuple-element.105), channel_id=1, source_target_pairs={{0,32},{1,33},{2,34},{3,35},{4,36},{5,37},{6,38},{7,39},{8,104},{9... | collective-permute-start | bytes 2359304 | tf_op jit(solution)/shard_map/ppermute | solution.py:512
  101.3 11.7 %collective-permute-start.15 = (bf16[256,1408]{1,0:T(8,128)(2,1)S(1)}, bf16[256,1408]{1,0:T(8,128)(2,1)S(1)}, u32[]{:S(2)}, u32[]{:S(2)}) collective-permute-start(bf16[256,1408]{1,0:T(8,128)(2,1)S(1)} %bitcast.107), channel_id=1, source_target_pairs={{0,4},{1,5},{2,6},{3,7},{4,0},{5,1},{6,2},{7,3},{8,28},{9,29},{10,... | collective-permute-start | bytes 2162696 | tf_op jit(solution)/shard_map/ppermute | solution.py:512
  103.0 10.0 %collective-permute-start.16 = (bf16[256,1152]{1,0:T(8,128)(2,1)S(1)}, bf16[256,1152]{1,0:T(8,128)(2,1)S(1)}, u32[]{:S(2)}, u32[]{:S(2)}) collective-permute-start(bf16[256,1152]{1,0:T(8,128)(2,1)S(1)} %get-tuple-element.111), channel_id=1, source_target_pairs={{0,1},{1,0},{2,3},{3,2},{4,5},{5,4},{6,7},{7,6},{8,11},{9,10},{10,... | collective-permute-start | bytes 1769480 | tf_op jit(solution)/shard_map/ppermute | solution.py:512
  113.2 10.3 %collective-permute-start.17 = (bf16[128,1536]{1,0:T(8,128)(2,1)S(1)}, bf16[128,1536]{1,0:T(8,128)(2,1)S(1)}, u32[]{:S(2)}, u32[]{:S(2)}) collective-permute-start(bf16[128,1536]{1,0:T(8,128)(2,1)S(1)} %get-tuple-element.109), channel_id=1, source_target_pairs={{0,4},{1,5},{2,6},{3,7},{4,0},{5,1},{6,2},{7,3},{8,28},{9,29},{10,... | collective-permute-start | bytes 1179656 | tf_op jit(solution)/shard_map/ppermute | solution.py:512
  114.5 9.0 %collective-permute-start.18 = (bf16[128,1408]{1,0:T(8,128)(2,1)S(1)}, bf16[128,1408]{1,0:T(8,128)(2,1)S(1)}, u32[]{:S(2)}, u32[]{:S(2)}) collective-permute-start(bf16[128,1408]{1,0:T(8,128)(2,1)S(1)} %get-tuple-element.113), channel_id=1, source_target_pairs={{0,1},{1,0},{2,3},{3,2},{4,5},{5,4},{6,7},{7,6},{8,11},{9,10},{10,... | collective-permute-start | bytes 1081352 | tf_op jit(solution)/shard_map/ppermute | solution.py:512
  116.7 6.8 %collective-permute-start.19 = (bf16[128,1152]{1,0:T(8,128)(2,1)S(1)}, bf16[128,1152]{1,0:T(8,128)(2,1)S(1)}, u32[]{:S(2)}, u32[]{:S(2)}) collective-permute-start(bf16[128,1152]{1,0:T(8,128)(2,1)S(1)} %get-tuple-element.115), channel_id=1, source_target_pairs={{0,32},{1,33},{2,34},{3,35},{4,36},{5,37},{6,38},{7,39},{8,104},{9... | collective-permute-start | bytes 884744 | tf_op jit(solution)/shard_map/ppermute | solution.py:512
  123.8 12.6 %collective-permute-start.20 = (bf16[64,4096]{1,0:T(8,128)(2,1)S(1)}, bf16[64,4096]{1,0:T(8,128)(2,1)S(1)}, u32[]{:S(2)}, u32[]{:S(2)}) collective-permute-start(bf16[64,4096]{1,0:T(8,128)(2,1)S(1)} %pad_maximum_fusion), channel_id=1, source_target_pairs={{0,3},{1,2},{2,1},{3,0},{4,7},{5,6},{6,5},{7,4},{8,9},{9,8},{10,11... | collective-permute-start | bytes 1572872 | tf_op jit(solution)/shard_map/ppermute | solution.py:533
  136.5 6.3 %collective-permute-start.23 = (bf16[16,4096]{1,0:T(8,128)(2,1)S(1)}, bf16[16,4096]{1,0:T(8,128)(2,1)S(1)}, u32[]{:S(2)}, u32[]{:S(2)}) collective-permute-start(bf16[16,4096]{1,0:T(8,128)(2,1)S(1)} %get-tuple-element.122), channel_id=1, source_target_pairs={{0,20},{1,21},{2,22},{3,23},{4,16},{5,17},{6,18},{7,19},{8,12},{9,... | collective-permute-start | bytes 393224 | tf_op jit(solution)/shard_map/ppermute | solution.py:544
  139.1 6.2 %collective-permute-start.22 = (bf16[16,4096]{1,0:T(8,128)(2,1)S(1)}, bf16[16,4096]{1,0:T(8,128)(2,1)S(1)}, u32[]{:S(2)}, u32[]{:S(2)}) collective-permute-start(bf16[16,4096]{1,0:T(8,128)(2,1)S(1)} %get-tuple-element.123), channel_id=1, source_target_pairs={{0,96},{1,97},{2,98},{3,99},{4,100},{5,101},{6,102},{7,103},{8,40}... | collective-permute-start | bytes 393224 | tf_op jit(solution)/shard_map/ppermute | solution.py:544
  139.1 8.3 %collective-permute-start.21 = (bf16[16,4096]{1,0:T(8,128)(2,1)S(1)}, bf16[16,4096]{1,0:T(8,128)(2,1)S(1)}, u32[]{:S(2)}, u32[]{:S(2)}) collective-permute-start(bf16[16,4096]{1,0:T(8,128)(2,1)S(1)} %get-tuple-element.124), channel_id=1, source_target_pairs={{0,116},{1,117},{2,118},{3,119},{4,112},{5,113},{6,114},{7,115},{8... | collective-permute-start | bytes 393224 | tf_op jit(solution)/shard_map/ppermute | solution.py:544
  147.5 1.3 collective-permute-start.24

commit v2 on v1

--- a/solution.py
+++ b/solution.py
@@ -351,15 +351,16 @@
         copy.wait()
 
 
-def project_kernel(level, half, left_ref, left2_ref, own_ref, other_ref, out_ref):
+def project_kernel(level, half, left_ref, cols_ref, *refs):
+    start_ref, out_ref = refs if len(refs) == 2 else (None, refs[0])
     run = 512 >> level
     step = min(run, 256)
     for at in range(0, 512, step):
         rows = slice(at, at + step)
         source = (at // run) * 2 * run + half * run + at % run
-        source = slice(source, source + step)
-        term = dot(left_ref[source, :], own_ref[...], (1, 0))
-        term += dot(left2_ref[source, :], other_ref[...], (1, 0))
+        term = dot(left_ref[source : source + step, :], cols_ref[...], (1, 0))
+        if start_ref is not None:
+            term += start_ref[rows, :]
         out_ref[rows, :] = term.astype(out_ref.dtype)
 
 
@@ -469,7 +470,7 @@
             pltpu.VMEM((QUERIES, ROWS), jnp.float32),
             pltpu.SemaphoreType.DMA((6,)),
         ],
-        compiler_params=pltpu.CompilerParams(vmem_limit_bytes=28 * MIB),
+        compiler_params=pltpu.CompilerParams(vmem_limit_bytes=20 * MIB),
         cost_estimate=pl.CostEstimate(
             flops=10**10, bytes_accessed=16 * MIB, transcendentals=0
         ),
@@ -493,59 +494,71 @@
     own_cols, other_cols = columns[:3], columns[3:]
     left2 = lax.ppermute(swap_left, AXES, swap)
 
-    def project(part, half):
+    def project(part, half, side, start, dtype):
         return vmem_call(
             functools.partial(project_kernel, part, half),
-            shape(512, WIDTHS[part]),
-            operands=(left, left2, own_cols[part], other_cols[part]),
-            flops=2 * 512 * 1024 * WIDTHS[part],
+            shape(512, WIDTHS[part], dtype),
+            operands=(side, *start),
+            flops=2 * 512 * 512 * WIDTHS[part],
             nbytes=5 * MIB,
         )
 
+    own_terms = [project(part, 1, left, (own_cols[part],), jnp.float32) for part in range(3)]
     sends = []
     for part in range(3):
-        sends.append(project(part, 1))
-        left, _ = lax.optimization_barrier((left, sends[-1]))
-    keeps = [project(part, 0) for part in range(3)]
+        sends.append(project(part, 1, left2, (other_cols[part], own_terms[part]), jnp.bfloat16))
+        left2, _ = lax.optimization_barrier((left2, sends[-1]))
+    keeps = []
+    for part in range(3):
+        term = project(part, 0, left2, (other_cols[part],), jnp.float32)
+        keeps.append(project(part, 0, left, (own_cols[part], term), jnp.bfloat16))
+    coming = [
+        lax.ppermute(sends[part], AXES, flip_pairs([ORDERS[c][part][0] for c in range(2)]))
+        for part in range(3)
+    ]
+    keeps, coming[0] = lax.optimization_barrier((keeps, coming[0]))
     for level in range(3):
-        coming = [
-            lax.ppermute(
-                sends[part], AXES, flip_pairs([ORDERS[c][part][level] for c in range(2)])
-            )
-            for part in range(3)
-        ]
-        coming, keeps = lax.optimization_barrier((coming, keeps))
-        halves = []
         for part in range(3):
             lead = 2 if (level, part) == (0, 1) else 1
             width = WIDTHS[part]
-            halves.append(
+            came = coming[part]
+            if True and part > 0:
+                came, _ = lax.optimization_barrier((came, sends[part - 1]))
+            halves = [
                 [
-                    [a.reshape(lead, 2, -1, width)[:, bit].reshape(-1, width).astype(jnp.float32)
-                     for a in (keeps[part], coming[part])]
-                    for bit in range(2)
+                    a.reshape(lead, 2, -1, width)[:, bit].reshape(-1, width).astype(jnp.float32)
+                    for a in (keeps[part], came)
                 ]
-            )
-        sends = [(pair[1][0] + pair[1][1]).astype(jnp.bfloat16) for pair in halves]
-        keeps = [pair[0][0] + pair[0][1] for pair in halves]
+                for bit in range(2)
+            ]
+            sends[part] = (halves[1][0] + halves[1][1]).astype(jnp.bfloat16)
+            keeps[part] = halves[0][0] + halves[0][1]
+            if level < 2:
+                coming[part] = lax.ppermute(
+                    sends[part],
+                    AXES,
+                    flip_pairs([ORDERS[c][part][level + 1] for c in range(2)]),
+                )
     keep, send = jnp.concatenate(keeps, axis=1), jnp.concatenate(sends, axis=1)
-    for level in range(3, 4):
-        came = lax.ppermute(send, AXES, flip_pairs([ORDERS[c][0][level] for c in range(2)]))
-        total = keep + came.astype(jnp.float32)
-        rows = total.shape[0] // 2
-        keep, send = total[:rows], total[rows:].astype(jnp.bfloat16)
-    blocks = total.reshape(-1, 16, HALF)
-    coming = []
-    for block in range(blocks.shape[0] - 1, 0, -1):
-        names = [
-            [ORDERS[c][0][5 - bit] for bit in range(2) if (block >> bit) & 1]
-            for c in range(2)
-        ]
-        coming.append(lax.ppermute(blocks[block].astype(jnp.bfloat16), AXES, flip_pairs(names)))
+    blocks = (
+        (send[32:], (3, 4)),
+        (send[:32], (3,)),
+        (keep[32:].astype(jnp.bfloat16), (4,)),
+    )
+    coming = [
+        lax.ppermute(
+            block, AXES, flip_pairs([[ORDERS[c][0][level] for level in levels] for c in range(2)])
+        )
+        for block, levels in blocks
+    ]
     coming = lax.optimization_barrier(coming)
-    total = blocks[0]
+    total = keep[:32]
     for came in coming:
         total = total + came.astype(jnp.float32)
+    came = lax.ppermute(
+        total[16:].astype(jnp.bfloat16), AXES, flip_pairs([ORDERS[c][0][5] for c in range(2)])
+    )
+    total = total[:16] + came.astype(jnp.float32)
     both = total.reshape(2, 8, HALF)
     mine = lax.dynamic_index_in_dim(both, core, 0, keepdims=False)
     theirs = lax.dynamic_index_in_dim(both, 1 - core, 0, keepdims=False).astype(jnp.bfloat16)

time: 152 us -> 146 us (0.961); the launches traced: 150 us -> 145 us
  waiting for transfers between devices: 59.4 us -> 43.6 us
  starting transfers between devices: 47.6 us -> 60.9 us
  local copies, waits for them, and re-layouts: 12.1 us -> 10.3 us
    ppermute x13, waiting for transfers between devices: 34.9 us -> 18.7 us  [the longest x6 6.97 us: body(): lax.ppermute(sends[part], AXES, flip_pairs([ORDERS[c][part][level + 1] fo...]
    ppermute x13, starting transfers between devices: 28.8 us -> 42.2 us  [the longest x6 22.1 us: body(): lax.ppermute(sends[part], AXES, flip_pairs([ORDERS[c][part][level + 1] fo...]
    unnamed x12 -> x10, local copies, waits for them, and re-layouts: 1.97 us -> 0.02 us
    pallas_call x7 -> x13, Pallas kernels: 14.5 us -> 15.7 us  [vmem_call(): pl.pallas_call(body, out_shape=out_shape, in_specs=specs, out_specs=out_s...]
  transfers between devices with their start and end apart: 26 -> 26, of which waited for: 13 -> 12; matrix products, arithmetic and copies ran while one was open for 7% -> 8% of each run, Pallas kernels for 9% -> 11%
where the time goes in v2:
time: 146 us; the launch traced here: 145 us
  starting transfers between devices  60.9 us (42%)
  waiting for transfers between devices  43.6 us (30%)
  Pallas kernels  26.9 us (18%)
  local copies, waits for them, and re-layouts  10.3 us (7%)
  other arithmetic  2.65 us (2%)
    ppermute x6, starting transfers between devices, body(): lax.ppermute(sends[part], AXES, flip_pairs([ORDERS[c][part][level + 1] fo...  22.1 us
    pallas_call x13, Pallas kernels, vmem_call(): pl.pallas_call(body, out_shape=out_shape, in_specs=specs, out_specs=out_s...  15.7 us
    ppermute x3, starting transfers between devices, body(): lax.ppermute(sends[part], AXES, flip_pairs([ORDERS[c][part][0] for c in r...  13.1 us
    all_to_all x1, waiting for transfers between devices, body(): lax.all_to_all(sent.reshape(GROUPS, ROWS // GROUPS, SENT), 'dp', 0, 0, ti...  11.1 us
    dynamic_slice x3, local copies, waits for them, and re-layouts, body(): lax.dynamic_slice(tokens, (0, (1 - core) * HALF + at), (ROWS, width))  10.1 us
    all_to_all x1, starting transfers between devices, body(): lax.all_to_all(sent.reshape(GROUPS, ROWS // GROUPS, SENT), 'dp', 0, 0, ti...  7.98 us
    ppermute x6, waiting for transfers between devices, body(): lax.ppermute(sends[part], AXES, flip_pairs([ORDERS[c][part][level + 1] fo...  6.97 us
    ppermute x3, waiting for transfers between devices, body(): lax.ppermute(block, AXES, flip_pairs([[ORDERS[c][0][level] for level in l...  6.49 us
  transfers between devices with their start and end apart: 26, of which 12 were waited for; matrix products, arithmetic and copies ran while one was open for 8% of the time, Pallas kernels for 11%

profile of v2, /device:TPU:0, one launch (start us, length us, event | category | flops | bytes accessed | tf_op | source)
XLA Modules:
  0.0 145.5 jit_solution(12768094600405164005)
XLA Ops:
  0.6 4.1 %shard_map.68 = bf16[512,1408]{1,0:T(8,128)(2,1)} custom-call(s32[1,512]{1,0:T(1,128)} %dest_ref.1, bf16[1,512,1280]{2,1,0:T(8,128)(2,1)} %rows_ref.1), custom_call_target="tpu_custom_call" | custom-call | flops 1000000000 | bytes 3145728 | tf_op jit(solution)/shard_map/pallas_call | solution.py:390
  4.8 8.0 %all-to-all-start = ((bf16[16,32,1408]{2,1,0:T(8,128)(2,1)}), bf16[16,32,1408]{2,1,0:T(8,128)(2,1)S(1)}, u32[]{:S(2)}, u32[]{:S(2)}) async-start(bf16[16,32,1408]{2,1,0:T(8,128)(2,1)} %bitcast.92), calls=%async_computation | async-start | bytes 2883584 | tf_op jit(solution)/shard_map/all_to_all | solution.py:405
  12.8 3.3 %dynamic-slice_bitcast_fusion.4 = (bf16[512,1152]{1,0:T(8,128)(2,1)}, bf16[512,1152]{1,0:T(8,128)(2,1)}) fusion(bf16[1,512,8192]{2,1,0:T(8,128)(2,1)} %param.8, s32[]{:T(128)S(6)} %select_n.92, s32[]{:T(128)S(6)} %select_n.89), kind=kLoop, calls=%fused_computation.10 | loop fusion | bytes 4718600 | tf_op jit(solution)/shard_map/dynamic_slice | solution.py:385
  16.4 3.2 %dynamic-slice_bitcast_fusion = (bf16[512,1536]{1,0:T(8,128)(2,1)}, bf16[512,1536]{1,0:T(8,128)(2,1)S(1)}) fusion(bf16[1,512,8192]{2,1,0:T(8,128)(2,1)} %param.8, s32[]{:T(128)S(6)} %select_n.90, s32[]{:T(128)S(6)} %select_n.87), kind=kLoop, calls=%fused_computation.2 | loop fusion | bytes 6291464 | tf_op jit(solution)/shard_map/dynamic_slice | solution.py:385
  19.8 3.6 %dynamic-slice_bitcast_fusion.2 = (bf16[512,1408]{1,0:T(8,128)(2,1)}, bf16[512,1408]{1,0:T(8,128)(2,1)}) fusion(bf16[1,512,8192]{2,1,0:T(8,128)(2,1)} %param.8, s32[]{:T(128)S(6)} %select_n.91, s32[]{:T(128)S(6)} %select_n.88), kind=kLoop, calls=%fused_computation.6 | loop fusion | bytes 5767176 | tf_op jit(solution)/shard_map/dynamic_slice | solution.py:385
  23.5 0.4 collective-permute-start.4
  23.9 11.1 %all-to-all-done = bf16[16,32,1408]{2,1,0:T(8,128)(2,1)S(1)} async-done(((bf16[16,32,1408]{2,1,0:T(8,128)(2,1)}), bf16[16,32,1408]{2,1,0:T(8,128)(2,1)S(1)}, u32[]{:S(2)}, u32[]{:S(2)}) %all-to-all-start) | async-done | bytes 1441824 | tf_op jit(solution)/shard_map/all_to_all | solution.py:405
  35.0 1.2 shard_map.69
  36.2 1.5 %collective-permute-start = (bf16[512,256]{1,0:T(8,128)(2,1)}, bf16[512,256]{1,0:T(8,128)(2,1)}, u32[]{:S(2)}, u32[]{:S(2)}) collective-permute-start(bf16[512,256]{1,0:T(8,128)(2,1)} %get-tuple-element.42.kv_ref), channel_id=1, source_target_pairs={{0,1},{1,0},{2,3},{3,2},{4,5},{5,4},{6,7},{7,6},{8,11},{9,10},{10,... | collective-permute-start | bytes 786440 | tf_op jit(solution)/shard_map/ppermute | solution.py:420
  37.7 1.0 collective-permute-start.7
  38.7 2.1 %collective-permute-start.6 = (bf16[512,256]{1,0:T(8,128)(2,1)}, bf16[512,256]{1,0:T(8,128)(2,1)}, u32[]{:S(2)}, u32[]{:S(2)}) collective-permute-start(bf16[512,256]{1,0:T(8,128)(2,1)} %get-tuple-element.42.kv_ref), channel_id=1, source_target_pairs={{0,3},{1,2},{2,1},{3,0},{4,7},{5,6},{6,5},{7,4},{8,12},{9,13},{10,... | collective-permute-start | bytes 786440 | tf_op jit(solution)/shard_map/ppermute | solution.py:421
  40.8 3.9 %collective-permute-done.near0_ref = bf16[512,256]{1,0:T(8,128)(2,1)} collective-permute-done((bf16[512,256]{1,0:T(8,128)(2,1)}, bf16[512,256]{1,0:T(8,128)(2,1)}, u32[]{:S(2)}, u32[]{:S(2)}) %collective-permute-start) | collective-permute-done | bytes 262176 | tf_op jit(solution)/shard_map/ppermute | solution.py:420
  44.7 2.6 %collective-permute-start.1 = (bf16[512,256]{1,0:T(8,128)(2,1)}, bf16[512,256]{1,0:T(8,128)(2,1)}, u32[]{:S(2)}, u32[]{:S(2)}) collective-permute-start(bf16[512,256]{1,0:T(8,128)(2,1)} %collective-permute-done.near0_ref), channel_id=1, source_target_pairs={{0,3},{1,2},{2,1},{3,0},{4,7},{5,6},{6,5},{7,4},{8,9},{9,8},{10,11... | collective-permute-start | bytes 786440 | tf_op jit(solution)/shard_map/ppermute | solution.py:423
  47.8 1.0 collective-permute-start.8
  48.8 5.7 %collective-permute-done.1.far0_ref = bf16[512,256]{1,0:T(8,128)(2,1)} collective-permute-done((bf16[512,256]{1,0:T(8,128)(2,1)}, bf16[512,256]{1,0:T(8,128)(2,1)}, u32[]{:S(2)}, u32[]{:S(2)}) %collective-permute-start.1) | collective-permute-done | bytes 262176 | tf_op jit(solution)/shard_map/ppermute | solution.py:423
  54.4 1.0 collective-permute-start.2
  55.5 4.0 %shard_map.70 = (bf16[512,1024]{1,0:T(8,128)(2,1)S(1)}, f32[4096,128]{1,0:T(8,128)S(1)}, f32[4096,256]{1,0:T(8,128)S(1)}) custom-call(s32[2]{0:T(128)S(1)} %pad_add_fusion.slot_ref, s32[1,4]{1,0:T(1,128)S(1)} %copy-done.2, bf16[512,512]{1,0:T(8,128)(2,1)S(1)} %get-tuple-element.41.inverse_ref, bf16[512,1408]{1,0:T(8,128)(2,1)S(1)} %bitcast.83, ...), custom_call_target="tpu_custom_call" | custom-call | flops 2000000000 | bytes 4194304 | tf_op jit(solution)/shard_map/pallas_call | solution.py:110
  59.6 1.4 collective-permute-done.2.last_ref
  61.0 5.8 %shard_map.71 = (bf16[512,1024]{1,0:T(8,128)(2,1)}, bf16[1024,512]{1,0:T(8,128)(2,1)S(1)}, bf16[1024,512]{1,0:T(8,128)(2,1)S(1)}, bf16[512,1536]{1,0:T(8,128)(2,...) custom-call(s32[2]{0:T(128)S(1)} %pad_add_fusion.slot_ref, ...), custom_call_target="tpu_custom_call" | custom-call | flops 10000000000 | bytes 16777216 | tf_op jit(solution)/shard_map/pallas_call | solution.py:455
  66.9 1.0 shard_map.72.refs_0_
  67.9 1.7 %collective-permute-done.10.left_ref = bf16[1024,512]{1,0:T(8,128)(2,1)S(1)} collective-permute-done((bf16[1024,512]{1,0:T(8,128)(2,1)S(1)}, bf16[1024,512]{1,0:T(8,128)(2,1)S(1)}, u32[]{:S(2)}, u32[]{:S(2)}) %collective-permute-start.10) | collective-permute-done | bytes 1048608 | tf_op jit(solution)/shard_map/ppermute | solution.py:495
  69.6 1.0 shard_map.73
  70.6 4.0 %collective-permute-start.11 = (bf16[512,1536]{1,0:T(8,128)(2,1)S(1)}, bf16[512,1536]{1,0:T(8,128)(2,1)S(1)}, u32[]{:S(2)}, u32[]{:S(2)}) collective-permute-start(bf16[512,1536]{1,0:T(8,128)(2,1)S(1)} %shard_map.73), channel_id=1, source_target_pairs={{0,1},{1,0},{2,3},{3,2},{4,5},{5,4},{6,7},{7,6},{8,11},{9,10},{10,... | collective-permute-start | bytes 4718600 | tf_op jit(solution)/shard_map/ppermute | solution.py:516
  74.6 1.0 shard_map.74.refs_0_
  75.6 1.0 shard_map.75
  76.7 0.9 shard_map.76.refs_0_
  77.6 0.9 shard_map.77
  78.5 9.0 %collective-permute-start.17 = (bf16[512,1152]{1,0:T(8,128)(2,1)S(1)}, bf16[512,1152]{1,0:T(8,128)(2,1)S(1)}, u32[]{:S(2)}, u32[]{:S(2)}) collective-permute-start(bf16[512,1152]{1,0:T(8,128)(2,1)S(1)} %shard_map.77), channel_id=1, source_target_pairs={{0,4},{1,5},{2,6},{3,7},{4,0},{5,1},{6,2},{7,3},{8,28},{9,29},{10,... | collective-permute-start | bytes 3538952 | tf_op jit(solution)/shard_map/ppermute | solution.py:516
  87.5 0.9 shard_map.82.refs_0_
  88.4 1.0 shard_map.80.refs_0_
  89.4 1.0 shard_map.81
  90.5 1.0 shard_map.78.refs_0_
  91.4 1.0 shard_map.79
  92.5 0.9 shard_map.83
  93.8 2.1 %collective-permute-start.12 = (bf16[256,1536]{1,0:T(8,128)(2,1)S(1)}, bf16[256,1536]{1,0:T(8,128)(2,1)S(1)}, u32[]{:S(2)}, u32[]{:S(2)}) collective-permute-start(bf16[256,1536]{1,0:T(8,128)(2,1)S(1)} %get-tuple-element.87), channel_id=1, source_target_pairs={{0,32},{1,33},{2,34},{3,35},{4,36},{5,37},{6,38},{7,39},{8,104},{9... | collective-permute-start | bytes 2359304 | tf_op jit(solution)/shard_map/ppermute | solution.py:537
  96.2 8.6 %collective-permute-start.15 = (bf16[256,1408]{1,0:T(8,128)(2,1)S(1)}, bf16[256,1408]{1,0:T(8,128)(2,1)S(1)}, u32[]{:S(2)}, u32[]{:S(2)}) collective-permute-start(bf16[256,1408]{1,0:T(8,128)(2,1)S(1)} %bitcast.96), channel_id=1, source_target_pairs={{0,4},{1,5},{2,6},{3,7},{4,0},{5,1},{6,2},{7,3},{8,28},{9,29},{10,... | collective-permute-start | bytes 2162696 | tf_op jit(solution)/shard_map/ppermute | solution.py:537
  105.0 2.1 %collective-permute-start.18 = (bf16[256,1152]{1,0:T(8,128)(2,1)S(1)}, bf16[256,1152]{1,0:T(8,128)(2,1)S(1)}, u32[]{:S(2)}, u32[]{:S(2)}) collective-permute-start(bf16[256,1152]{1,0:T(8,128)(2,1)S(1)} %get-tuple-element.92), channel_id=1, source_target_pairs={{0,1},{1,0},{2,3},{3,2},{4,5},{5,4},{6,7},{7,6},{8,11},{9,10},{10,... | collective-permute-start | bytes 1769480 | tf_op jit(solution)/shard_map/ppermute | solution.py:537
  107.3 9.0 %collective-permute-start.13 = (bf16[128,1536]{1,0:T(8,128)(2,1)S(1)}, bf16[128,1536]{1,0:T(8,128)(2,1)S(1)}, u32[]{:S(2)}, u32[]{:S(2)}) collective-permute-start(bf16[128,1536]{1,0:T(8,128)(2,1)S(1)} %get-tuple-element.91), channel_id=1, source_target_pairs={{0,4},{1,5},{2,6},{3,7},{4,0},{5,1},{6,2},{7,3},{8,28},{9,29},{10,... | collective-permute-start | bytes 1179656 | tf_op jit(solution)/shard_map/ppermute | solution.py:537
  117.0 5.2 %collective-permute-done.13 = bf16[128,1536]{1,0:T(8,128)(2,1)S(1)} collective-permute-done((bf16[128,1536]{1,0:T(8,128)(2,1)S(1)}, bf16[128,1536]{1,0:T(8,128)(2,1)S(1)}, u32[]{:S(2)}, u32[]{:S(2)}) %collective-permute-start.13) | collective-permute-done | bytes 393248 | tf_op jit(solution)/shard_map/ppermute | solution.py:537
  122.2 1.8 %collective-permute-done.16 = bf16[128,1408]{1,0:T(8,128)(2,1)S(1)} collective-permute-done((bf16[128,1408]{1,0:T(8,128)(2,1)S(1)}, bf16[128,1408]{1,0:T(8,128)(2,1)S(1)}, u32[]{:S(2)}, u32[]{:S(2)}) %collective-permute-start.16) | collective-permute-done | bytes 360480 | tf_op jit(solution)/shard_map/ppermute | solution.py:537
  124.6 5.9 %collective-permute-start.22 = (bf16[32,4096]{1,0:T(8,128)(2,1)S(1)}, bf16[32,4096]{1,0:T(8,128)(2,1)S(1)}, u32[]{:S(2)}, u32[]{:S(2)}) collective-permute-start(bf16[32,4096]{1,0:T(8,128)(2,1)S(1)} %slice.324), channel_id=1, source_target_pairs={{0,96},{1,97},{2,98},{3,99},{4,100},{5,101},{6,102},{7,103},{8,40}... | collective-permute-start | bytes 786440 | tf_op jit(solution)/shard_map/ppermute | solution.py:549
  130.4 1.5 %collective-permute-done.21 = bf16[32,4096]{1,0:T(8,128)(2,1)S(1)} collective-permute-done((bf16[32,4096]{1,0:T(8,128)(2,1)S(1)}, bf16[32,4096]{1,0:T(8,128)(2,1)S(1)}, u32[]{:S(2)}, u32[]{:S(2)}) %collective-permute-start.21) | collective-permute-done | bytes 262176 | tf_op jit(solution)/shard_map/ppermute | solution.py:549
  131.9 2.3 %collective-permute-done.20 = bf16[32,4096]{1,0:T(8,128)(2,1)S(1)} collective-permute-done((bf16[32,4096]{1,0:T(8,128)(2,1)S(1)}, bf16[32,4096]{1,0:T(8,128)(2,1)S(1)}, u32[]{:S(2)}, u32[]{:S(2)}) %collective-permute-start.20) | collective-permute-done | bytes 262176 | tf_op jit(solution)/shard_map/ppermute | solution.py:549
  134.2 2.7 %collective-permute-done.22 = bf16[32,4096]{1,0:T(8,128)(2,1)S(1)} collective-permute-done((bf16[32,4096]{1,0:T(8,128)(2,1)S(1)}, bf16[32,4096]{1,0:T(8,128)(2,1)S(1)}, u32[]{:S(2)}, u32[]{:S(2)}) %collective-permute-start.22) | collective-permute-done | bytes 262176 | tf_op jit(solution)/shard_map/ppermute | solution.py:549
  137.1 1.0 collective-permute-start.23
  138.1 5.3 %collective-permute-done.23 = bf16[16,4096]{1,0:T(8,128)(2,1)S(1)} collective-permute-done((bf16[16,4096]{1,0:T(8,128)(2,1)S(1)}, bf16[16,4096]{1,0:T(8,128)(2,1)S(1)}, u32[]{:S(2)}, u32[]{:S(2)}) %collective-permute-start.23) | collective-permute-done | bytes 131104 | tf_op jit(solution)/shard_map/ppermute | solution.py:558
  143.5 1.2 collective-permute-done.24
  144.7 0.7 maximum_select_fusion
  (56 shorter events, 3.7 us)
Async XLA Ops:
  4.8 30.2 %all-to-all-start = ((bf16[16,32,1408]{2,1,0:T(8,128)(2,1)}), bf16[16,32,1408]{2,1,0:T(8,128)(2,1)S(1)}, u32[]{:S(2)}, u32[]{:S(2)}) async-start(bf16[16,32,1408]{2,1,0:T(8,128)(2,1)} %bitcast.92), calls=%async_computation | async-start | bytes 2883584 | tf_op jit(solution)/shard_map/all_to_all | solution.py:405
  16.1 22.6 %collective-permute-start.5 = (bf16[512,1152]{1,0:T(8,128)(2,1)}, bf16[512,1152]{1,0:T(8,128)(2,1)}, u32[]{:S(2)}, u32[]{:S(2)}) collective-permute-start(bf16[512,1152]{1,0:T(8,128)(2,1)} %get-tuple-element.80), channel_id=1, source_target_pairs={{0,8},{1,9},{2,10},{3,11},{4,12},{5,13},{6,14},{7,15},{8,0},{9,1},... | collective-permute-start | bytes 3538952 | tf_op jit(solution)/shard_map/ppermute | solution.py:384
  19.7 39.9 %collective-permute-start.3 = (bf16[512,1536]{1,0:T(8,128)(2,1)}, bf16[512,1536]{1,0:T(8,128)(2,1)}, u32[]{:S(2)}, u32[]{:S(2)}) collective-permute-start(bf16[512,1536]{1,0:T(8,128)(2,1)} %get-tuple-element.84), channel_id=1, source_target_pairs={{0,8},{1,9},{2,10},{3,11},{4,12},{5,13},{6,14},{7,15},{8,0},{9,1},... | collective-permute-start | bytes 4718600 | tf_op jit(solution)/shard_map/ppermute | solution.py:384
  23.4 23.8 %copy-start.3 = (s32[2,64,3]{1,0,2:T(2,128)S(1)}, s32[2,64,3]{1,0,2:T(2,128)}, u32[]{:S(2)}) copy-start(s32[2,64,3]{1,0,2:T(2,128)} %constant.121) | copy-start | bytes 4612
  23.4 23.9 %copy-start.4 = (s32[2,64,3]{1,0,2:T(2,128)S(1)}, s32[2,64,3]{1,0,2:T(2,128)}, u32[]{:S(2)}) copy-start(s32[2,64,3]{1,0,2:T(2,128)} %constant.116.clone) | copy-start | bytes 4612
  23.4 32.1 %copy-start.2 = (s32[1,4]{1,0:T(1,128)S(1)}, s32[1,4]{1,0:T(1,128)}, u32[]{:S(2)}) copy-start(s32[1,4]{1,0:T(1,128)} %lengths_ref.3) | copy-start | bytes 52
  23.5 36.1 %collective-permute-start.4 = (bf16[512,1408]{1,0:T(8,128)(2,1)}, bf16[512,1408]{1,0:T(8,128)(2,1)}, u32[]{:S(2)}, u32[]{:S(2)}) collective-permute-start(bf16[512,1408]{1,0:T(8,128)(2,1)} %get-tuple-element.82), channel_id=1, source_target_pairs={{0,8},{1,9},{2,10},{3,11},{4,12},{5,13},{6,14},{7,15},{8,0},{9,1},... | collective-permute-start | bytes 4325384 | tf_op jit(solution)/shard_map/ppermute | solution.py:384
  36.2 8.5 %collective-permute-start = (bf16[512,256]{1,0:T(8,128)(2,1)}, bf16[512,256]{1,0:T(8,128)(2,1)}, u32[]{:S(2)}, u32[]{:S(2)}) collective-permute-start(bf16[512,256]{1,0:T(8,128)(2,1)} %get-tuple-element.42.kv_ref), channel_id=1, source_target_pairs={{0,1},{1,0},{2,3},{3,2},{4,5},{5,4},{6,7},{7,6},{8,11},{9,10},{10,... | collective-permute-start | bytes 786440 | tf_op jit(solution)/shard_map/ppermute | solution.py:420
  37.7 9.7 %collective-permute-start.7 = (bf16[512,256]{1,0:T(8,128)(2,1)}, bf16[512,256]{1,0:T(8,128)(2,1)}, u32[]{:S(2)}, u32[]{:S(2)}) collective-permute-start(bf16[512,256]{1,0:T(8,128)(2,1)} %get-tuple-element.42.kv_ref), channel_id=1, source_target_pairs={{0,4},{1,5},{2,6},{3,7},{4,0},{5,1},{6,2},{7,3},{8,9},{9,8},{10,11... | collective-permute-start | bytes 786440 | tf_op jit(solution)/shard_map/ppermute | solution.py:422
  38.7 9.1 %collective-permute-start.6 = (bf16[512,256]{1,0:T(8,128)(2,1)}, bf16[512,256]{1,0:T(8,128)(2,1)}, u32[]{:S(2)}, u32[]{:S(2)}) collective-permute-start(bf16[512,256]{1,0:T(8,128)(2,1)} %get-tuple-element.42.kv_ref), channel_id=1, source_target_pairs={{0,3},{1,2},{2,1},{3,0},{4,7},{5,6},{6,5},{7,4},{8,12},{9,13},{10,... | collective-permute-start | bytes 786440 | tf_op jit(solution)/shard_map/ppermute | solution.py:421
  44.7 9.8 %collective-permute-start.1 = (bf16[512,256]{1,0:T(8,128)(2,1)}, bf16[512,256]{1,0:T(8,128)(2,1)}, u32[]{:S(2)}, u32[]{:S(2)}) collective-permute-start(bf16[512,256]{1,0:T(8,128)(2,1)} %collective-permute-done.near0_ref), channel_id=1, source_target_pairs={{0,3},{1,2},{2,1},{3,0},{4,7},{5,6},{6,5},{7,4},{8,9},{9,8},{10,11... | collective-permute-start | bytes 786440 | tf_op jit(solution)/shard_map/ppermute | solution.py:423
  47.4 13.6 %collective-permute-start.9 = (bf16[512,256]{1,0:T(8,128)(2,1)}, bf16[512,256]{1,0:T(8,128)(2,1)S(1)}, u32[]{:S(2)}, u32[]{:S(2)}) collective-permute-start(bf16[512,256]{1,0:T(8,128)(2,1)} %collective-permute-done.7.near2_ref), channel_id=1, source_target_pairs={{0,1},{1,0},{2,3},{3,2},{4,5},{5,4},{6,7},{7,6},{8,12},{9,13},{10,... | collective-permute-start | bytes 786440 | tf_op jit(solution)/shard_map/ppermute | solution.py:425
  47.8 13.3 %collective-permute-start.8 = (bf16[512,256]{1,0:T(8,128)(2,1)}, bf16[512,256]{1,0:T(8,128)(2,1)S(1)}, u32[]{:S(2)}, u32[]{:S(2)}) collective-permute-start(bf16[512,256]{1,0:T(8,128)(2,1)} %collective-permute-done.6.near1_ref), channel_id=1, source_target_pairs={{0,4},{1,5},{2,6},{3,7},{4,0},{5,1},{6,2},{7,3},{8,11},{9,10},{10,... | collective-permute-start | bytes 786440 | tf_op jit(solution)/shard_map/ppermute | solution.py:424
  54.4 6.6 %collective-permute-start.2 = (bf16[512,256]{1,0:T(8,128)(2,1)}, bf16[512,256]{1,0:T(8,128)(2,1)S(1)}, u32[]{:S(2)}, u32[]{:S(2)}) collective-permute-start(bf16[512,256]{1,0:T(8,128)(2,1)} %collective-permute-done.1.far0_ref), channel_id=1, source_target_pairs={{0,4},{1,5},{2,6},{3,7},{4,0},{5,1},{6,2},{7,3},{8,12},{9,13},{10,... | collective-permute-start | bytes 786440 | tf_op jit(solution)/shard_map/ppermute | solution.py:426
  55.5 5.5 %copy-start = (bf16[512,1408]{1,0:T(8,128)(2,1)S(1)}, bf16[512,1408]{1,0:T(8,128)(2,1)}, u32[]{:S(2)}) copy-start(bf16[512,1408]{1,0:T(8,128)(2,1)} %get-tuple-element.50.refs_1_) | copy-start | bytes 4325380
  55.5 5.5 %copy-start.1 = (bf16[512,1152]{1,0:T(8,128)(2,1)S(1)}, bf16[512,1152]{1,0:T(8,128)(2,1)}, u32[]{:S(2)}) copy-start(bf16[512,1152]{1,0:T(8,128)(2,1)} %get-tuple-element.51.refs_2_) | copy-start | bytes 3538948
  66.8 2.7 %collective-permute-start.10 = (bf16[1024,512]{1,0:T(8,128)(2,1)S(1)}, bf16[1024,512]{1,0:T(8,128)(2,1)S(1)}, u32[]{:S(2)}, u32[]{:S(2)}) collective-permute-start(bf16[1024,512]{1,0:T(8,128)(2,1)S(1)} %get-tuple-element.58), channel_id=1, source_target_pairs={{0,8},{1,9},{2,10},{3,11},{4,12},{5,13},{6,14},{7,15},{8,0},{9,1},... | collective-permute-start | bytes 3145736 | tf_op jit(solution)/shard_map/ppermute | solution.py:495
  70.6 22.8 %collective-permute-start.11 = (bf16[512,1536]{1,0:T(8,128)(2,1)S(1)}, bf16[512,1536]{1,0:T(8,128)(2,1)S(1)}, u32[]{:S(2)}, u32[]{:S(2)}) collective-permute-start(bf16[512,1536]{1,0:T(8,128)(2,1)S(1)} %shard_map.73), channel_id=1, source_target_pairs={{0,1},{1,0},{2,3},{3,2},{4,5},{5,4},{6,7},{7,6},{8,11},{9,10},{10,... | collective-permute-start | bytes 4718600 | tf_op jit(solution)/shard_map/ppermute | solution.py:516
  76.6 19.3 %collective-permute-start.14 = (bf16[512,1408]{1,0:T(8,128)(2,1)S(1)}, bf16[512,1408]{1,0:T(8,128)(2,1)S(1)}, u32[]{:S(2)}, u32[]{:S(2)}) collective-permute-start(bf16[512,1408]{1,0:T(8,128)(2,1)S(1)} %shard_map.75), channel_id=1, source_target_pairs={{0,32},{1,33},{2,34},{3,35},{4,36},{5,37},{6,38},{7,39},{8,104},{9... | collective-permute-start | bytes 4325384 | tf_op jit(solution)/shard_map/ppermute | solution.py:516
  78.5 26.3 %collective-permute-start.17 = (bf16[512,1152]{1,0:T(8,128)(2,1)S(1)}, bf16[512,1152]{1,0:T(8,128)(2,1)S(1)}, u32[]{:S(2)}, u32[]{:S(2)}) collective-permute-start(bf16[512,1152]{1,0:T(8,128)(2,1)S(1)} %shard_map.77), channel_id=1, source_target_pairs={{0,4},{1,5},{2,6},{3,7},{4,0},{5,1},{6,2},{7,3},{8,28},{9,29},{10,... | collective-permute-start | bytes 3538952 | tf_op jit(solution)/shard_map/ppermute | solution.py:516
  93.8 13.3 %collective-permute-start.12 = (bf16[256,1536]{1,0:T(8,128)(2,1)S(1)}, bf16[256,1536]{1,0:T(8,128)(2,1)S(1)}, u32[]{:S(2)}, u32[]{:S(2)}) collective-permute-start(bf16[256,1536]{1,0:T(8,128)(2,1)S(1)} %get-tuple-element.87), channel_id=1, source_target_pairs={{0,32},{1,33},{2,34},{3,35},{4,36},{5,37},{6,38},{7,39},{8,104},{9... | collective-permute-start | bytes 2359304 | tf_op jit(solution)/shard_map/ppermute | solution.py:537
  96.2 20.2 %collective-permute-start.15 = (bf16[256,1408]{1,0:T(8,128)(2,1)S(1)}, bf16[256,1408]{1,0:T(8,128)(2,1)S(1)}, u32[]{:S(2)}, u32[]{:S(2)}) collective-permute-start(bf16[256,1408]{1,0:T(8,128)(2,1)S(1)} %bitcast.96), channel_id=1, source_target_pairs={{0,4},{1,5},{2,6},{3,7},{4,0},{5,1},{6,2},{7,3},{8,28},{9,29},{10,... | collective-permute-start | bytes 2162696 | tf_op jit(solution)/shard_map/ppermute | solution.py:537
  105.0 11.6 %collective-permute-start.18 = (bf16[256,1152]{1,0:T(8,128)(2,1)S(1)}, bf16[256,1152]{1,0:T(8,128)(2,1)S(1)}, u32[]{:S(2)}, u32[]{:S(2)}) collective-permute-start(bf16[256,1152]{1,0:T(8,128)(2,1)S(1)} %get-tuple-element.92), channel_id=1, source_target_pairs={{0,1},{1,0},{2,3},{3,2},{4,5},{5,4},{6,7},{7,6},{8,11},{9,10},{10,... | collective-permute-start | bytes 1769480 | tf_op jit(solution)/shard_map/ppermute | solution.py:537
  107.3 14.8 %collective-permute-start.13 = (bf16[128,1536]{1,0:T(8,128)(2,1)S(1)}, bf16[128,1536]{1,0:T(8,128)(2,1)S(1)}, u32[]{:S(2)}, u32[]{:S(2)}) collective-permute-start(bf16[128,1536]{1,0:T(8,128)(2,1)S(1)} %get-tuple-element.91), channel_id=1, source_target_pairs={{0,4},{1,5},{2,6},{3,7},{4,0},{5,1},{6,2},{7,3},{8,28},{9,29},{10,... | collective-permute-start | bytes 1179656 | tf_op jit(solution)/shard_map/ppermute | solution.py:537
  116.5 7.5 %collective-permute-start.16 = (bf16[128,1408]{1,0:T(8,128)(2,1)S(1)}, bf16[128,1408]{1,0:T(8,128)(2,1)S(1)}, u32[]{:S(2)}, u32[]{:S(2)}) collective-permute-start(bf16[128,1408]{1,0:T(8,128)(2,1)S(1)} %get-tuple-element.95), channel_id=1, source_target_pairs={{0,1},{1,0},{2,3},{3,2},{4,5},{5,4},{6,7},{7,6},{8,11},{9,10},{10,... | collective-permute-start | bytes 1081352 | tf_op jit(solution)/shard_map/ppermute | solution.py:537
  116.7 7.4 %collective-permute-start.19 = (bf16[128,1152]{1,0:T(8,128)(2,1)S(1)}, bf16[128,1152]{1,0:T(8,128)(2,1)S(1)}, u32[]{:S(2)}, u32[]{:S(2)}) collective-permute-start(bf16[128,1152]{1,0:T(8,128)(2,1)S(1)} %get-tuple-element.96), channel_id=1, source_target_pairs={{0,32},{1,33},{2,34},{3,35},{4,36},{5,37},{6,38},{7,39},{8,104},{9... | collective-permute-start | bytes 884744 | tf_op jit(solution)/shard_map/ppermute | solution.py:537
  124.3 7.7 %collective-permute-start.21 = (bf16[32,4096]{1,0:T(8,128)(2,1)S(1)}, bf16[32,4096]{1,0:T(8,128)(2,1)S(1)}, u32[]{:S(2)}, u32[]{:S(2)}) collective-permute-start(bf16[32,4096]{1,0:T(8,128)(2,1)S(1)} %get-tuple-element.104), channel_id=1, source_target_pairs={{0,3},{1,2},{2,1},{3,0},{4,7},{5,6},{6,5},{7,4},{8,9},{9,8},{10,11... | collective-permute-start | bytes 786440 | tf_op jit(solution)/shard_map/ppermute | solution.py:549
  124.4 9.9 %collective-permute-start.20 = (bf16[32,4096]{1,0:T(8,128)(2,1)S(1)}, bf16[32,4096]{1,0:T(8,128)(2,1)S(1)}, u32[]{:S(2)}, u32[]{:S(2)}) collective-permute-start(bf16[32,4096]{1,0:T(8,128)(2,1)S(1)} %get-tuple-element.105), channel_id=1, source_target_pairs={{0,99},{1,98},{2,97},{3,96},{4,103},{5,102},{6,101},{7,100},{8,41}... | collective-permute-start | bytes 786440 | tf_op jit(solution)/shard_map/ppermute | solution.py:549
  124.6 12.4 %collective-permute-start.22 = (bf16[32,4096]{1,0:T(8,128)(2,1)S(1)}, bf16[32,4096]{1,0:T(8,128)(2,1)S(1)}, u32[]{:S(2)}, u32[]{:S(2)}) collective-permute-start(bf16[32,4096]{1,0:T(8,128)(2,1)S(1)} %slice.324), channel_id=1, source_target_pairs={{0,96},{1,97},{2,98},{3,99},{4,100},{5,101},{6,102},{7,103},{8,40}... | collective-permute-start | bytes 786440 | tf_op jit(solution)/shard_map/ppermute | solution.py:549
  137.1 6.3 %collective-permute-start.23 = (bf16[16,4096]{1,0:T(8,128)(2,1)S(1)}, bf16[16,4096]{1,0:T(8,128)(2,1)S(1)}, u32[]{:S(2)}, u32[]{:S(2)}) collective-permute-start(bf16[16,4096]{1,0:T(8,128)(2,1)S(1)} %slice.325), channel_id=1, source_target_pairs={{0,20},{1,21},{2,22},{3,23},{4,16},{5,17},{6,18},{7,19},{8,12},{9,... | collective-permute-start | bytes 393224 | tf_op jit(solution)/shard_map/ppermute | solution.py:558
  143.4 1.3 collective-permute-start.24

commit v3 on v2

--- a/solution.py
+++ b/solution.py
@@ -75,11 +75,12 @@
     return pairs
 
 
-def core_pairs():
+def core_pairs(names_of_core=((), ())):
     pairs = []
     for index in range(2 * CHIPS):
         x, y, z, core = place_of(index)
-        pairs.append((index, index_of(x, y, z, 1 - core)))
+        fx, fy, fz = flip_of(names_of_core[core]) if names_of_core[core] else (0, 0, 0)
+        pairs.append((index, index_of(x ^ fx, y ^ fy, z ^ fz, 1 - core)))
     return pairs
 
 
@@ -541,9 +542,9 @@
                 )
     keep, send = jnp.concatenate(keeps, axis=1), jnp.concatenate(sends, axis=1)
     blocks = (
-        (send[32:], (3, 4)),
         (send[:32], (3,)),
         (keep[32:].astype(jnp.bfloat16), (4,)),
+        (send[32:], (3, 4)),
     )
     coming = [
         lax.ppermute(
@@ -555,14 +556,17 @@
     total = keep[:32]
     for came in coming:
         total = total + came.astype(jnp.float32)
-    came = lax.ppermute(
-        total[16:].astype(jnp.bfloat16), AXES, flip_pairs([ORDERS[c][0][5] for c in range(2)])
-    )
-    total = total[:16] + came.astype(jnp.float32)
-    both = total.reshape(2, 8, HALF)
-    mine = lax.dynamic_index_in_dim(both, core, 0, keepdims=False)
-    theirs = lax.dynamic_index_in_dim(both, 1 - core, 0, keepdims=False).astype(jnp.bfloat16)
-    came = lax.ppermute(theirs, AXES, swap).astype(jnp.float32)
+    blocks = total.reshape(2, 2, 8, HALF)
+    mine = lax.dynamic_index_in_dim(blocks, core, 1, keepdims=False)
+    theirs = lax.dynamic_index_in_dim(blocks, 1 - core, 1, keepdims=False).astype(jnp.bfloat16)
+    last_flip = [(ORDERS[c][0][5],) for c in range(2)]
+    coming = [
+        lax.ppermute(theirs[1], AXES, core_pairs(last_flip)),
+        lax.ppermute(mine[1].astype(jnp.bfloat16), AXES, flip_pairs(last_flip)),
+        lax.ppermute(theirs[0], AXES, swap),
+    ]
+    coming = [came.astype(jnp.float32) for came in lax.optimization_barrier(coming)]
+    mine, came = mine[0] + coming[1], coming[0] + coming[2]
     grad_proj = jnp.where(
         core == 0,
         jnp.concatenate([mine, came], axis=1),

time: 146 us -> 144 us (0.986)
  starting transfers between devices: 60.9 us -> 55.2 us
  waiting for transfers between devices: 43.6 us -> 48.4 us
    ppermute x6, starting transfers between devices: 22.1 us -> 14.3 us  [body(): lax.ppermute(sends[part], AXES, flip_pairs([ORDERS[c][part][level + 1] fo...]
    ppermute x3, waiting for transfers between devices: 0.01 us -> 5.69 us  [body(): lax.ppermute(sends[part], AXES, flip_pairs([ORDERS[c][part][0] for c in r...]
    ppermute x2 -> x3, waiting for transfers between devices: 6.48 us -> 2.24 us  [the longest x1 2.24 us: body(): lax.ppermute(mine[1].astype(jnp.bfloat16), AXES, flip_pairs(last_flip))]
    ppermute x3, starting transfers between devices: 13.1 us -> 9.04 us  [body(): lax.ppermute(sends[part], AXES, flip_pairs([ORDERS[c][part][0] for c in r...]
    ppermute x2 -> x3, starting transfers between devices: 1.08 us -> 4.83 us  [the longest x1 4.39 us: body(): lax.ppermute(mine[1].astype(jnp.bfloat16), AXES, flip_pairs(last_flip))]
    ppermute x3, waiting for transfers between devices: 6.49 us -> 9.21 us  [body(): lax.ppermute(block, AXES, flip_pairs([[ORDERS[c][0][level] for level in l...]
    ppermute x6, waiting for transfers between devices: 6.97 us -> 9.12 us  [body(): lax.ppermute(sends[part], AXES, flip_pairs([ORDERS[c][part][level + 1] fo...]
  transfers between devices with their start and end apart: 26 -> 27, of which waited for: 12 -> 14; matrix products, arithmetic and copies ran while one was open for 8% -> 8% of each run, Pallas kernels for 11% -> 11%
where the time goes in v3:
time: 144 us
  starting transfers between devices  55.2 us (38%)
  waiting for transfers between devices  48.4 us (34%)
  Pallas kernels  26.9 us (19%)
  local copies, waits for them, and re-layouts  10.2 us (7%)
  other arithmetic  2.62 us (2%)
    pallas_call x13, Pallas kernels, vmem_call(): pl.pallas_call(body, out_shape=out_shape, in_specs=specs, out_specs=out_s...  15.7 us
    ppermute x6, starting transfers between devices, body(): lax.ppermute(sends[part], AXES, flip_pairs([ORDERS[c][part][level + 1] fo...  14.3 us
    all_to_all x1, waiting for transfers between devices, body(): lax.all_to_all(sent.reshape(GROUPS, ROWS // GROUPS, SENT), 'dp', 0, 0, ti...  11.1 us
    dynamic_slice x3, local copies, waits for them, and re-layouts, body(): lax.dynamic_slice(tokens, (0, (1 - core) * HALF + at), (ROWS, width))  10.1 us
    ppermute x3, waiting for transfers between devices, body(): lax.ppermute(block, AXES, flip_pairs([[ORDERS[c][0][level] for level in l...  9.21 us
    ppermute x6, waiting for transfers between devices, body(): lax.ppermute(sends[part], AXES, flip_pairs([ORDERS[c][part][level + 1] fo...  9.12 us
    ppermute x3, starting transfers between devices, body(): lax.ppermute(sends[part], AXES, flip_pairs([ORDERS[c][part][0] for c in r...  9.04 us
    all_to_all x1, starting transfers between devices, body(): lax.all_to_all(sent.reshape(GROUPS, ROWS // GROUPS, SENT), 'dp', 0, 0, ti...  7.98 us
  transfers between devices with their start and end apart: 27, of which 14 were waited for; matrix products, arithmetic and copies ran while one was open for 8% of the time, Pallas kernels for 11%

profile of v3, /device:TPU:0, one launch (start us, length us, event | category | flops | bytes accessed | tf_op | source)
XLA Modules:
  0.0 144.3 jit_solution(1045402410265902413)
XLA Ops:
  0.6 4.1 %shard_map.68 = bf16[512,1408]{1,0:T(8,128)(2,1)} custom-call(s32[1,512]{1,0:T(1,128)} %dest_ref.1, bf16[1,512,1280]{2,1,0:T(8,128)(2,1)} %rows_ref.1), custom_call_target="tpu_custom_call" | custom-call | flops 1000000000 | bytes 3145728 | tf_op jit(solution)/shard_map/pallas_call | solution.py:391
  4.8 8.0 %all-to-all-start = ((bf16[16,32,1408]{2,1,0:T(8,128)(2,1)}), bf16[16,32,1408]{2,1,0:T(8,128)(2,1)S(1)}, u32[]{:S(2)}, u32[]{:S(2)}) async-start(bf16[16,32,1408]{2,1,0:T(8,128)(2,1)} %bitcast.97), calls=%async_computation | async-start | bytes 2883584 | tf_op jit(solution)/shard_map/all_to_all | solution.py:406
  12.8 3.2 %dynamic-slice_bitcast_fusion.4 = (bf16[512,1152]{1,0:T(8,128)(2,1)}, bf16[512,1152]{1,0:T(8,128)(2,1)}) fusion(bf16[1,512,8192]{2,1,0:T(8,128)(2,1)} %param.8, s32[]{:T(128)S(6)} %select_n.92, s32[]{:T(128)S(6)} %select_n.89), kind=kLoop, calls=%fused_computation.10 | loop fusion | bytes 4718600 | tf_op jit(solution)/shard_map/dynamic_slice | solution.py:386
  16.4 3.2 %dynamic-slice_bitcast_fusion = (bf16[512,1536]{1,0:T(8,128)(2,1)}, bf16[512,1536]{1,0:T(8,128)(2,1)S(1)}) fusion(bf16[1,512,8192]{2,1,0:T(8,128)(2,1)} %param.8, s32[]{:T(128)S(6)} %select_n.90, s32[]{:T(128)S(6)} %select_n.87), kind=kLoop, calls=%fused_computation.2 | loop fusion | bytes 6291464 | tf_op jit(solution)/shard_map/dynamic_slice | solution.py:386
  19.8 3.6 %dynamic-slice_bitcast_fusion.2 = (bf16[512,1408]{1,0:T(8,128)(2,1)}, bf16[512,1408]{1,0:T(8,128)(2,1)}) fusion(bf16[1,512,8192]{2,1,0:T(8,128)(2,1)} %param.8, s32[]{:T(128)S(6)} %select_n.91, s32[]{:T(128)S(6)} %select_n.88), kind=kLoop, calls=%fused_computation.6 | loop fusion | bytes 5767176 | tf_op jit(solution)/shard_map/dynamic_slice | solution.py:386
  23.8 11.1 %all-to-all-done = bf16[16,32,1408]{2,1,0:T(8,128)(2,1)S(1)} async-done(((bf16[16,32,1408]{2,1,0:T(8,128)(2,1)}), bf16[16,32,1408]{2,1,0:T(8,128)(2,1)S(1)}, u32[]{:S(2)}, u32[]{:S(2)}) %all-to-all-start) | async-done | bytes 1441824 | tf_op jit(solution)/shard_map/all_to_all | solution.py:406
  35.0 1.2 shard_map.69
  36.2 1.5 %collective-permute-start = (bf16[512,256]{1,0:T(8,128)(2,1)}, bf16[512,256]{1,0:T(8,128)(2,1)}, u32[]{:S(2)}, u32[]{:S(2)}) collective-permute-start(bf16[512,256]{1,0:T(8,128)(2,1)} %get-tuple-element.45.kv_ref), channel_id=1, source_target_pairs={{0,1},{1,0},{2,3},{3,2},{4,5},{5,4},{6,7},{7,6},{8,11},{9,10},{10,... | collective-permute-start | bytes 786440 | tf_op jit(solution)/shard_map/ppermute | solution.py:421
  37.7 2.1 %collective-permute-start.6 = (bf16[512,256]{1,0:T(8,128)(2,1)}, bf16[512,256]{1,0:T(8,128)(2,1)}, u32[]{:S(2)}, u32[]{:S(2)}) collective-permute-start(bf16[512,256]{1,0:T(8,128)(2,1)} %get-tuple-element.45.kv_ref), channel_id=1, source_target_pairs={{0,3},{1,2},{2,1},{3,0},{4,7},{5,6},{6,5},{7,4},{8,12},{9,13},{10,... | collective-permute-start | bytes 786440 | tf_op jit(solution)/shard_map/ppermute | solution.py:422
  39.8 1.0 collective-permute-start.7
  40.8 3.2 %collective-permute-done.near0_ref = bf16[512,256]{1,0:T(8,128)(2,1)} collective-permute-done((bf16[512,256]{1,0:T(8,128)(2,1)}, bf16[512,256]{1,0:T(8,128)(2,1)}, u32[]{:S(2)}, u32[]{:S(2)}) %collective-permute-start) | collective-permute-done | bytes 262176 | tf_op jit(solution)/shard_map/ppermute | solution.py:421
  44.0 4.0 %collective-permute-start.1 = (bf16[512,256]{1,0:T(8,128)(2,1)}, bf16[512,256]{1,0:T(8,128)(2,1)}, u32[]{:S(2)}, u32[]{:S(2)}) collective-permute-start(bf16[512,256]{1,0:T(8,128)(2,1)} %collective-permute-done.near0_ref), channel_id=1, source_target_pairs={{0,3},{1,2},{2,1},{3,0},{4,7},{5,6},{6,5},{7,4},{8,9},{9,8},{10,11... | collective-permute-start | bytes 786440 | tf_op jit(solution)/shard_map/ppermute | solution.py:424
  48.1 1.1 collective-permute-start.8
  49.5 4.7 %collective-permute-done.1.far0_ref = bf16[512,256]{1,0:T(8,128)(2,1)} collective-permute-done((bf16[512,256]{1,0:T(8,128)(2,1)}, bf16[512,256]{1,0:T(8,128)(2,1)}, u32[]{:S(2)}, u32[]{:S(2)}) %collective-permute-start.1) | collective-permute-done | bytes 262176 | tf_op jit(solution)/shard_map/ppermute | solution.py:424
  54.2 1.0 collective-permute-start.2
  55.3 4.0 %shard_map.70 = (bf16[512,1024]{1,0:T(8,128)(2,1)S(1)}, f32[4096,128]{1,0:T(8,128)S(1)}, f32[4096,256]{1,0:T(8,128)S(1)}) custom-call(s32[2]{0:T(128)S(1)} %pad_add_fusion.slot_ref, s32[1,4]{1,0:T(1,128)S(1)} %copy-done.2, bf16[512,512]{1,0:T(8,128)(2,1)S(1)} %get-tuple-element.44.inverse_ref, bf16[512,1408]{1,0:T(8,128)(2,1)S(1)} %bitcast.88, ...), custom_call_target="tpu_custom_call" | custom-call | flops 2000000000 | bytes 4194304 | tf_op jit(solution)/shard_map/pallas_call | solution.py:111
  59.3 1.4 collective-permute-done.2.last_ref
  60.8 5.8 %shard_map.71 = (bf16[512,1024]{1,0:T(8,128)(2,1)}, bf16[1024,512]{1,0:T(8,128)(2,1)S(1)}, bf16[1024,512]{1,0:T(8,128)(2,1)S(1)}, bf16[512,1536]{1,0:T(8,128)(2,...) custom-call(s32[2]{0:T(128)S(1)} %pad_add_fusion.slot_ref, ...), custom_call_target="tpu_custom_call" | custom-call | flops 10000000000 | bytes 16777216 | tf_op jit(solution)/shard_map/pallas_call | solution.py:456
  66.7 1.0 shard_map.72.refs_0_
  67.6 1.7 %collective-permute-done.10.left_ref = bf16[1024,512]{1,0:T(8,128)(2,1)S(1)} collective-permute-done((bf16[1024,512]{1,0:T(8,128)(2,1)S(1)}, bf16[1024,512]{1,0:T(8,128)(2,1)S(1)}, u32[]{:S(2)}, u32[]{:S(2)}) %collective-permute-start.10) | collective-permute-done | bytes 1048608 | tf_op jit(solution)/shard_map/ppermute | solution.py:496
  69.3 1.0 shard_map.73
  70.3 3.8 %collective-permute-start.11 = (bf16[512,1536]{1,0:T(8,128)(2,1)S(1)}, bf16[512,1536]{1,0:T(8,128)(2,1)S(1)}, u32[]{:S(2)}, u32[]{:S(2)}) collective-permute-start(bf16[512,1536]{1,0:T(8,128)(2,1)S(1)} %shard_map.73), channel_id=1, source_target_pairs={{0,1},{1,0},{2,3},{3,2},{4,5},{5,4},{6,7},{7,6},{8,11},{9,10},{10,... | collective-permute-start | bytes 4718600 | tf_op jit(solution)/shard_map/ppermute | solution.py:517
  74.2 1.0 shard_map.74.refs_0_
  75.2 1.0 shard_map.75
  76.3 0.9 shard_map.76.refs_0_
  77.2 0.9 shard_map.77
  78.1 5.1 %collective-permute-start.17 = (bf16[512,1152]{1,0:T(8,128)(2,1)S(1)}, bf16[512,1152]{1,0:T(8,128)(2,1)S(1)}, u32[]{:S(2)}, u32[]{:S(2)}) collective-permute-start(bf16[512,1152]{1,0:T(8,128)(2,1)S(1)} %shard_map.77), channel_id=1, source_target_pairs={{0,4},{1,5},{2,6},{3,7},{4,0},{5,1},{6,2},{7,3},{8,28},{9,29},{10,... | collective-permute-start | bytes 3538952 | tf_op jit(solution)/shard_map/ppermute | solution.py:517
  83.2 0.9 shard_map.82.refs_0_
  84.1 1.0 shard_map.80.refs_0_
  85.1 1.0 shard_map.81
  86.2 1.0 shard_map.78.refs_0_
  87.2 1.0 shard_map.79
  88.2 0.9 shard_map.83
  89.2 3.4 %collective-permute-done.11 = bf16[512,1536]{1,0:T(8,128)(2,1)S(1)} collective-permute-done((bf16[512,1536]{1,0:T(8,128)(2,1)S(1)}, bf16[512,1536]{1,0:T(8,128)(2,1)S(1)}, u32[]{:S(2)}, u32[]{:S(2)}) %collective-permute-start.11) | collective-permute-done | bytes 1572896 | tf_op jit(solution)/shard_map/ppermute | solution.py:517
  93.0 2.3 %collective-permute-done.14 = bf16[512,1408]{1,0:T(8,128)(2,1)S(1)} collective-permute-done((bf16[512,1408]{1,0:T(8,128)(2,1)S(1)}, bf16[512,1408]{1,0:T(8,128)(2,1)S(1)}, u32[]{:S(2)}, u32[]{:S(2)}) %collective-permute-start.14) | collective-permute-done | bytes 1441824 | tf_op jit(solution)/shard_map/ppermute | solution.py:517
  95.6 4.9 %collective-permute-start.15 = (bf16[256,1408]{1,0:T(8,128)(2,1)S(1)}, bf16[256,1408]{1,0:T(8,128)(2,1)S(1)}, u32[]{:S(2)}, u32[]{:S(2)}) collective-permute-start(bf16[256,1408]{1,0:T(8,128)(2,1)S(1)} %bitcast.104), channel_id=1, source_target_pairs={{0,4},{1,5},{2,6},{3,7},{4,0},{5,1},{6,2},{7,3},{8,28},{9,29},{10,... | collective-permute-start | bytes 2162696 | tf_op jit(solution)/shard_map/ppermute | solution.py:538
  100.8 2.1 %collective-permute-start.18 = (bf16[256,1152]{1,0:T(8,128)(2,1)S(1)}, bf16[256,1152]{1,0:T(8,128)(2,1)S(1)}, u32[]{:S(2)}, u32[]{:S(2)}) collective-permute-start(bf16[256,1152]{1,0:T(8,128)(2,1)S(1)} %get-tuple-element.98), channel_id=1, source_target_pairs={{0,1},{1,0},{2,3},{3,2},{4,5},{5,4},{6,7},{7,6},{8,11},{9,10},{10,... | collective-permute-start | bytes 1769480 | tf_op jit(solution)/shard_map/ppermute | solution.py:538
  102.9 2.1 %collective-permute-done.12 = bf16[256,1536]{1,0:T(8,128)(2,1)S(1)} collective-permute-done((bf16[256,1536]{1,0:T(8,128)(2,1)S(1)}, bf16[256,1536]{1,0:T(8,128)(2,1)S(1)}, u32[]{:S(2)}, u32[]{:S(2)}) %collective-permute-start.12) | collective-permute-done | bytes 786464 | tf_op jit(solution)/shard_map/ppermute | solution.py:538
  105.2 6.9 %collective-permute-start.13 = (bf16[128,1536]{1,0:T(8,128)(2,1)S(1)}, bf16[128,1536]{1,0:T(8,128)(2,1)S(1)}, u32[]{:S(2)}, u32[]{:S(2)}) collective-permute-start(bf16[128,1536]{1,0:T(8,128)(2,1)S(1)} %get-tuple-element.97), channel_id=1, source_target_pairs={{0,4},{1,5},{2,6},{3,7},{4,0},{5,1},{6,2},{7,3},{8,28},{9,29},{10,... | collective-permute-start | bytes 1179656 | tf_op jit(solution)/shard_map/ppermute | solution.py:538
  112.7 5.2 %collective-permute-done.13 = bf16[128,1536]{1,0:T(8,128)(2,1)S(1)} collective-permute-done((bf16[128,1536]{1,0:T(8,128)(2,1)S(1)}, bf16[128,1536]{1,0:T(8,128)(2,1)S(1)}, u32[]{:S(2)}, u32[]{:S(2)}) %collective-permute-start.13) | collective-permute-done | bytes 393248 | tf_op jit(solution)/shard_map/ppermute | solution.py:538
  117.9 1.8 %collective-permute-done.16 = bf16[128,1408]{1,0:T(8,128)(2,1)S(1)} collective-permute-done((bf16[128,1408]{1,0:T(8,128)(2,1)S(1)}, bf16[128,1408]{1,0:T(8,128)(2,1)S(1)}, u32[]{:S(2)}, u32[]{:S(2)}) %collective-permute-start.16) | collective-permute-done | bytes 360480 | tf_op jit(solution)/shard_map/ppermute | solution.py:538
  120.0 3.7 %collective-permute-start.20 = (bf16[32,4096]{1,0:T(8,128)(2,1)S(1)}, bf16[32,4096]{1,0:T(8,128)(2,1)S(1)}, u32[]{:S(2)}, u32[]{:S(2)}) collective-permute-start(bf16[32,4096]{1,0:T(8,128)(2,1)S(1)} %get-tuple-element.111), channel_id=1, source_target_pairs={{0,3},{1,2},{2,1},{3,0},{4,7},{5,6},{6,5},{7,4},{8,9},{9,8},{10,11... | collective-permute-start | bytes 786440 | tf_op jit(solution)/shard_map/ppermute | solution.py:550
  123.7 2.7 %collective-permute-start.22 = (bf16[32,4096]{1,0:T(8,128)(2,1)S(1)}, bf16[32,4096]{1,0:T(8,128)(2,1)S(1)}, u32[]{:S(2)}, u32[]{:S(2)}) collective-permute-start(bf16[32,4096]{1,0:T(8,128)(2,1)S(1)} %get-tuple-element.110), channel_id=1, source_target_pairs={{0,99},{1,98},{2,97},{3,96},{4,103},{5,102},{6,101},{7,100},{8,41}... | collective-permute-start | bytes 786440 | tf_op jit(solution)/shard_map/ppermute | solution.py:550
  127.1 1.0 collective-permute-done.20
  128.1 5.5 %collective-permute-done.22 = bf16[32,4096]{1,0:T(8,128)(2,1)S(1)} collective-permute-done((bf16[32,4096]{1,0:T(8,128)(2,1)S(1)}, bf16[32,4096]{1,0:T(8,128)(2,1)S(1)}, u32[]{:S(2)}, u32[]{:S(2)}) %collective-permute-start.22) | collective-permute-done | bytes 262176 | tf_op jit(solution)/shard_map/ppermute | solution.py:550
  133.6 2.7 %collective-permute-done.21 = bf16[32,4096]{1,0:T(8,128)(2,1)S(1)} collective-permute-done((bf16[32,4096]{1,0:T(8,128)(2,1)S(1)}, bf16[32,4096]{1,0:T(8,128)(2,1)S(1)}, u32[]{:S(2)}, u32[]{:S(2)}) %collective-permute-start.21) | collective-permute-done | bytes 262176 | tf_op jit(solution)/shard_map/ppermute | solution.py:550
  136.9 4.4 %collective-permute-start.24 = (bf16[8,4096]{1,0:T(8,128)(2,1)S(1)}, bf16[8,4096]{1,0:T(8,128)(2,1)S(1)}, u32[]{:S(2)}, u32[]{:S(2)}) collective-permute-start(bf16[8,4096]{1,0:T(8,128)(2,1)S(1)} %fusion.20), channel_id=1, source_target_pairs={{0,20},{1,21},{2,22},{3,23},{4,16},{5,17},{6,18},{7,19},{8,12},{9,... | collective-permute-start | bytes 196616 | tf_op jit(solution)/shard_map/ppermute | solution.py:565
  141.3 2.2 %collective-permute-done.24 = bf16[8,4096]{1,0:T(8,128)(2,1)S(1)} collective-permute-done((bf16[8,4096]{1,0:T(8,128)(2,1)S(1)}, bf16[8,4096]{1,0:T(8,128)(2,1)S(1)}, u32[]{:S(2)}, u32[]{:S(2)}) %collective-permute-start.24) | collective-permute-done | bytes 65568 | tf_op jit(solution)/shard_map/ppermute | solution.py:565
  (57 shorter events, 5.6 us)
Async XLA Ops:
  4.8 30.2 %all-to-all-start = ((bf16[16,32,1408]{2,1,0:T(8,128)(2,1)}), bf16[16,32,1408]{2,1,0:T(8,128)(2,1)S(1)}, u32[]{:S(2)}, u32[]{:S(2)}) async-start(bf16[16,32,1408]{2,1,0:T(8,128)(2,1)} %bitcast.97), calls=%async_computation | async-start | bytes 2883584 | tf_op jit(solution)/shard_map/all_to_all | solution.py:406
  16.0 23.7 %collective-permute-start.5 = (bf16[512,1152]{1,0:T(8,128)(2,1)}, bf16[512,1152]{1,0:T(8,128)(2,1)}, u32[]{:S(2)}, u32[]{:S(2)}) collective-permute-start(bf16[512,1152]{1,0:T(8,128)(2,1)} %get-tuple-element.86), channel_id=1, source_target_pairs={{0,8},{1,9},{2,10},{3,11},{4,12},{5,13},{6,14},{7,15},{8,0},{9,1},... | collective-permute-start | bytes 3538952 | tf_op jit(solution)/shard_map/ppermute | solution.py:385
  19.6 39.7 %collective-permute-start.3 = (bf16[512,1536]{1,0:T(8,128)(2,1)}, bf16[512,1536]{1,0:T(8,128)(2,1)}, u32[]{:S(2)}, u32[]{:S(2)}) collective-permute-start(bf16[512,1536]{1,0:T(8,128)(2,1)} %get-tuple-element.90), channel_id=1, source_target_pairs={{0,8},{1,9},{2,10},{3,11},{4,12},{5,13},{6,14},{7,15},{8,0},{9,1},... | collective-permute-start | bytes 4718600 | tf_op jit(solution)/shard_map/ppermute | solution.py:385
  23.4 24.7 %copy-start.3 = (s32[2,64,3]{1,0,2:T(2,128)S(1)}, s32[2,64,3]{1,0,2:T(2,128)}, u32[]{:S(2)}) copy-start(s32[2,64,3]{1,0,2:T(2,128)} %constant.116.clone) | copy-start | bytes 4612
  23.4 24.7 %copy-start.4 = (s32[2,64,3]{1,0,2:T(2,128)S(1)}, s32[2,64,3]{1,0,2:T(2,128)}, u32[]{:S(2)}) copy-start(s32[2,64,3]{1,0,2:T(2,128)} %constant.121) | copy-start | bytes 4612
  23.4 31.9 %copy-start.2 = (s32[1,4]{1,0:T(1,128)S(1)}, s32[1,4]{1,0:T(1,128)}, u32[]{:S(2)}) copy-start(s32[1,4]{1,0:T(1,128)} %lengths_ref.3) | copy-start | bytes 52
  23.4 36.0 %collective-permute-start.4 = (bf16[512,1408]{1,0:T(8,128)(2,1)}, bf16[512,1408]{1,0:T(8,128)(2,1)}, u32[]{:S(2)}, u32[]{:S(2)}) collective-permute-start(bf16[512,1408]{1,0:T(8,128)(2,1)} %get-tuple-element.88), channel_id=1, source_target_pairs={{0,8},{1,9},{2,10},{3,11},{4,12},{5,13},{6,14},{7,15},{8,0},{9,1},... | collective-permute-start | bytes 4325384 | tf_op jit(solution)/shard_map/ppermute | solution.py:385
  36.2 7.8 %collective-permute-start = (bf16[512,256]{1,0:T(8,128)(2,1)}, bf16[512,256]{1,0:T(8,128)(2,1)}, u32[]{:S(2)}, u32[]{:S(2)}) collective-permute-start(bf16[512,256]{1,0:T(8,128)(2,1)} %get-tuple-element.45.kv_ref), channel_id=1, source_target_pairs={{0,1},{1,0},{2,3},{3,2},{4,5},{5,4},{6,7},{7,6},{8,11},{9,10},{10,... | collective-permute-start | bytes 786440 | tf_op jit(solution)/shard_map/ppermute | solution.py:421
  37.7 10.5 %collective-permute-start.6 = (bf16[512,256]{1,0:T(8,128)(2,1)}, bf16[512,256]{1,0:T(8,128)(2,1)}, u32[]{:S(2)}, u32[]{:S(2)}) collective-permute-start(bf16[512,256]{1,0:T(8,128)(2,1)} %get-tuple-element.45.kv_ref), channel_id=1, source_target_pairs={{0,3},{1,2},{2,1},{3,0},{4,7},{5,6},{6,5},{7,4},{8,12},{9,13},{10,... | collective-permute-start | bytes 786440 | tf_op jit(solution)/shard_map/ppermute | solution.py:422
  39.8 9.5 %collective-permute-start.7 = (bf16[512,256]{1,0:T(8,128)(2,1)}, bf16[512,256]{1,0:T(8,128)(2,1)}, u32[]{:S(2)}, u32[]{:S(2)}) collective-permute-start(bf16[512,256]{1,0:T(8,128)(2,1)} %get-tuple-element.45.kv_ref), channel_id=1, source_target_pairs={{0,4},{1,5},{2,6},{3,7},{4,0},{5,1},{6,2},{7,3},{8,9},{9,8},{10,11... | collective-permute-start | bytes 786440 | tf_op jit(solution)/shard_map/ppermute | solution.py:423
  44.0 10.2 %collective-permute-start.1 = (bf16[512,256]{1,0:T(8,128)(2,1)}, bf16[512,256]{1,0:T(8,128)(2,1)}, u32[]{:S(2)}, u32[]{:S(2)}) collective-permute-start(bf16[512,256]{1,0:T(8,128)(2,1)} %collective-permute-done.near0_ref), channel_id=1, source_target_pairs={{0,3},{1,2},{2,1},{3,0},{4,7},{5,6},{6,5},{7,4},{8,9},{9,8},{10,11... | collective-permute-start | bytes 786440 | tf_op jit(solution)/shard_map/ppermute | solution.py:424
  48.1 12.6 %collective-permute-start.8 = (bf16[512,256]{1,0:T(8,128)(2,1)}, bf16[512,256]{1,0:T(8,128)(2,1)S(1)}, u32[]{:S(2)}, u32[]{:S(2)}) collective-permute-start(bf16[512,256]{1,0:T(8,128)(2,1)} %collective-permute-done.6.near1_ref), channel_id=1, source_target_pairs={{0,4},{1,5},{2,6},{3,7},{4,0},{5,1},{6,2},{7,3},{8,11},{9,10},{10,... | collective-permute-start | bytes 786440 | tf_op jit(solution)/shard_map/ppermute | solution.py:425
  49.2 11.5 %collective-permute-start.9 = (bf16[512,256]{1,0:T(8,128)(2,1)}, bf16[512,256]{1,0:T(8,128)(2,1)S(1)}, u32[]{:S(2)}, u32[]{:S(2)}) collective-permute-start(bf16[512,256]{1,0:T(8,128)(2,1)} %collective-permute-done.7.near2_ref), channel_id=1, source_target_pairs={{0,1},{1,0},{2,3},{3,2},{4,5},{5,4},{6,7},{7,6},{8,12},{9,13},{10,... | collective-permute-start | bytes 786440 | tf_op jit(solution)/shard_map/ppermute | solution.py:426
  54.2 6.6 %collective-permute-start.2 = (bf16[512,256]{1,0:T(8,128)(2,1)}, bf16[512,256]{1,0:T(8,128)(2,1)S(1)}, u32[]{:S(2)}, u32[]{:S(2)}) collective-permute-start(bf16[512,256]{1,0:T(8,128)(2,1)} %collective-permute-done.1.far0_ref), channel_id=1, source_target_pairs={{0,4},{1,5},{2,6},{3,7},{4,0},{5,1},{6,2},{7,3},{8,12},{9,13},{10,... | collective-permute-start | bytes 786440 | tf_op jit(solution)/shard_map/ppermute | solution.py:427
  55.3 5.5 %copy-start = (bf16[512,1408]{1,0:T(8,128)(2,1)S(1)}, bf16[512,1408]{1,0:T(8,128)(2,1)}, u32[]{:S(2)}) copy-start(bf16[512,1408]{1,0:T(8,128)(2,1)} %get-tuple-element.53.refs_1_) | copy-start | bytes 4325380
  55.3 5.5 %copy-start.1 = (bf16[512,1152]{1,0:T(8,128)(2,1)S(1)}, bf16[512,1152]{1,0:T(8,128)(2,1)}, u32[]{:S(2)}) copy-start(bf16[512,1152]{1,0:T(8,128)(2,1)} %get-tuple-element.54.refs_2_) | copy-start | bytes 3538948
  66.6 2.7 %collective-permute-start.10 = (bf16[1024,512]{1,0:T(8,128)(2,1)S(1)}, bf16[1024,512]{1,0:T(8,128)(2,1)S(1)}, u32[]{:S(2)}, u32[]{:S(2)}) collective-permute-start(bf16[1024,512]{1,0:T(8,128)(2,1)S(1)} %get-tuple-element.61), channel_id=1, source_target_pairs={{0,8},{1,9},{2,10},{3,11},{4,12},{5,13},{6,14},{7,15},{8,0},{9,1},... | collective-permute-start | bytes 3145736 | tf_op jit(solution)/shard_map/ppermute | solution.py:496
  70.3 22.2 %collective-permute-start.11 = (bf16[512,1536]{1,0:T(8,128)(2,1)S(1)}, bf16[512,1536]{1,0:T(8,128)(2,1)S(1)}, u32[]{:S(2)}, u32[]{:S(2)}) collective-permute-start(bf16[512,1536]{1,0:T(8,128)(2,1)S(1)} %shard_map.73), channel_id=1, source_target_pairs={{0,1},{1,0},{2,3},{3,2},{4,5},{5,4},{6,7},{7,6},{8,11},{9,10},{10,... | collective-permute-start | bytes 4718600 | tf_op jit(solution)/shard_map/ppermute | solution.py:517
  76.2 19.1 %collective-permute-start.14 = (bf16[512,1408]{1,0:T(8,128)(2,1)S(1)}, bf16[512,1408]{1,0:T(8,128)(2,1)S(1)}, u32[]{:S(2)}, u32[]{:S(2)}) collective-permute-start(bf16[512,1408]{1,0:T(8,128)(2,1)S(1)} %shard_map.75), channel_id=1, source_target_pairs={{0,32},{1,33},{2,34},{3,35},{4,36},{5,37},{6,38},{7,39},{8,104},{9... | collective-permute-start | bytes 4325384 | tf_op jit(solution)/shard_map/ppermute | solution.py:517
  78.1 22.4 %collective-permute-start.17 = (bf16[512,1152]{1,0:T(8,128)(2,1)S(1)}, bf16[512,1152]{1,0:T(8,128)(2,1)S(1)}, u32[]{:S(2)}, u32[]{:S(2)}) collective-permute-start(bf16[512,1152]{1,0:T(8,128)(2,1)S(1)} %shard_map.77), channel_id=1, source_target_pairs={{0,4},{1,5},{2,6},{3,7},{4,0},{5,1},{6,2},{7,3},{8,28},{9,29},{10,... | collective-permute-start | bytes 3538952 | tf_op jit(solution)/shard_map/ppermute | solution.py:517
  92.9 12.1 %collective-permute-start.12 = (bf16[256,1536]{1,0:T(8,128)(2,1)S(1)}, bf16[256,1536]{1,0:T(8,128)(2,1)S(1)}, u32[]{:S(2)}, u32[]{:S(2)}) collective-permute-start(bf16[256,1536]{1,0:T(8,128)(2,1)S(1)} %get-tuple-element.93), channel_id=1, source_target_pairs={{0,32},{1,33},{2,34},{3,35},{4,36},{5,37},{6,38},{7,39},{8,104},{9... | collective-permute-start | bytes 2359304 | tf_op jit(solution)/shard_map/ppermute | solution.py:538
  95.6 16.5 %collective-permute-start.15 = (bf16[256,1408]{1,0:T(8,128)(2,1)S(1)}, bf16[256,1408]{1,0:T(8,128)(2,1)S(1)}, u32[]{:S(2)}, u32[]{:S(2)}) collective-permute-start(bf16[256,1408]{1,0:T(8,128)(2,1)S(1)} %bitcast.104), channel_id=1, source_target_pairs={{0,4},{1,5},{2,6},{3,7},{4,0},{5,1},{6,2},{7,3},{8,28},{9,29},{10,... | collective-permute-start | bytes 2162696 | tf_op jit(solution)/shard_map/ppermute | solution.py:538
  100.8 11.6 %collective-permute-start.18 = (bf16[256,1152]{1,0:T(8,128)(2,1)S(1)}, bf16[256,1152]{1,0:T(8,128)(2,1)S(1)}, u32[]{:S(2)}, u32[]{:S(2)}) collective-permute-start(bf16[256,1152]{1,0:T(8,128)(2,1)S(1)} %get-tuple-element.98), channel_id=1, source_target_pairs={{0,1},{1,0},{2,3},{3,2},{4,5},{5,4},{6,7},{7,6},{8,11},{9,10},{10,... | collective-permute-start | bytes 1769480 | tf_op jit(solution)/shard_map/ppermute | solution.py:538
  105.2 12.7 %collective-permute-start.13 = (bf16[128,1536]{1,0:T(8,128)(2,1)S(1)}, bf16[128,1536]{1,0:T(8,128)(2,1)S(1)}, u32[]{:S(2)}, u32[]{:S(2)}) collective-permute-start(bf16[128,1536]{1,0:T(8,128)(2,1)S(1)} %get-tuple-element.97), channel_id=1, source_target_pairs={{0,4},{1,5},{2,6},{3,7},{4,0},{5,1},{6,2},{7,3},{8,28},{9,29},{10,... | collective-permute-start | bytes 1179656 | tf_op jit(solution)/shard_map/ppermute | solution.py:538
  112.2 7.5 %collective-permute-start.16 = (bf16[128,1408]{1,0:T(8,128)(2,1)S(1)}, bf16[128,1408]{1,0:T(8,128)(2,1)S(1)}, u32[]{:S(2)}, u32[]{:S(2)}) collective-permute-start(bf16[128,1408]{1,0:T(8,128)(2,1)S(1)} %get-tuple-element.101), channel_id=1, source_target_pairs={{0,1},{1,0},{2,3},{3,2},{4,5},{5,4},{6,7},{7,6},{8,11},{9,10},{10,... | collective-permute-start | bytes 1081352 | tf_op jit(solution)/shard_map/ppermute | solution.py:538
  112.5 7.4 %collective-permute-start.19 = (bf16[128,1152]{1,0:T(8,128)(2,1)S(1)}, bf16[128,1152]{1,0:T(8,128)(2,1)S(1)}, u32[]{:S(2)}, u32[]{:S(2)}) collective-permute-start(bf16[128,1152]{1,0:T(8,128)(2,1)S(1)} %get-tuple-element.102), channel_id=1, source_target_pairs={{0,32},{1,33},{2,34},{3,35},{4,36},{5,37},{6,38},{7,39},{8,104},{9... | collective-permute-start | bytes 884744 | tf_op jit(solution)/shard_map/ppermute | solution.py:538
  120.0 8.1 %collective-permute-start.20 = (bf16[32,4096]{1,0:T(8,128)(2,1)S(1)}, bf16[32,4096]{1,0:T(8,128)(2,1)S(1)}, u32[]{:S(2)}, u32[]{:S(2)}) collective-permute-start(bf16[32,4096]{1,0:T(8,128)(2,1)S(1)} %get-tuple-element.111), channel_id=1, source_target_pairs={{0,3},{1,2},{2,1},{3,0},{4,7},{5,6},{6,5},{7,4},{8,9},{9,8},{10,11... | collective-permute-start | bytes 786440 | tf_op jit(solution)/shard_map/ppermute | solution.py:550
  123.7 9.9 %collective-permute-start.22 = (bf16[32,4096]{1,0:T(8,128)(2,1)S(1)}, bf16[32,4096]{1,0:T(8,128)(2,1)S(1)}, u32[]{:S(2)}, u32[]{:S(2)}) collective-permute-start(bf16[32,4096]{1,0:T(8,128)(2,1)S(1)} %get-tuple-element.110), channel_id=1, source_target_pairs={{0,99},{1,98},{2,97},{3,96},{4,103},{5,102},{6,101},{7,100},{8,41}... | collective-permute-start | bytes 786440 | tf_op jit(solution)/shard_map/ppermute | solution.py:550
  126.5 9.8 %collective-permute-start.21 = (bf16[32,4096]{1,0:T(8,128)(2,1)S(1)}, bf16[32,4096]{1,0:T(8,128)(2,1)S(1)}, u32[]{:S(2)}, u32[]{:S(2)}) collective-permute-start(bf16[32,4096]{1,0:T(8,128)(2,1)S(1)} %slice.334), channel_id=1, source_target_pairs={{0,96},{1,97},{2,98},{3,99},{4,100},{5,101},{6,102},{7,103},{8,40}... | collective-permute-start | bytes 786440 | tf_op jit(solution)/shard_map/ppermute | solution.py:550
  136.5 4.8 %collective-permute-start.23 = (bf16[8,4096]{1,0:T(8,128)(2,1)S(1)}, bf16[8,4096]{1,0:T(8,128)(2,1)S(1)}, u32[]{:S(2)}, u32[]{:S(2)}) collective-permute-start(bf16[8,4096]{1,0:T(8,128)(2,1)S(1)} %get-tuple-element.113), channel_id=1, source_target_pairs={{0,28},{1,29},{2,30},{3,31},{4,24},{5,25},{6,26},{7,27},{8,4},{9,5... | collective-permute-start | bytes 196616 | tf_op jit(solution)/shard_map/ppermute | solution.py:564
  136.6 4.7 %collective-permute-start.25 = (bf16[8,4096]{1,0:T(8,128)(2,1)S(1)}, bf16[8,4096]{1,0:T(8,128)(2,1)S(1)}, u32[]{:S(2)}, u32[]{:S(2)}) collective-permute-start(bf16[8,4096]{1,0:T(8,128)(2,1)S(1)} %get-tuple-element.112), channel_id=1, source_target_pairs={{0,8},{1,9},{2,10},{3,11},{4,12},{5,13},{6,14},{7,15},{8,0},{9,1},... | collective-permute-start | bytes 196616 | tf_op jit(solution)/shard_map/ppermute | solution.py:566
  136.9 6.6 %collective-permute-start.24 = (bf16[8,4096]{1,0:T(8,128)(2,1)S(1)}, bf16[8,4096]{1,0:T(8,128)(2,1)S(1)}, u32[]{:S(2)}, u32[]{:S(2)}) collective-permute-start(bf16[8,4096]{1,0:T(8,128)(2,1)S(1)} %fusion.20), channel_id=1, source_target_pairs={{0,20},{1,21},{2,22},{3,23},{4,16},{5,17},{6,18},{7,19},{8,12},{9,... | collective-permute-start | bytes 196616 | tf_op jit(solution)/shard_map/ppermute | solution.py:565
